TPU v7x, 32 devices: a whole 2x2x4 slice. The times are simulated.
32 devices in a mesh: items: 16 (over z, x, core), narrow: 2 (over y).
Axes of the slice: x: 2, y: 2, z: 4, core: 2. Of those that a mesh axis runs over, the one named last changes fastest.
Arguments:
- series: bfloat16 [16, 27648], P('items'), may hold values from -6 to 6
- amplitudes: float32 [16, 5], P('items'), may hold values from -5 to 5
- periods: int32 [16, 5], P('items'), may hold values from 2 to 48, as said below
- conv_in: bfloat16 [18304, 64], replicated, may hold values from -0.25 to 0.25
- bias_in: float32 [64], replicated, may hold values from -3 to 3
- conv_out: bfloat16 [18304, 64], replicated, may hold values from -0.25 to 0.25
- bias_out: float32 [64], replicated, may hold values from -3 to 3
- norm_gain: float32 [64], replicated, may hold values from 0.5 to 1.5
- norm_bias: float32 [64], replicated, may hold values from -3 to 3
- cotangent: bfloat16 [16, 27648], P('items', 'narrow'), may hold values from -6 to 6
Outputs:
- output: bfloat16 [16, 27648], P('items', 'narrow')
- grad_series: float32 [16, 27648], P('items', 'narrow')
- grad_amplitudes: float32 [16, 5], P('items')
- grad_conv_in: float32 [18304, 64], replicated
- grad_bias_in: float32 [64], replicated
- grad_conv_out: float32 [18304, 64], replicated
- grad_bias_out: float32 [64], replicated
- grad_gain: float32 [64], replicated
- grad_norm_bias: float32 [64], replicated
Inputs may be any that keep to these rules, and one draw needn't show every extreme that they name: Each item's 5 periods are distinct; some item has the period 48.
All inputs are finite; a program needn't handle non-finite values.
Results may differ from a plain program's by a relative error of at most 0.0096.
Values may be sent and summed in bfloat16 or wider, within the bound.
No kernel may reach another device: no remote copies, remote signals or barrier semaphores. Data moves between devices by JAX's collectives and lax.ppermute only.
A program may use at most 192 MiB of HBM per device.

v0:
```python
import jax
import jax.numpy as jnp
from jax import lax
from jax.sharding import PartitionSpec as P

D = 64
FF = 64
K = 5
TAPS = 286
STEPS = 432
PMAX = 48
GRID = 480


kernel_sizes = (1, 3, 5, 7, 9, 11)
epsilon = 1e-05


def for_sending(value):
    return jax.tree.map(lambda a: a.astype(jnp.bfloat16) if a.dtype == jnp.float32 else a, value)


def stacked_offsets():
    listed = []
    for kernel in kernel_sizes:
        radius = (kernel - 1) // 2
        for offset_row in range(-radius, radius + 1):
            for offset_col in range(-radius, radius + 1):
                listed.append((offset_row, offset_col))
    return listed


def offset_list():
    return stacked_offsets()


def unfold(values, period, direction):
    length = values.shape[0]
    margin = 5 * PMAX + 5
    padded = jnp.pad(values, ((margin, margin), (0, 0)))
    column = jnp.arange(length, dtype=jnp.int32) % period
    shifted = {}
    for offset_row in range(-5, 6):
        begin_at = (margin - 5 + direction * offset_row * period).astype(jnp.int32)
        window = lax.dynamic_slice_in_dim(padded, begin_at, length + 10, 0)
        for offset_col in range(-5, 6):
            moved = window[5 + direction * offset_col : 5 + direction * offset_col + length]
            inside = (column + direction * offset_col >= 0) & (
                column + direction * offset_col < period
            )
            shifted[offset_row, offset_col] = jnp.where(
                inside[:, None], moved, jnp.zeros((), values.dtype)
            )
    pieces = [shifted[place] for place in offset_list()]
    return jnp.concatenate(pieces, axis=1)


def apply_weight(unfolded, prepared):
    product = jnp.dot(unfolded, prepared, preferred_element_type=jnp.float32)
    return product


def grid_mask(length, period):
    position = jnp.arange(length, dtype=jnp.int32)
    return position < (STEPS + period - 1) // period * period


def gelu_exact(values):
    return jax.nn.gelu(values, approximate=False)


def slots_of(source, count_narrow, items_here):
    per_item = -(-K // count_narrow)
    slot_index = jnp.arange(items_here * per_item, dtype=jnp.int32)
    branch_index = source + count_narrow * (slot_index % per_item)
    is_valid = branch_index < K
    return (slot_index // per_item, jnp.minimum(branch_index, K - 1), is_valid)


def transpose_taps(weight, rows_in, cols_out):
    return (
        weight.reshape(TAPS, rows_in, cols_out).transpose(0, 2, 1).reshape(TAPS * cols_out, rows_in)
    )


def on_device(
    series,
    amplitudes,
    periods,
    conv_in,
    bias_in,
    conv_out,
    bias_out,
    norm_gain,
    norm_bias,
    cotangent,
):
    highest = lax.Precision.HIGHEST
    count_narrow = lax.axis_size("narrow")
    my_rank = lax.axis_index("narrow")
    items_here = series.shape[0]
    share_size = STEPS * D // count_narrow
    tap_count = len(offset_list())
    inputs_all = series.reshape(items_here, STEPS, D)
    mixing = jax.nn.softmax(amplitudes, axis=-1)
    item_index, branch_index, is_valid = slots_of(my_rank, count_narrow, items_here)
    slot_period = periods[item_index, branch_index]
    slot_weight = jnp.where(is_valid, mixing[item_index, branch_index], 0.0)
    capacity = item_index.shape[0]
    conv_out_back = transpose_taps(conv_out, FF, D)
    conv_in_back = transpose_taps(conv_in, D, FF)

    def forward_slot(slot_args):
        item_at, period = slot_args
        grid_input = jnp.pad(inputs_all[item_at], ((0, GRID - STEPS), (0, 0)))
        hidden_pre = apply_weight(unfold(grid_input, period, 1), conv_in) / 6.0 + bias_in
        active = jnp.where(grid_mask(GRID, period)[:, None], gelu_exact(hidden_pre), 0.0).astype(
            jnp.bfloat16
        )
        branch = apply_weight(unfold(active, period, 1), conv_out) / 6.0 + bias_out
        return (branch[:STEPS].astype(jnp.bfloat16), hidden_pre, active)

    branch_out, hidden_all, active_all = lax.map(forward_slot, (item_index, slot_period))
    branch_flat = branch_out.reshape(capacity, STEPS * D)
    inputs_flat = series.reshape(items_here, STEPS * D)
    own_inputs = lax.dynamic_slice_in_dim(inputs_flat, my_rank * share_size, share_size, 1).astype(
        jnp.float32
    )
    item_rows = jnp.arange(items_here, dtype=jnp.int32)[:, None]
    own_onehot = (item_rows == item_index[None, :]).astype(jnp.float32)
    received = lax.all_to_all(
        for_sending(branch_flat), "narrow", split_axis=1, concat_axis=0, tiled=True
    ).astype(branch_flat.dtype)
    blocks = []
    for source in range(count_narrow):
        src_item, src_branch, src_valid = slots_of(source, count_narrow, items_here)
        weight_here = jnp.where(src_valid, mixing[src_item, src_branch], 0.0)
        blocks.append((item_rows == src_item[None, :]).astype(jnp.float32) * weight_here[None, :])
    combine = jnp.concatenate(blocks, axis=1)
    branch_sum = jnp.dot(combine, received.astype(jnp.float32), precision=highest)
    merged = (own_inputs + branch_sum).reshape(items_here, share_size // D, D)
    centered = merged - jnp.mean(merged, axis=-1, keepdims=True)
    variance = jnp.mean(centered * centered, axis=-1, keepdims=True)
    inv_std = lax.rsqrt(variance + epsilon)
    normed = centered * inv_std
    output = (normed * norm_gain + norm_bias).astype(jnp.bfloat16).reshape(items_here, share_size)
    grad_out = cotangent.astype(jnp.float32).reshape(items_here, share_size // D, D)
    grad_gain = jnp.sum(grad_out * normed, axis=(0, 1))
    grad_norm_bias = jnp.sum(grad_out, axis=(0, 1))
    scaled = grad_out * norm_gain
    grad_merged = inv_std * (
        scaled
        - jnp.mean(scaled, axis=-1, keepdims=True)
        - normed * jnp.mean(scaled * normed, axis=-1, keepdims=True)
    )
    grad_flat = grad_merged.reshape(items_here, share_size)
    grad_full = lax.all_gather(grad_flat, "narrow", axis=1, tiled=True)
    slot_grad = grad_full[item_index]
    dot_values = jnp.where(
        is_valid, jnp.sum(slot_grad * branch_flat.astype(jnp.float32), axis=1), 0.0
    )
    branch_onehot = (jnp.arange(K, dtype=jnp.int32)[None, :] == branch_index[:, None]).astype(
        jnp.float32
    )
    dot_table = jnp.dot(own_onehot * dot_values[None, :], branch_onehot, precision=highest)
    dot_total = lax.psum(dot_table, "narrow")
    grad_amplitudes = mixing * (dot_total - jnp.sum(mixing * dot_total, axis=-1, keepdims=True))
    grad_branch = (
        (slot_weight[:, None] * slot_grad).astype(jnp.bfloat16).reshape(capacity, STEPS, D)
    )
    contract_rows = (((0,), (0,)), ((), ()))

    def outer_step(totals, slot_args):
        sum_weight, sum_bias = totals
        grad_here, active, hidden_pre, period = slot_args
        grad_grid = jnp.pad(grad_here, ((0, GRID - STEPS), (0, 0)))
        sum_weight = (
            sum_weight
            + lax.dot_general(
                unfold(active, period, 1),
                grad_grid,
                contract_rows,
                preferred_element_type=jnp.float32,
            )
            / 6.0
        )
        sum_bias = sum_bias + jnp.sum(grad_here.astype(jnp.float32), axis=0)
        grad_active = apply_weight(unfold(grad_grid, period, -1), conv_out_back) / 6.0
        grad_active = jnp.where(grid_mask(GRID, period)[:, None], grad_active, 0.0)
        grad_hidden = jax.vjp(gelu_exact, hidden_pre)[1](grad_active)[0].astype(jnp.bfloat16)
        return ((sum_weight, sum_bias), grad_hidden)

    outer_init = (jnp.zeros((tap_count * FF, D), jnp.float32), jnp.zeros((D,), jnp.float32))
    (grad_conv_out, grad_bias_out), grad_hidden_all = lax.scan(
        outer_step, outer_init, (grad_branch, active_all, hidden_all, slot_period)
    )

    def inner_step(totals, slot_args):
        sum_weight, sum_bias = totals
        grad_hidden, item_at, period = slot_args
        grid_input = jnp.pad(inputs_all[item_at], ((0, GRID - STEPS), (0, 0)))
        sum_weight = (
            sum_weight
            + lax.dot_general(
                unfold(grid_input, period, 1),
                grad_hidden,
                contract_rows,
                preferred_element_type=jnp.float32,
            )
            / 6.0
        )
        sum_bias = sum_bias + jnp.sum(grad_hidden.astype(jnp.float32), axis=0)
        grad_input = apply_weight(unfold(grad_hidden, period, -1), conv_in_back) / 6.0
        return ((sum_weight, sum_bias), grad_input[:STEPS].reshape(STEPS * D))

    inner_init = (jnp.zeros((tap_count * D, FF), jnp.float32), jnp.zeros((FF,), jnp.float32))
    (grad_conv_in, grad_bias_in), grad_slots = lax.scan(
        inner_step, inner_init, (grad_hidden_all, item_index, slot_period)
    )
    partial_input = jnp.dot(own_onehot, grad_slots, precision=highest)
    grad_series = (
        lax.psum_scatter(
            partial_input.astype(jnp.bfloat16), "narrow", scatter_dimension=1, tiled=True
        ).astype(jnp.float32)
        + grad_flat
    )
    grad_conv_in, grad_bias_in, grad_conv_out, grad_bias_out, grad_gain, grad_norm_bias = lax.psum(
        (grad_conv_in, grad_bias_in, grad_conv_out, grad_bias_out, grad_gain, grad_norm_bias),
        ("items", "narrow"),
    )
    return (
        output,
        grad_series,
        grad_amplitudes,
        grad_conv_in,
        grad_bias_in,
        grad_conv_out,
        grad_bias_out,
        grad_gain,
        grad_norm_bias,
    )


def solution(mesh):
    in_specs = (
        P("items", None),
        P("items", None),
        P("items", None),
        P(),
        P(),
        P(),
        P(),
        P(),
        P(),
        P("items", "narrow"),
    )
    out_specs = (
        P("items", "narrow"),
        P("items", "narrow"),
        P("items", None),
        P(),
        P(),
        P(),
        P(),
        P(),
        P(),
    )
    return jax.shard_map(
        on_device, mesh=mesh, in_specs=in_specs, out_specs=out_specs, check_vma=False
    )
```

profile of v0, /device:TPU:0, one launch (start us, length us, event | category | flops | bytes accessed | tf_op | source)
XLA Modules:
  0.0 2602.0 jit_solution(262430459755670835)
XLA Ops:
  10.2 816.5 %while.59 = (s32[]{:T(128)}, bf16[3,432,64]{1,2,0:T(8,128)(2,1)S(1)}, f32[3,480,64]{1,2,0:T(8,128)S(1)}, bf16[3,480,64]{1,2,0:T(8,128)(2,1)S(1)}, s32[3]{0:T(128...) while((s32[]{:T(128)}, ...), condition=%wide.region_3.4_spmd, body=%wide.region_2.3_spmd.sunk | while | flops 2339268096 | bytes 195042208 | solution.py:123
  876.0 716.8 %while.60 = (s32[]{:T(128)}, f32[18304,64]{0,1:T(8,128)}, f32[64]{0:T(128)}, bf16[3,480,64]{1,2,0:T(8,128)(2,1)}, s32[3]{0:T(128)S(1)}, /*index=5*/bf16[3,480,64...) while((s32[]{:T(128)}, f32[18304,64]{0,1:T(8,128)}, ...), condition=%wide.region_10.11_spmd.clone, body=%wide.region_8.10_spmd.clone.sunk | while | flops 2332801536 | bytes 138409648 | solution.py:194
  942.0 46.9 %concatenate.114 = bf16[480,16384]{1,0:T(8,128)(2,1)} concatenate(bf16[480,64]{1,0:T(8,128)(2,1)S(1)} %get-tuple-element.2345, bf16[480,64]{1,0:T(8,128)(2,1)S(1)} %get-tuple-element.2346, bf16[480,64]{1,0:T(8,128)(2,1)S(1)} %get-tuple-element.2347, bf16[480,64]{1,0:T(8,128)(2,1)S(1)} %get-tuple-element.2348, bf16[480,64]{1,0:T(8,128)(2,1)S(1)} %get-tuple-element.2349, ...), dimensions={1} | concatenate | bytes 31457280 | tf_op jit(solution)/shard_map/while
  1051.0 47.0 %concatenate.116 = bf16[480,16384]{1,0:T(8,128)(2,1)} concatenate(bf16[480,64]{1,0:T(8,128)(2,1)S(1)} %get-tuple-element.2469, bf16[480,64]{1,0:T(8,128)(2,1)S(1)} %get-tuple-element.2470, bf16[480,64]{1,0:T(8,128)(2,1)S(1)} %get-tuple-element.2471, bf16[480,64]{1,0:T(8,128)(2,1)S(1)} %get-tuple-element.2472, bf16[480,64]{1,0:T(8,128)(2,1)S(1)} %get-tuple-element.2473, ...), dimensions={1} | concatenate | bytes 31457280 | tf_op jit(solution)/shard_map/while
  1179.5 46.9 %concatenate.114 = bf16[480,16384]{1,0:T(8,128)(2,1)} concatenate(bf16[480,64]{1,0:T(8,128)(2,1)S(1)} %get-tuple-element.2345, bf16[480,64]{1,0:T(8,128)(2,1)S(1)} %get-tuple-element.2346, bf16[480,64]{1,0:T(8,128)(2,1)S(1)} %get-tuple-element.2347, bf16[480,64]{1,0:T(8,128)(2,1)S(1)} %get-tuple-element.2348, bf16[480,64]{1,0:T(8,128)(2,1)S(1)} %get-tuple-element.2349, ...), dimensions={1} | concatenate | bytes 31457280 | tf_op jit(solution)/shard_map/while
  1227.4 12.8 fusion.1016
  1290.0 47.0 %concatenate.116 = bf16[480,16384]{1,0:T(8,128)(2,1)} concatenate(bf16[480,64]{1,0:T(8,128)(2,1)S(1)} %get-tuple-element.2469, bf16[480,64]{1,0:T(8,128)(2,1)S(1)} %get-tuple-element.2470, bf16[480,64]{1,0:T(8,128)(2,1)S(1)} %get-tuple-element.2471, bf16[480,64]{1,0:T(8,128)(2,1)S(1)} %get-tuple-element.2472, bf16[480,64]{1,0:T(8,128)(2,1)S(1)} %get-tuple-element.2473, ...), dimensions={1} | concatenate | bytes 31457280 | tf_op jit(solution)/shard_map/while
  1418.5 46.9 %concatenate.114 = bf16[480,16384]{1,0:T(8,128)(2,1)} concatenate(bf16[480,64]{1,0:T(8,128)(2,1)S(1)} %get-tuple-element.2345, bf16[480,64]{1,0:T(8,128)(2,1)S(1)} %get-tuple-element.2346, bf16[480,64]{1,0:T(8,128)(2,1)S(1)} %get-tuple-element.2347, bf16[480,64]{1,0:T(8,128)(2,1)S(1)} %get-tuple-element.2348, bf16[480,64]{1,0:T(8,128)(2,1)S(1)} %get-tuple-element.2349, ...), dimensions={1} | concatenate | bytes 31457280 | tf_op jit(solution)/shard_map/while
  1466.5 12.8 fusion.1016
  1529.1 47.0 %concatenate.116 = bf16[480,16384]{1,0:T(8,128)(2,1)} concatenate(bf16[480,64]{1,0:T(8,128)(2,1)S(1)} %get-tuple-element.2469, bf16[480,64]{1,0:T(8,128)(2,1)S(1)} %get-tuple-element.2470, bf16[480,64]{1,0:T(8,128)(2,1)S(1)} %get-tuple-element.2471, bf16[480,64]{1,0:T(8,128)(2,1)S(1)} %get-tuple-element.2472, bf16[480,64]{1,0:T(8,128)(2,1)S(1)} %get-tuple-element.2473, ...), dimensions={1} | concatenate | bytes 31457280 | tf_op jit(solution)/shard_map/while
  1592.8 713.2 %while.61 = (s32[]{:T(128)}, f32[18304,64]{0,1:T(8,128)}, f32[64]{0:T(128)}, f32[3,27648]{1,0:T(4,128)}, s32[3]{0:T(128)S(1)}, /*index=5*/bf16[1,432,64]{2,1,0:T...) while((s32[]{:T(128)}, f32[18304,64]{0,1:T(8,128)}, ...), condition=%wide.region_13.14_spmd.clone, body=%wide.region_11.13_spmd.clone.sunk | while | flops 2330561536 | bytes 135547120 | solution.py:217
  1663.4 48.3 %concatenate.118 = bf16[480,16384]{1,0:T(8,128)(2,1)} concatenate(bf16[480,64]{1,0:T(8,128)(2,1)S(1)} %get-tuple-element.2609, bf16[480,64]{1,0:T(8,128)(2,1)S(1)} %get-tuple-element.2610, bf16[480,64]{1,0:T(8,128)(2,1)S(1)} %get-tuple-element.2611, bf16[480,64]{1,0:T(8,128)(2,1)S(1)} %get-tuple-element.2612, bf16[480,64]{1,0:T(8,128)(2,1)S(1)} %get-tuple-element.2613, ...), dimensions={1} | concatenate | bytes 31457280 | tf_op jit(solution)/shard_map/while
  1770.8 46.9 %concatenate.120 = bf16[480,16384]{1,0:T(8,128)(2,1)} concatenate(bf16[480,64]{1,0:T(8,128)(2,1)S(1)} %get-tuple-element.2730, bf16[480,64]{1,0:T(8,128)(2,1)S(1)} %get-tuple-element.2731, bf16[480,64]{1,0:T(8,128)(2,1)S(1)} %get-tuple-element.2732, bf16[480,64]{1,0:T(8,128)(2,1)S(1)} %get-tuple-element.2733, bf16[480,64]{1,0:T(8,128)(2,1)S(1)} %get-tuple-element.2734, ...), dimensions={1} | concatenate | bytes 31457280 | tf_op jit(solution)/shard_map/while
  1817.7 13.0 fusion.1068
  1896.6 48.3 %concatenate.118 = bf16[480,16384]{1,0:T(8,128)(2,1)} concatenate(bf16[480,64]{1,0:T(8,128)(2,1)S(1)} %get-tuple-element.2609, bf16[480,64]{1,0:T(8,128)(2,1)S(1)} %get-tuple-element.2610, bf16[480,64]{1,0:T(8,128)(2,1)S(1)} %get-tuple-element.2611, bf16[480,64]{1,0:T(8,128)(2,1)S(1)} %get-tuple-element.2612, bf16[480,64]{1,0:T(8,128)(2,1)S(1)} %get-tuple-element.2613, ...), dimensions={1} | concatenate | bytes 31457280 | tf_op jit(solution)/shard_map/while
  2004.7 46.9 %concatenate.120 = bf16[480,16384]{1,0:T(8,128)(2,1)} concatenate(bf16[480,64]{1,0:T(8,128)(2,1)S(1)} %get-tuple-element.2730, bf16[480,64]{1,0:T(8,128)(2,1)S(1)} %get-tuple-element.2731, bf16[480,64]{1,0:T(8,128)(2,1)S(1)} %get-tuple-element.2732, bf16[480,64]{1,0:T(8,128)(2,1)S(1)} %get-tuple-element.2733, bf16[480,64]{1,0:T(8,128)(2,1)S(1)} %get-tuple-element.2734, ...), dimensions={1} | concatenate | bytes 31457280 | tf_op jit(solution)/shard_map/while
  2051.6 13.0 fusion.1068
  2130.5 48.3 %concatenate.118 = bf16[480,16384]{1,0:T(8,128)(2,1)} concatenate(bf16[480,64]{1,0:T(8,128)(2,1)S(1)} %get-tuple-element.2609, bf16[480,64]{1,0:T(8,128)(2,1)S(1)} %get-tuple-element.2610, bf16[480,64]{1,0:T(8,128)(2,1)S(1)} %get-tuple-element.2611, bf16[480,64]{1,0:T(8,128)(2,1)S(1)} %get-tuple-element.2612, bf16[480,64]{1,0:T(8,128)(2,1)S(1)} %get-tuple-element.2613, ...), dimensions={1} | concatenate | bytes 31457280 | tf_op jit(solution)/shard_map/while
  2238.6 46.9 %concatenate.120 = bf16[480,16384]{1,0:T(8,128)(2,1)} concatenate(bf16[480,64]{1,0:T(8,128)(2,1)S(1)} %get-tuple-element.2730, bf16[480,64]{1,0:T(8,128)(2,1)S(1)} %get-tuple-element.2731, bf16[480,64]{1,0:T(8,128)(2,1)S(1)} %get-tuple-element.2732, bf16[480,64]{1,0:T(8,128)(2,1)S(1)} %get-tuple-element.2733, bf16[480,64]{1,0:T(8,128)(2,1)S(1)} %get-tuple-element.2734, ...), dimensions={1} | concatenate | bytes 31457280 | tf_op jit(solution)/shard_map/while
  2285.5 13.0 fusion.1068
  2307.7 14.3 reshape_bitcast_fusion
  2327.9 42.0 %all-reduce.9 = (f32[64]{0:T(128)}, f32[64]{0:T(128)}, f32[64]{0:T(128)}, f32[64]{0:T(128)}) all-reduce(f32[64]{0:T(128)S(1)} %copy-done.39, f32[64]{0:T(128)S(1)} %copy-done.42, f32[64]{0:T(128)S(1)} %copy-done.48, f32[64]{0:T(128)S(1)} %reduce_sum.119), channel_id=1, replica_groups=mesh['items'=16,'narrow'=2] {'items','narrow'}, use_global_device_ids=true, to_apply=%region_19.20 | all-reduce | flops 256 | bytes 2048 | tf_op jit(solution)/shard_map/psum | solution.py:227
  2374.4 43.7 %reduce-scatter.4.cloned.1.call-done = bf16[13824,1]{1,0:T(8,128)(2,1)} async-done(((bf16[27648,1]{1,0:T(8,128)(2,1)}), bf16[13824,1]{1,0:T(8,128)(2,1)}) %reduce-scatter.4.cloned.1.call-update) | async-done | bytes 27664
  2422.1 162.5 %all-reduce.13.cloned.1.call-done = (f32[18304,64]{0,1:T(8,128)}, f32[18304,64]{0,1:T(8,128)}) async-done(((f32[18304,64]{0,1:T(8,128)}, f32[18304,64]{0,1:T(8,128)}), (f32[18304,64]{0,1:T(8,128)}, f32[18304,64]{0,1:T(8,128)})) %all-reduce.13.cloned.1.call-update) | async-done | bytes 9371664 | tf_op jit(solution)/shard_map/psum | solution.py:227
  (2302 shorter events, 1564.8 us)
Async XLA Ops:
  10.2 836.1 %copy-start.45 = (f32[1,5]{1,0:T(1,128)S(1)}, f32[1,5]{1,0:T(1,128)}, u32[]{:S(2)}) copy-start(f32[1,5]{1,0:T(1,128)} %param.17) | copy-start | bytes 64
  44.4 183.0 %copy-start.6 = (bf16[18304,64]{0,1:T(8,128)(2,1)S(1)}, bf16[18304,64]{0,1:T(8,128)(2,1)}, u32[]{:S(2)}) copy-start(bf16[18304,64]{0,1:T(8,128)(2,1)} %get-tuple-element.2895) | copy-start | bytes 7028740 | tf_op jit(solution)/shard_map/while
  44.4 183.0 %copy-start.56 = (f32[64]{0:T(128)S(1)}, f32[64]{0:T(128)}, u32[]{:S(2)}) copy-start(f32[64]{0:T(128)} %get-tuple-element.2896) | copy-start | bytes 772 | tf_op jit(solution)/shard_map/while
  314.1 183.0 %copy-start.6 = (bf16[18304,64]{0,1:T(8,128)(2,1)S(1)}, bf16[18304,64]{0,1:T(8,128)(2,1)}, u32[]{:S(2)}) copy-start(bf16[18304,64]{0,1:T(8,128)(2,1)} %get-tuple-element.2895) | copy-start | bytes 7028740 | tf_op jit(solution)/shard_map/while
  314.1 183.0 %copy-start.56 = (f32[64]{0:T(128)S(1)}, f32[64]{0:T(128)}, u32[]{:S(2)}) copy-start(f32[64]{0:T(128)} %get-tuple-element.2896) | copy-start | bytes 772 | tf_op jit(solution)/shard_map/while
  583.8 183.2 %copy-start.6 = (bf16[18304,64]{0,1:T(8,128)(2,1)S(1)}, bf16[18304,64]{0,1:T(8,128)(2,1)}, u32[]{:S(2)}) copy-start(bf16[18304,64]{0,1:T(8,128)(2,1)} %get-tuple-element.2895) | copy-start | bytes 7028740 | tf_op jit(solution)/shard_map/while
  583.8 183.2 %copy-start.56 = (f32[64]{0:T(128)S(1)}, f32[64]{0:T(128)}, u32[]{:S(2)}) copy-start(f32[64]{0:T(128)} %get-tuple-element.2896) | copy-start | bytes 772 | tf_op jit(solution)/shard_map/while
  826.7 38.1 %copy-start.55 = (f32[3,480,64]{1,2,0:T(8,128)}, f32[3,480,64]{1,2,0:T(8,128)S(1)}, u32[]{:S(2)}) copy-start(f32[3,480,64]{1,2,0:T(8,128)S(1)} %get-tuple-element.2930) | copy-start | bytes 1105924
  828.0 36.8 %all-to-all-start = ((bf16[3,2,13824]{2,0,1:T(4,128)(2,1)}), bf16[3,2,13824]{2,0,1:T(4,128)(2,1)S(1)}, u32[]{:S(2)}, u32[]{:S(2)}) async-start(bf16[3,2,13824]{2,0,1:T(4,128)(2,1)} %copy.46), calls=%async_computation | async-start | bytes 442368 | tf_op jit(solution)/shard_map/all_to_all | solution.py:131
  832.2 1585.8 %reduce-scatter.4.cloned.1.call-start = ((), (), s32[]{:S(2)}) async-start(), calls=%async_computation.2 | async-start | bytes 10616832
  876.0 716.8 %copy-start.3 = (bf16[1,432,64]{2,1,0:T(8,128)(2,1)S(1)}, bf16[1,432,64]{2,1,0:T(8,128)(2,1)}, u32[]{:S(2)}) copy-start(bf16[1,432,64]{2,1,0:T(8,128)(2,1)} %copy-done.2) | copy-start | bytes 165892
  990.0 38.5 %copy-start.20 = (pred[480]{0:T(512)(128)(4,1)S(1)}, pred[480]{0:T(512)(128)(4,1)}, u32[]{:S(2)}) copy-start(pred[480]{0:T(512)(128)(4,1)} %copy-done.19) | copy-start | bytes 1444 | tf_op jit(solution)/shard_map/while
  1227.4 37.3 %copy-start.18 = (pred[480]{0:T(512)(128)(4,1)S(1)}, pred[480]{0:T(512)(128)(4,1)}, u32[]{:S(2)}) copy-start(pred[480]{0:T(512)(128)(4,1)} %copy-done.17) | copy-start | bytes 1444 | tf_op jit(solution)/shard_map/while
  1227.4 40.1 %copy-start.20 = (pred[480]{0:T(512)(128)(4,1)S(1)}, pred[480]{0:T(512)(128)(4,1)}, u32[]{:S(2)}) copy-start(pred[480]{0:T(512)(128)(4,1)} %copy-done.19) | copy-start | bytes 1444 | tf_op jit(solution)/shard_map/while
  1466.4 37.3 %copy-start.18 = (pred[480]{0:T(512)(128)(4,1)S(1)}, pred[480]{0:T(512)(128)(4,1)}, u32[]{:S(2)}) copy-start(pred[480]{0:T(512)(128)(4,1)} %copy-done.17) | copy-start | bytes 1444 | tf_op jit(solution)/shard_map/while
  1466.5 37.3 %copy-start.22 = (pred[480]{0:T(512)(128)(4,1)S(1)}, pred[480]{0:T(512)(128)(4,1)}, u32[]{:S(2)}) copy-start(pred[480]{0:T(512)(128)(4,1)} %copy-done.21) | copy-start | bytes 1444 | tf_op jit(solution)/shard_map/while
  1466.5 40.1 %copy-start.20 = (pred[480]{0:T(512)(128)(4,1)S(1)}, pred[480]{0:T(512)(128)(4,1)}, u32[]{:S(2)}) copy-start(pred[480]{0:T(512)(128)(4,1)} %copy-done.19) | copy-start | bytes 1444 | tf_op jit(solution)/shard_map/while
  1604.7 38.2 %copy-start.13 = (pred[480]{0:T(512)(128)(4,1)}, pred[480]{0:T(512)(128)(4,1)S(1)}, u32[]{:S(2)}) copy-start(pred[480]{0:T(512)(128)(4,1)S(1)} %get-tuple-element.2582) | copy-start | bytes 1444 | tf_op jit(solution)/shard_map/while
  1837.9 38.2 %copy-start.13 = (pred[480]{0:T(512)(128)(4,1)}, pred[480]{0:T(512)(128)(4,1)S(1)}, u32[]{:S(2)}) copy-start(pred[480]{0:T(512)(128)(4,1)S(1)} %get-tuple-element.2582) | copy-start | bytes 1444 | tf_op jit(solution)/shard_map/while
  2071.8 38.2 %copy-start.13 = (pred[480]{0:T(512)(128)(4,1)}, pred[480]{0:T(512)(128)(4,1)S(1)}, u32[]{:S(2)}) copy-start(pred[480]{0:T(512)(128)(4,1)S(1)} %get-tuple-element.2582) | copy-start | bytes 1444 | tf_op jit(solution)/shard_map/while
  2306.1 63.9 %copy-start.46 = (f32[1,5]{1,0:T(1,128)S(1)}, f32[1,5]{1,0:T(1,128)}, u32[]{:S(2)}) copy-start(f32[1,5]{1,0:T(1,128)} %param.17) | copy-start | bytes 64
  2306.1 115.3 %copy-start.12 = (f32[1,13824]{1,0:T(1,128)S(1)}, f32[1,13824]{1,0:T(1,128)}, u32[]{:S(2)}) copy-start(f32[1,13824]{1,0:T(1,128)} %copy-done.11) | copy-start | bytes 165892
  2322.1 272.2 %copy-start.1 = (s32[1,5]{1,0:T(1,128)S(1)}, s32[1,5]{1,0:T(1,128)}, u32[]{:S(2)}) copy-start(s32[1,5]{1,0:T(1,128)} %param.18) | copy-start | bytes 64
  2322.1 262.6 %all-reduce.13.cloned.1.call-start = ((), (), s32[]{:S(2)}) async-start(), calls=%async_computation.3 | async-start | bytes 18743296 | tf_op jit(solution)/shard_map/psum | solution.py:227
  (110 other events, 1929.0 us)
Sparse Core Ops, SparseCore 0:
  2322.2 95.8 reduce-scatter.3
Sparse Core Ops, SparseCore 1:
  2330.2 254.5 all-reduce.12
where the time goes:
time: 2640 us; the launch traced here: 2600 us
  other arithmetic  1260 us (48%)
  local copies, waits for them, and re-layouts  729 us (28%)
  waiting for transfers between devices  207 us (8%)
  matrix products  203 us (8%)
  loops' own time  126 us (5%)
  blocking collectives  52 us (2%)
    while x1650, other arithmetic  692 us
    while x246, local copies, waits for them, and re-layouts  648 us
    select_n x174, other arithmetic, unfold(): jnp.where(inside[:, None], moved, jnp.zeros((), values.dtype))  512 us
    psum x1, waiting for transfers between devices, on_device(): lax.psum((grad_conv_in, grad_bias_in, grad_conv_out, grad_bias_out, grad_...  163 us
    dot_general x12, matrix products, apply_weight(): product = jnp.dot(unfolded, prepared, preferred_element_type=jnp.float32)  126 us
  transfers between devices with their start and end apart: 3, of which 2 were waited for; matrix products, arithmetic and copies ran while one was open for 2% of the time, Pallas kernels for 0%

commit v1 on v0

v1 whole, which is shorter than its diff:
```python
import functools
import math

import jax
import jax.numpy as jnp
from jax import lax
from jax.experimental import pallas as pl
from jax.experimental.pallas import tpu as pltpu
from jax.sharding import PartitionSpec as P

D = 64
FF = 64
K = 5
TAPS = 286
STEPS = 432
PMAX = 48
GRID = 480
PAIR = 448
HALF = STEPS // 2
LANES = 128
kernel_sizes = (1, 3, 5, 7, 9, 11)
epsilon = 1e-05
f32 = jnp.float32
bf16 = jnp.bfloat16

NEAR = 5 * PMAX
WIDE = 2 * FF // 2 * 6
FULL = 12 * D


def tap_index(size, row, col):
    radius = (size - 1) // 2
    first = sum(k * k for k in kernel_sizes if k < size)
    return first + (row + radius) * size + col + radius


def lane_of(rows):
    return lax.broadcasted_iota(jnp.int32, (rows, LANES), 1)


def low_half(rows):
    return lane_of(rows) < D


def both_halves(v):
    return v + pltpu.roll(v, D, 1)


def four_quarters(v):
    v = v + pltpu.roll(v, 64, 1)
    return v + pltpu.roll(v, 32, 1)


def quarter_select(parts, rows):
    lane = lane_of(rows)
    upper = jnp.where(lane < 96, parts[2], parts[3])
    lower = jnp.where(lane < 32, parts[0], parts[1])
    return jnp.where(lane < 64, lower, upper)


def rounded(v):
    return v.astype(bf16).astype(f32)


def spread_pairs(pairs, ref, start):
    rows = pairs.shape[0]
    other = pltpu.roll(pairs, D, 1)
    low = low_half(rows)
    ref[pl.ds(start, rows, stride=2), :] = jnp.where(low, pairs, other)
    ref[pl.ds(start + 1, rows, stride=2), :] = jnp.where(low, other, pairs)


def gather_pairs(ref, start, rows):
    return jnp.where(
        low_half(rows),
        ref[pl.ds(start, rows, stride=2), :],
        ref[pl.ds(start + 1, rows, stride=2), :],
    )


def combine_tile(load, rows, row, plane):
    low = low_half(rows)
    col0, col1 = 2 * plane - 5, 2 * plane - 4
    even = odd = None
    for size in kernel_sizes:
        radius = (size - 1) // 2
        in0, in1 = abs(col0) <= radius, abs(col1) <= radius
        if abs(row) > radius or not (in0 or in1):
            continue
        first = tap_index(size, row, col0)
        if first % 2 == 0:
            v = load(first // 2)
            if not in0:
                v = jnp.where(low, 0.0, v)
            if not in1:
                v = jnp.where(low, v, 0.0)
            even = v if even is None else even + v
        else:
            left = load(first // 2) if in0 else 0.0
            right = load(first // 2 + 1) if in1 else 0.0
            v = jnp.where(low, right, left)
            odd = v if odd is None else odd + v
    if odd is not None:
        odd = pltpu.roll(odd, D, 1)
        even = odd if even is None else even + odd
    return even


def column_of(period, rows, start):
    position = (lax.broadcasted_iota(jnp.int32, (rows, LANES), 0) + start).astype(f32)
    width = jnp.full((rows, LANES), period, jnp.int32).astype(f32)
    return position - jnp.floor((position + 0.5) / width) * width


def mixing_of(amp):
    shifted = jnp.exp(amp - jnp.max(amp, axis=-1, keepdims=True))
    return shifted / jnp.sum(shifted, axis=-1, keepdims=True)


def gelu_both(v):
    cdf = 0.5 * (1.0 + lax.erf(v * (1.0 / math.sqrt(2.0))))
    density = jnp.exp(-0.5 * v * v) * (1.0 / math.sqrt(2.0 * math.pi))
    return v * cdf, cdf + v * density


def forward_kernel(
    where_ref,
    periods_ref,
    amp_ref,
    x_ref,
    cot_ref,
    conv_in_ref,
    conv_out_ref,
    bias_in_ref,
    bias_out_ref,
    send_ref,
    sum_ref,
    part_ref,
    w1_ref,
    w2_ref,
    ux_ref,
    ua_ref,
    slope_ref,
    xs,
    act,
    act4,
    ys,
    ss,
    c2,
):
    side = where_ref[0]
    half = pl.multiple_of(side * 32, 32)
    for row in range(-5, 6):
        at = (row + 5) * 32
        for plane in range(6):
            lanes = slice(plane * LANES, (plane + 1) * LANES)

            def load_in(tile):
                return conv_in_ref[pl.ds(half, 32), tile * LANES : (tile + 1) * LANES].astype(f32)

            def load_out(tile):
                return conv_out_ref[:, tile * LANES : (tile + 1) * LANES].astype(f32)

            w1_ref[at : at + 32, lanes] = combine_tile(load_in, 32, row, plane).astype(bf16)
            c2[2 * at : 2 * at + 64, lanes] = combine_tile(load_out, 64, row, plane).astype(bf16)
    w1_ref[352:384, :] = jnp.zeros((32, FULL), bf16)
    c2[704:768, :] = jnp.zeros((64, FULL), bf16)
    source = lax.broadcasted_iota(jnp.int32, (FULL, WIDE), 0)
    target = lax.broadcasted_iota(jnp.int32, (FULL, WIDE), 1)
    wanted = (target // 32) * 64 + side * 32 + target % 32
    choose = (source == wanted).astype(f32).astype(bf16)
    w2_ref[...] = jnp.dot(c2[...], choose, preferred_element_type=f32).astype(bf16)

    xs[...] = jnp.zeros_like(xs)
    act[...] = jnp.zeros_like(act)
    ys[...] = jnp.zeros_like(ys)
    spread_pairs(x_ref[...].astype(f32), xs, 16)
    bias_in = jnp.concatenate([bias_in_ref[...], bias_in_ref[...]], axis=1)
    bias_in = jnp.where(side == 0, bias_in, pltpu.roll(bias_in, 96, 1))
    bias_in = four_quarters(jnp.where(lane_of(1) < 32, bias_in, 0.0))
    bias_out = jnp.concatenate([bias_out_ref[...], bias_out_ref[...]], axis=1)
    bias_out = jnp.where(side == 0, bias_out, 0.0)
    mixing = mixing_of(amp_ref[...])
    sum_ref[...] = jnp.zeros_like(sum_ref)
    step = 48

    def branch(k, carry):
        period = periods_ref[0, k]
        weight = jnp.sum(
            jnp.where(lax.broadcasted_iota(jnp.int32, (1, K), 1) == k, mixing, 0.0),
            axis=1,
            keepdims=True,
        )
        rows_used = lax.div(STEPS + period - 1, period) * period
        width = jnp.full((step, LANES), period, jnp.int32).astype(f32)
        low = low_half(step)
        lane = lane_of(step)
        for t in range(0, GRID, step):
            col = column_of(period, step, t) + jnp.where(low, 0.0, 1.0)
            for plane in range(6):
                shift = 2 * plane - 5
                moved = jnp.where(low, xs[pl.ds(16 + t + shift, step), :], xs[pl.ds(17 + t + shift, step), :])
                c = col + shift
                ux_ref[k, t : t + step, plane * LANES : (plane + 1) * LANES] = jnp.where(
                    (c >= 0.0) & (c < width), moved, 0.0
                ).astype(bf16)
        product = lax.dot_general(
            ux_ref[k], w1_ref[...], (((1,), (1,)), ((), ())), preferred_element_type=f32
        )
        for plane in range(3):
            ys[plane, NEAR : NEAR + GRID, :] = product[:, plane * LANES : (plane + 1) * LANES]
        for t in range(0, GRID + 3 * PMAX, step):
            total = ys[0, pl.ds(NEAR + t - 5 * period, step), :]
            for plane in range(1, 3):
                total = total + ys[plane, pl.ds(NEAR + t + (4 * plane - 5) * period, step), :]
            ss[t : t + step, :] = total
        for t in range(0, GRID, step):
            parts = [ss[pl.ds(t + q * period, step), :] for q in range(4)]
            hidden = four_quarters(quarter_select(parts, step)) / 6.0 + bias_in
            inside = lax.broadcasted_iota(jnp.int32, (step, LANES), 0) + t < rows_used
            active, slope = gelu_both(hidden)
            act[16 + t : 16 + t + step, :] = jnp.where(inside, rounded(active), 0.0)
            slope_ref[k, t : t + step, :] = jnp.where(inside, slope, 0.0)
        for t in range(0, 496, 16):
            parts = [act[pl.ds(8 + t + q, 16), :] for q in range(4)]
            act4[t : t + 16, :] = quarter_select(parts, 16)
        for t in range(0, GRID, step):
            col = column_of(period, step, t) + (lane // 32).astype(f32)
            for plane in range(3):
                shift = 4 * plane - 5
                c = col + shift
                ua_ref[k, t : t + step, plane * LANES : (plane + 1) * LANES] = jnp.where(
                    (c >= 0.0) & (c < width), act4[pl.ds(8 + t + shift, step), :], 0.0
                ).astype(bf16)
        product = lax.dot_general(
            ua_ref[k], w2_ref[...], (((1,), (1,)), ((), ())), preferred_element_type=f32
        )
        for plane in range(6):
            ys[plane, NEAR : NEAR + GRID, :] = product[:, plane * LANES : (plane + 1) * LANES]
        for t in range(0, GRID + PMAX, step):
            total = ys[0, pl.ds(NEAR + t - 5 * period, step), :]
            for plane in range(1, 6):
                total = total + ys[plane, pl.ds(NEAR + t + (2 * plane - 5) * period, step), :]
            ss[t : t + step, :] = total
        for t in range(0, PAIR, 56):
            own = jnp.where(low_half(56), ss[pl.ds(t, 56), :], ss[pl.ds(t + period, 56), :])
            out = both_halves(own) / 6.0 + bias_out
            part_ref[k, t : t + 56, :] = out
            sum_ref[t : t + 56, :] += weight * out
        return carry

    lax.fori_loop(0, K, branch, 0)
    send_ref[0 : PAIR // 2, :] = gather_pairs(sum_ref, 0, PAIR // 2).astype(bf16)
    send_ref[PAIR // 2 :, :] = cot_ref[...]


def backward_kernel(
    where_ref,
    periods_ref,
    amp_ref,
    x_ref,
    cot_ref,
    recv_ref,
    sum_ref,
    part_ref,
    w1_ref,
    w2_ref,
    ux_ref,
    ua_ref,
    slope_ref,
    gain_ref,
    shift_ref,
    out_ref,
    keep_ref,
    send_ref,
    own_ref,
    other_ref,
    dots_ref,
    merged,
    cot,
    outs,
    gm,
    rowed,
    gb,
    gab,
    gah,
    zs,
    vs,
    gh,
    hrow,
    dw1,
    dw2,
    zsum,
    small,
):
    side = where_ref[0]
    core = where_ref[1]
    step = 48
    spread_pairs(recv_ref[0 : PAIR // 2, :].astype(f32), merged, 0)
    spread_pairs(x_ref[...].astype(f32), outs, 0)
    mine = cot_ref[...].astype(f32)
    theirs = recv_ref[PAIR // 2 :, :].astype(f32)
    cot[...] = jnp.zeros_like(cot)
    spread_pairs(jnp.where(side == 0, mine, theirs), cot, 0)
    spread_pairs(jnp.where(side == 0, theirs, mine), cot, HALF)
    gain = jnp.concatenate([gain_ref[...], gain_ref[...]], axis=1)
    shift = jnp.concatenate([shift_ref[...], shift_ref[...]], axis=1)
    mixing = mixing_of(amp_ref[...])
    gm[...] = jnp.zeros_like(gm)
    small[...] = jnp.zeros_like(small)
    dots_ref[...] = jnp.zeros_like(dots_ref)
    rowed[...] = jnp.zeros_like(rowed)
    hrow[...] = jnp.zeros_like(hrow)
    gh[...] = jnp.zeros_like(gh)
    zs[...] = jnp.zeros_like(zs)
    zsum[...] = jnp.zeros_like(zsum)
    dw1[...] = jnp.zeros_like(dw1)
    dw2[...] = jnp.zeros_like(dw2)
    for t in range(0, PAIR, 56):
        rows = slice(t, t + 56)
        total = merged[rows, :] + outs[rows, :] + sum_ref[rows, :]
        centred = total - jnp.mean(total, axis=-1, keepdims=True)
        variance = jnp.mean(centred * centred, axis=-1, keepdims=True)
        inverse = lax.rsqrt(variance + epsilon)
        normed = centred * inverse
        outs[rows, :] = normed * gain + shift
        c = cot[rows, :]
        small[2:3, :] += jnp.sum(c * normed, axis=0, keepdims=True)
        small[3:4, :] += jnp.sum(c, axis=0, keepdims=True)
        e = c * gain
        grad = inverse * (
            e
            - jnp.mean(e, axis=-1, keepdims=True)
            - normed * jnp.mean(e * normed, axis=-1, keepdims=True)
        )
        gm[PMAX + t : PMAX + t + 56, :] = grad
        for k in range(K):
            dots_ref[k : k + 1, :] += jnp.sum(grad * part_ref[k, rows, :], axis=0, keepdims=True)
    first = pl.multiple_of(side * HALF, 8)
    out_ref[...] = gather_pairs(outs, first, 112).astype(bf16)

    def branch(k, carry):
        period = periods_ref[0, k]
        weight = jnp.sum(
            jnp.where(lax.broadcasted_iota(jnp.int32, (1, K), 1) == k, mixing, 0.0),
            axis=1,
            keepdims=True,
        )
        width = jnp.full((step, LANES), period, jnp.int32).astype(f32)
        low = low_half(step)
        lane = lane_of(step)
        for t in range(0, GRID, step):
            here = rounded(weight * gm[PMAX + t : PMAX + t + step, :])
            back = rounded(weight * gm[pl.ds(PMAX + t - period, step), :])
            small[1:2, :] += jnp.sum(here, axis=0, keepdims=True)
            rowed[NEAR + t : NEAR + t + step, :] = jnp.where(low, here, back)
        for t in range(0, GRID, step):
            for plane in range(6):
                gab[t : t + step, plane * LANES : (plane + 1) * LANES] = rowed[
                    pl.ds(NEAR + t - (2 * plane - 5) * period, step), :
                ].astype(bf16)
        product = jnp.dot(gab[...], w2_ref[...], preferred_element_type=f32)
        for t in range(0, GRID, step):
            col = column_of(period, step, t) + (lane // 32).astype(f32)
            for plane in range(3):
                c = col + (4 * plane - 5)
                zs[plane, 16 + t : 16 + t + step, :] = jnp.where(
                    (c >= 0.0) & (c < width),
                    product[t : t + step, plane * LANES : (plane + 1) * LANES],
                    0.0,
                )
        dw2[...] += lax.dot_general(
            ua_ref[k], gab[...], (((0,), (0,)), ((), ())), preferred_element_type=f32
        )
        for t in range(0, 496, 16):
            total = zs[0, pl.ds(16 - 8 + t + 5, 16), :]
            for plane in range(1, 3):
                total = total + zs[plane, pl.ds(16 - 8 + t - (4 * plane - 5), 16), :]
            vs[t : t + 16, :] = total
        for t in range(0, GRID, step):
            parts = [vs[pl.ds(8 + t - q, step), :] for q in range(4)]
            back = four_quarters(quarter_select(parts, step)) / 6.0
            grad = rounded(back * slope_ref[k, t : t + step, :])
            small[0:1, :] += jnp.sum(grad, axis=0, keepdims=True)
            gh[3 * PMAX + t : 3 * PMAX + t + step, :] = grad
        for t in range(0, GRID + 3 * PMAX, step):
            parts = [gh[pl.ds(3 * PMAX + t - q * period, step), :] for q in range(4)]
            hrow[3 * PMAX + t : 3 * PMAX + t + step, :] = quarter_select(parts, step)
        for t in range(0, GRID, step):
            for plane in range(3):
                gah[t : t + step, plane * LANES : (plane + 1) * LANES] = hrow[
                    pl.ds(3 * PMAX + t - (4 * plane - 5) * period, step), :
                ].astype(bf16)
        dw1[...] += lax.dot_general(
            gah[...], ux_ref[k], (((0,), (0,)), ((), ())), preferred_element_type=f32
        )
        product = jnp.dot(gah[...], w1_ref[...], preferred_element_type=f32)
        for t in range(0, GRID, step):
            col = column_of(period, step, t) + jnp.where(low, 0.0, 1.0)
            for plane in range(6):
                c = col + (2 * plane - 5)
                zsum[plane, 16 + t : 16 + t + step, :] += jnp.where(
                    (c >= 0.0) & (c < width),
                    product[t : t + step, plane * LANES : (plane + 1) * LANES],
                    0.0,
                )
        return carry

    lax.fori_loop(0, K, branch, 0)
    for t in range(0, 464, 16):
        total = zsum[0, pl.ds(16 - 8 + t + 5, 16), :]
        for plane in range(1, 6):
            total = total + zsum[plane, pl.ds(16 - 8 + t - (2 * plane - 5), 16), :]
        vs[t : t + 16, :] = total
    for t in range(0, PAIR, 56):
        own = jnp.where(low_half(56), vs[pl.ds(8 + t, 56), :], vs[pl.ds(8 + t - 1, 56), :])
        merged[t : t + 56, :] = both_halves(own) / 6.0
    for t in range(0, PAIR, 56):
        outs[t : t + 56, :] = merged[t : t + 56, :] + gm[PMAX + t : PMAX + t + 56, :]
    own_ref[...] = gather_pairs(outs, first, 112)
    last = pl.multiple_of((1 - side) * HALF, 8)
    other_ref[0:112, :] = gather_pairs(merged, last, 112).astype(bf16)
    dots = dots_ref[...] * 0.5
    total = jnp.broadcast_to(jnp.sum(dots, axis=1, keepdims=True), dots.shape)
    dots_ref[...] = total
    upper = rounded(total)
    other_ref[112:128, :] = jnp.concatenate([upper, total - upper], axis=0).astype(bf16)

    first_grad = dw1[...] * (1.0 / 6.0)
    second_grad = dw2[...] * (1.0 / 6.0)
    for rows in range(0, 384, 96):
        part = slice(rows, rows + 96)
        a = first_grad[part, :]
        b = second_grad[part, :]
        keep_ref[part, :] = jnp.where(core == 0, a, b).astype(bf16)
        send_ref[part, :] = jnp.where(core == 0, b, a).astype(bf16)
    spare = jnp.concatenate([small[...], jnp.zeros((8, LANES), f32)], axis=0).astype(bf16)

    @pl.when(core == 0)
    def _():
        keep_ref[352:368, 0:LANES] = spare

    @pl.when(core != 0)
    def _():
        send_ref[352:368, 0:LANES] = spare

    if keep_ref.shape[0] > 384:
        tail = jnp.zeros((keep_ref.shape[0] - 384, FULL), bf16)
        keep_ref[384:, :] = tail
        send_ref[384:, :] = tail


def final_kernel(
    places,
    block,
    where_ref,
    amp_ref,
    mine_ref,
    theirs_ref,
    own_ref,
    recv_ref,
    dots_ref,
    grad_in_ref,
    grad_out_ref,
    bias_in_ref,
    bias_out_ref,
    gain_ref,
    shift_ref,
    series_ref,
    amps_ref,
    first,
    second,
    c1,
    c1r,
    merged,
):
    core = where_ref[1]
    low = low_half(64)
    for half, target in ((0, first), (1, second)):
        for side in range(2):
            for index, place in enumerate(places[half][side]):
                if index * block >= 384:
                    continue
                a = mine_ref[place * block : (place + 1) * block, :]
                b = theirs_ref[place * block : (place + 1) * block, :]
                value = jnp.where(core == 0, a, b) if half == 0 else jnp.where(core == 0, b, a)
                target[side, index * block : (index + 1) * block, :] = value

    def expand(grad_ref):
        for tile in range(TAPS // 2):
            found = []
            for tap in (2 * tile, 2 * tile + 1):
                for size in kernel_sizes:
                    inside = tap - tap_index(size, -(size // 2), -(size // 2))
                    if 0 <= inside < size * size:
                        found.append(
                            (inside // size - size // 2 + 5, inside % size - size // 2 + 5)
                        )
            (a0, b0), (a1, b1) = found
            left = (c1 if b0 % 2 == 0 else c1r)[a0, b0 // 2]
            right = (c1 if b1 % 2 == 1 else c1r)[a1, b1 // 2]
            grad_ref[:, tile * LANES : (tile + 1) * LANES] = jnp.where(low, left, right)

    for row in range(11):
        for plane in range(6):
            lanes = slice(plane * LANES, (plane + 1) * LANES)
            for side in range(2):
                v = first[side, row * 32 : (row + 1) * 32, lanes].astype(f32)
                c1[row, plane, side * 32 : (side + 1) * 32, :] = v
                c1r[row, plane, side * 32 : (side + 1) * 32, :] = pltpu.roll(v, D, 1)
    expand(grad_in_ref)

    source = lax.broadcasted_iota(jnp.int32, (WIDE, FULL), 0)
    target = lax.broadcasted_iota(jnp.int32, (WIDE, FULL), 1)
    merge = None
    for side in range(2):
        wanted = (source // 32) * 64 + side * 32 + source % 32
        place = (target == wanted).astype(f32).astype(bf16)
        part = lax.dot_general(
            second[side], place, (((0,), (0,)), ((), ())), preferred_element_type=f32
        )
        merge = part if merge is None else merge + part
    merged[...] = merge
    for row in range(11):
        for plane in range(6):
            v = merged[row * 64 : (row + 1) * 64, plane * LANES : (plane + 1) * LANES]
            c1[row, plane] = v
            c1r[row, plane] = pltpu.roll(v, D, 1)
    expand(grad_out_ref)

    spare = first[0, 352:368, 0:LANES].astype(f32)
    other = first[1, 352:368, 0:LANES].astype(f32)
    bias_in_ref[...] = jnp.concatenate([spare[0:1, 0:32], other[0:1, 0:32]], axis=1)
    bias_out_ref[...] = spare[1:2, 0:64]
    gain_ref[...] = spare[2:3, 0:64]
    shift_ref[...] = spare[3:4, 0:64]
    series_ref[...] = own_ref[...] + recv_ref[0:112, :].astype(f32)
    tail = recv_ref[112:128, :].astype(f32)
    dots = dots_ref[...] + tail[0:8, :] + tail[8:16, :]
    mixing = mixing_of(amp_ref[...])
    pick = (
        lax.broadcasted_iota(jnp.int32, (8, K), 0) == lax.broadcasted_iota(jnp.int32, (8, K), 1)
    )
    table = jnp.sum(jnp.where(pick, dots[:, 0:K], 0.0), axis=0, keepdims=True)
    amps_ref[...] = mixing * (table - jnp.sum(mixing * table, axis=-1, keepdims=True))


def on_device(
    series,
    amplitudes,
    periods,
    conv_in,
    bias_in,
    conv_out,
    bias_out,
    norm_gain,
    norm_bias,
    cotangent,
):
    items = lax.axis_size("items")
    bits = items.bit_length() - 1
    me = lax.axis_index("items")
    side = lax.axis_index("narrow")
    core = me % 2
    where = jnp.stack([side, core]).astype(jnp.int32)
    vmem = pl.BlockSpec(memory_space=pltpu.VMEM)
    smem = pl.BlockSpec(memory_space=pltpu.SMEM)
    big = pltpu.CompilerParams(vmem_limit_bytes=58 * 1024 * 1024)
    shape = jax.ShapeDtypeStruct

    x_pairs = jnp.pad(series.reshape(HALF, LANES), ((0, 8), (0, 0)))
    cot_pairs = jnp.pad(cotangent.reshape(HALF // 2, LANES), ((0, 4), (0, 0)))
    in_flat = conv_in.T
    out_flat = conv_out.T

    send, total, part, w1, w2, ux, ua, slope = pl.pallas_call(
        forward_kernel,
        out_shape=(
            shape((PAIR // 2 + 112, LANES), bf16),
            shape((PAIR, LANES), f32),
            shape((K, PAIR, LANES), f32),
            shape((WIDE, FULL), bf16),
            shape((FULL, WIDE), bf16),
            shape((K, GRID, FULL), bf16),
            shape((K, GRID, WIDE), bf16),
            shape((K, GRID, LANES), f32),
        ),
        in_specs=[smem, smem] + [vmem] * 7,
        out_specs=[vmem] * 8,
        scratch_shapes=[
            pltpu.VMEM((512, LANES), f32),
            pltpu.VMEM((512, LANES), f32),
            pltpu.VMEM((496, LANES), f32),
            pltpu.VMEM((6, NEAR + GRID + 336, LANES), f32),
            pltpu.VMEM((GRID + 3 * PMAX, LANES), f32),
            pltpu.VMEM((FULL, FULL), bf16),
        ],
        compiler_params=big,
        name="forward",
    )(
        where,
        periods,
        amplitudes,
        x_pairs,
        cot_pairs,
        in_flat,
        out_flat,
        bias_in[None, :],
        bias_out[None, :],
    )

    def exchange(value, partner):
        pairs = []
        for item in range(items):
            for col in range(2):
                to_item, to_col = partner(item, col)
                pairs.append((item * 2 + col, to_item * 2 + to_col))
        return lax.ppermute(value, ("items", "narrow"), pairs)

    across = lambda item, col: (item, 1 - col)
    recv = exchange(send, across)

    blocks = 2 ** max(bits - 1, 0)
    block = -(-384 // (16 * blocks)) * 16
    rows = block * blocks
    out_pairs, keep, give, own, other, dots = pl.pallas_call(
        backward_kernel,
        out_shape=(
            shape((112, LANES), bf16),
            shape((rows, FULL), bf16),
            shape((rows, FULL), bf16),
            shape((112, LANES), f32),
            shape((128, LANES), bf16),
            shape((8, LANES), f32),
        ),
        in_specs=[smem, smem] + [vmem] * 13,
        out_specs=[vmem] * 6,
        scratch_shapes=[
            pltpu.VMEM((PAIR, LANES), f32),
            pltpu.VMEM((PAIR, LANES), f32),
            pltpu.VMEM((PAIR, LANES), f32),
            pltpu.VMEM((PMAX + GRID, LANES), f32),
            pltpu.VMEM((NEAR + GRID + NEAR, LANES), f32),
            pltpu.VMEM((8, LANES), f32),
            pltpu.VMEM((GRID, FULL), bf16),
            pltpu.VMEM((GRID, WIDE), bf16),
            pltpu.VMEM((3, GRID + 32, LANES), f32),
            pltpu.VMEM((GRID + 16, LANES), f32),
            pltpu.VMEM((3 * PMAX + GRID + 3 * PMAX, LANES), f32),
            pltpu.VMEM((3 * PMAX + GRID + NEAR, LANES), f32),
            pltpu.VMEM((WIDE, FULL), f32),
            pltpu.VMEM((WIDE, FULL), f32),
            pltpu.VMEM((6, GRID + 32, LANES), f32),
            pltpu.VMEM((8, LANES), f32),
        ],
        compiler_params=big,
        name="backward",
    )(
        where,
        periods,
        amplitudes,
        x_pairs,
        cot_pairs,
        recv,
        total,
        part,
        w1,
        w2,
        ux,
        ua,
        slope,
        norm_gain[None, :],
        norm_bias[None, :],
    )

    def partner_of(stage):
        def partner(item, col):
            axis = stage[item % 2]
            if axis is None:
                return (item, 1 - col)
            return (item ^ (1 << axis), col)

        return partner

    def bit_of(stage):
        values = [side if axis is None else (me >> axis) & 1 for axis in stage]
        return jnp.where(core == 0, values[0], values[1])

    received = exchange(other, across)
    order = list(range(1, bits))
    orders = (order, order[1::-1] + order[2:])
    theirs = exchange(give, lambda item, col: (item ^ 1, col)) if bits else jnp.zeros_like(give)
    acc = keep.astype(f32) + theirs.astype(f32)
    for position in range(bits - 1):
        stage = (orders[0][position], orders[1][position])
        bit = bit_of(stage)
        size = acc.shape[0] // 2
        gone = lax.dynamic_slice_in_dim(acc, (1 - bit) * size, size, 0).astype(bf16)
        stay = lax.dynamic_slice_in_dim(acc, bit * size, size, 0)
        acc = stay + exchange(gone, partner_of(stage)).astype(f32)
    mine = acc.astype(bf16)
    back = order[::-1]
    sequences = (back[:1] + [None] + back[1:], back + [None])
    for position in range(len(sequences[0])):
        stage = (sequences[0][position], sequences[1][position])
        bit = bit_of(stage)
        theirs = exchange(mine, partner_of(stage))
        mine = jnp.concatenate(
            [jnp.where(bit == 0, mine, theirs), jnp.where(bit == 0, theirs, mine)], axis=0
        )
    theirs = exchange(mine, lambda item, col: (item ^ 1, col))

    places = []
    for half in range(2):
        by_side = []
        for narrow in range(2):
            listed = []
            for index in range(blocks):
                value = {None: narrow}
                for position, axis in enumerate(orders[half]):
                    value[axis] = (index >> (len(order) - 1 - position)) & 1
                place = 0
                for position, axis in enumerate(sequences[half]):
                    place += value[axis] << position
                listed.append(place)
            by_side.append(tuple(listed))
        places.append(tuple(by_side))

    results = pl.pallas_call(
        functools.partial(final_kernel, tuple(places), block),
        out_shape=(
            shape((FF, TAPS * D), f32),
            shape((D, TAPS * FF), f32),
            shape((1, FF), f32),
            shape((1, D), f32),
            shape((1, D), f32),
            shape((1, D), f32),
            shape((112, LANES), f32),
            shape((1, K), f32),
        ),
        in_specs=[smem] + [vmem] * 6,
        out_specs=[vmem] * 8,
        scratch_shapes=[
            pltpu.VMEM((2, 384, FULL), bf16),
            pltpu.VMEM((2, 384, FULL), bf16),
            pltpu.VMEM((11, 6, 64, LANES), f32),
            pltpu.VMEM((11, 6, 64, LANES), f32),
            pltpu.VMEM((FULL, FULL), f32),
        ],
        compiler_params=big,
        name="final",
    )(where, amplitudes, mine, theirs, own, received, dots)
    grad_in, grad_out, g_bias_in, g_bias_out, g_gain, g_shift, g_series, g_amps = results
    share = HALF * D
    return (
        out_pairs[: HALF // 2].reshape(1, share),
        g_series[: HALF // 2].reshape(1, share),
        g_amps,
        grad_in.T,
        g_bias_in[0],
        grad_out.T,
        g_bias_out[0],
        g_gain[0],
        g_shift[0],
    )


def solution(mesh):
    in_specs = (
        P("items", None),
        P("items", None),
        P("items", None),
        P(),
        P(),
        P(),
        P(),
        P(),
        P(),
        P("items", "narrow"),
    )
    out_specs = (
        P("items", "narrow"),
        P("items", "narrow"),
        P("items", None),
        P(),
        P(),
        P(),
        P(),
        P(),
        P(),
    )
    return jax.shard_map(
        on_device, mesh=mesh, in_specs=in_specs, out_specs=out_specs, check_vma=False
    )
```

time: 2640 us -> 111 us (0.04); the launches traced: 2600 us -> 110 us
  other arithmetic: 1260 us -> 4.61 us
  local copies, waits for them, and re-layouts: 729 us -> 5.71 us
  matrix products: 203 us -> 0 us
  waiting for transfers between devices: 207 us -> 36 us
  loops' own time: 126 us -> 0 us
  blocking collectives: 52 us -> 0 us
  Pallas kernels: 0 us -> 41.6 us
    while x1650 -> x0, other arithmetic: 692 us -> none
    while x248 -> x0, local copies, waits for them, and re-layouts: 649 us -> none
    select_n x175 -> x4, other arithmetic: 512 us -> 0.37 us  [on_device(): jnp.where(bit == 0, mine, theirs)]
    dot_general x21 -> x0, matrix products: 203 us -> none  [the longest x12 126 us: apply_weight(): product = jnp.dot(unfolded, prepared, preferred_element_type=jnp.float32)]
    psum x1 -> x0, waiting for transfers between devices: 163 us -> none  [on_device(): lax.psum((grad_conv_in, grad_bias_in, grad_conv_out, grad_bias_out, grad_...]
    another operation x3 -> x0, loops' own time: 126 us -> none  [the longest x1 46.8 us: on_device(): lax.map(forward_slot, (item_index, slot_period))]
    psum x2 -> x0, blocking collectives: 47 us -> none  [the longest x1 42 us: on_device(): lax.psum((grad_conv_in, grad_bias_in, grad_conv_out, grad_bias_out, grad_...]
    unnamed x3 -> x0, waiting for transfers between devices: 44.2 us -> none
  transfers between devices with their start and end apart: 3 -> 11, of which waited for: 2 -> 10; matrix products, arithmetic and copies ran while one was open for 2% -> 1% of each run, Pallas kernels for 0% -> 0%
where the time goes in v1:
time: 111 us; the launch traced here: 110 us
  Pallas kernels  41.6 us (37%)
  waiting for transfers between devices  36 us (32%)
  starting transfers between devices  21.7 us (20%)
  local copies, waits for them, and re-layouts  5.71 us (5%)
  other arithmetic  4.61 us (4%)
    ppermute x11, waiting for transfers between devices, exchange(): return lax.ppermute(value, ('items', 'narrow'), pairs)  36 us
    ppermute x11, starting transfers between devices, exchange(): return lax.ppermute(value, ('items', 'narrow'), pairs)  21.7 us
    pallas_call x1, Pallas kernels, on_device(): pl.pallas_call(backward_kernel, out_shape=(shape((112, LANES), bf16), sha...  17.8 us
    pallas_call x1, Pallas kernels, on_device(): pl.pallas_call(forward_kernel, out_shape=(shape((PAIR // 2 + 112, LANES),...  17.2 us
    pallas_call x1, Pallas kernels, on_device(): pl.pallas_call(functools.partial(final_kernel, tuple(places), block), out...  6.56 us
    unnamed x16, local copies, waits for them, and re-layouts  4.39 us
  transfers between devices with their start and end apart: 11, of which 10 were waited for; matrix products, arithmetic and copies ran while one was open for 1% of the time, Pallas kernels for 0%

profile of v1, /device:TPU:0, one launch (start us, length us, event | category | flops | bytes accessed | tf_op | source)
XLA Modules:
  0.0 110.4 jit_solution(5501043229705015564)
XLA Ops:
  0.7 1.2 %reduce = bf16[27648]{0:T(1024)(128)(2,1)S(1)} reduce(bf16[1,27648]{1,0:T(2,128)(2,1)} %param.10, bf16[]{:T(256)} %constant.43), dimensions={0}, to_apply=%param.10.reduce_sub_computation | reduce | bytes 110594 | tf_op args[0]
  4.7 17.2 %forward.1 = (bf16[336,128]{1,0:T(8,128)(2,1)}, f32[448,128]{1,0:T(8,128)}, f32[5,448,128]{2,1,0:T(8,128)}, bf16[384,768]{1,0:T(8,128)(2,1)}, bf16[768,384]{1,0:...) custom-call(s32[2]{0:T(128)} %pad_add_fusion.where_ref, ...), custom_call_target="tpu_custom_call" | custom-call | tf_op jit(solution)/shard_map/forward/pallas_call | solution.py:576
  21.9 3.0 %collective-permute-start = (bf16[336,128]{1,0:T(8,128)(2,1)}, bf16[336,128]{1,0:T(8,128)(2,1)S(1)}, u32[]{:S(2)}, u32[]{:S(2)}) collective-permute-start(bf16[336,128]{1,0:T(8,128)(2,1)} %get-tuple-element.31), channel_id=1, source_target_pairs={{0,1},{1,0},{2,3},{3,2},{4,5},{5,4},{6,7},{7,6},{8,9},{9,8},{10,11... | collective-permute-start | bytes 258056 | tf_op jit(solution)/shard_map/ppermute | solution.py:618
  24.9 2.7 %collective-permute-done.recv_ref = bf16[336,128]{1,0:T(8,128)(2,1)S(1)} collective-permute-done((bf16[336,128]{1,0:T(8,128)(2,1)}, bf16[336,128]{1,0:T(8,128)(2,1)S(1)}, u32[]{:S(2)}, u32[]{:S(2)}) %collective-permute-start) | collective-permute-done | bytes 86048 | tf_op jit(solution)/shard_map/ppermute | solution.py:618
  28.2 17.8 %backward.1 = (bf16[112,128]{1,0:T(8,128)(2,1)}, bf16[384,768]{1,0:T(8,128)(2,1)}, bf16[384,768]{1,0:T(8,128)(2,1)}, f32[112,128]{1,0:T(8,128)}, bf16[128,128]{1,0:T(8,128)(2,1)}, /*index=5*/f32[8,128]{1,0:T(8,128)}) custom-call(s32[2]{0:T(128)} %pad_add_fusion.where_ref, s32[1,5]{1,0:T(1,128)} %periods_ref.3, f32[1,5]{1,0:T(1,128)} %amp_ref.5, ...), custom_call_target="tpu_custom_call" | custom-call | tf_op jit(solution)/shard_map/backward/pallas_call | solution.py:626
  46.1 2.2 %collective-permute-done.1 = bf16[384,768]{1,0:T(8,128)(2,1)S(1)} collective-permute-done((bf16[384,768]{1,0:T(8,128)(2,1)}, bf16[384,768]{1,0:T(8,128)(2,1)S(1)}, u32[]{:S(2)}, u32[]{:S(2)}) %collective-permute-start.1) | collective-permute-done | bytes 589856 | tf_op jit(solution)/shard_map/ppermute | solution.py:618
  48.3 1.2 %convert_add_fusion = f32[384,768]{1,0:T(8,128)S(1)} fusion(bf16[384,768]{1,0:T(8,128)(2,1)S(1)} %collective-permute-done.1, bf16[384,768]{1,0:T(8,128)(2,1)} %get-tuple-element.40), kind=kLoop, calls=%fused_computation.1 | loop fusion | flops 884736 | bytes 2359296 | tf_op jit(solution)/shard_map/add | solution.py:693
  49.5 2.0 %collective-permute-start.2 = (bf16[192,768]{1,0:T(8,128)(2,1)S(1)}, bf16[192,768]{1,0:T(8,128)(2,1)S(1)}, u32[]{:S(2)}, u32[]{:S(2)}) collective-permute-start(bf16[192,768]{1,0:T(8,128)(2,1)S(1)} %dynamic-slice_convert_fusion), channel_id=1, source_target_pairs={{0,4},{1,5},{2,10},{3,11},{4,0},{5,1},{6,14},{7,15},{8,12},{9,13},... | collective-permute-start | bytes 884744 | tf_op jit(solution)/shard_map/ppermute | solution.py:618
  51.5 4.8 %collective-permute-done.2 = bf16[192,768]{1,0:T(8,128)(2,1)S(1)} collective-permute-done((bf16[192,768]{1,0:T(8,128)(2,1)S(1)}, bf16[192,768]{1,0:T(8,128)(2,1)S(1)}, u32[]{:S(2)}, u32[]{:S(2)}) %collective-permute-start.2) | collective-permute-done | bytes 294944 | tf_op jit(solution)/shard_map/ppermute | solution.py:618
  56.4 2.1 %collective-permute-start.3 = (bf16[96,768]{1,0:T(8,128)(2,1)S(1)}, bf16[96,768]{1,0:T(8,128)(2,1)S(1)}, u32[]{:S(2)}, u32[]{:S(2)}) collective-permute-start(bf16[96,768]{1,0:T(8,128)(2,1)S(1)} %dynamic-slice_convert_fusion.1), channel_id=1, source_target_pairs={{0,8},{1,9},{2,6},{3,7},{4,12},{5,13},{6,2},{7,3},{8,0},{9,1},{10,... | collective-permute-start | bytes 442376 | tf_op jit(solution)/shard_map/ppermute | solution.py:618
  58.5 3.1 %collective-permute-done.3 = bf16[96,768]{1,0:T(8,128)(2,1)S(1)} collective-permute-done((bf16[96,768]{1,0:T(8,128)(2,1)S(1)}, bf16[96,768]{1,0:T(8,128)(2,1)S(1)}, u32[]{:S(2)}, u32[]{:S(2)}) %collective-permute-start.3) | collective-permute-done | bytes 147488 | tf_op jit(solution)/shard_map/ppermute | solution.py:618
  61.7 3.0 %collective-permute-start.4 = (bf16[48,768]{1,0:T(8,128)(2,1)S(1)}, bf16[48,768]{1,0:T(8,128)(2,1)S(1)}, u32[]{:S(2)}, u32[]{:S(2)}) collective-permute-start(bf16[48,768]{1,0:T(8,128)(2,1)S(1)} %dynamic-slice_convert_fusion.2), channel_id=1, source_target_pairs={{0,16},{1,17},{2,18},{3,19},{4,20},{5,21},{6,22},{7,23},{8,24},{9,... | collective-permute-start | bytes 221192 | tf_op jit(solution)/shard_map/ppermute | solution.py:618
  64.7 2.3 %collective-permute-done.4 = bf16[48,768]{1,0:T(8,128)(2,1)S(1)} collective-permute-done((bf16[48,768]{1,0:T(8,128)(2,1)S(1)}, bf16[48,768]{1,0:T(8,128)(2,1)S(1)}, u32[]{:S(2)}, u32[]{:S(2)}) %collective-permute-start.4) | collective-permute-done | bytes 73760 | tf_op jit(solution)/shard_map/ppermute | solution.py:618
  67.1 3.1 %collective-permute-start.5 = (bf16[48,768]{1,0:T(8,128)(2,1)S(1)}, bf16[48,768]{1,0:T(8,128)(2,1)S(1)}, u32[]{:S(2)}, u32[]{:S(2)}) collective-permute-start(bf16[48,768]{1,0:T(8,128)(2,1)S(1)} %add_convert_fusion), channel_id=1, source_target_pairs={{0,16},{1,17},{2,18},{3,19},{4,20},{5,21},{6,22},{7,23},{8,24},{9,... | collective-permute-start | bytes 221192 | tf_op jit(solution)/shard_map/ppermute | solution.py:618
  70.1 2.7 %collective-permute-done.5 = bf16[48,768]{1,0:T(8,128)(2,1)S(1)} collective-permute-done((bf16[48,768]{1,0:T(8,128)(2,1)S(1)}, bf16[48,768]{1,0:T(8,128)(2,1)S(1)}, u32[]{:S(2)}, u32[]{:S(2)}) %collective-permute-start.5) | collective-permute-done | bytes 73760 | tf_op jit(solution)/shard_map/ppermute | solution.py:618
  72.8 1.7 %collective-permute-start.6 = (bf16[96,768]{1,0:T(8,128)(2,1)S(1)}, bf16[96,768]{1,0:T(8,128)(2,1)S(1)}, u32[]{:S(2)}, u32[]{:S(2)}) collective-permute-start(bf16[96,768]{1,0:T(8,128)(2,1)S(1)} %pad_maximum_fusion.3), channel_id=1, source_target_pairs={{0,1},{1,0},{2,10},{3,11},{4,5},{5,4},{6,14},{7,15},{8,9},{9,8},{1... | collective-permute-start | bytes 442376 | tf_op jit(solution)/shard_map/ppermute | solution.py:618
  74.5 3.5 %collective-permute-done.6 = bf16[96,768]{1,0:T(8,128)(2,1)S(1)} collective-permute-done((bf16[96,768]{1,0:T(8,128)(2,1)S(1)}, bf16[96,768]{1,0:T(8,128)(2,1)S(1)}, u32[]{:S(2)}, u32[]{:S(2)}) %collective-permute-start.6) | collective-permute-done | bytes 147488 | tf_op jit(solution)/shard_map/ppermute | solution.py:618
  78.1 3.5 %collective-permute-start.7 = (bf16[192,768]{1,0:T(8,128)(2,1)S(1)}, bf16[192,768]{1,0:T(8,128)(2,1)S(1)}, u32[]{:S(2)}, u32[]{:S(2)}) collective-permute-start(bf16[192,768]{1,0:T(8,128)(2,1)S(1)} %pad_maximum_fusion.2), channel_id=1, source_target_pairs={{0,8},{1,9},{2,6},{3,7},{4,12},{5,13},{6,2},{7,3},{8,0},{9,1},{10,... | collective-permute-start | bytes 884744 | tf_op jit(solution)/shard_map/ppermute | solution.py:618
  81.6 4.7 %collective-permute-done.7 = bf16[192,768]{1,0:T(8,128)(2,1)S(1)} collective-permute-done((bf16[192,768]{1,0:T(8,128)(2,1)S(1)}, bf16[192,768]{1,0:T(8,128)(2,1)S(1)}, u32[]{:S(2)}, u32[]{:S(2)}) %collective-permute-start.7) | collective-permute-done | bytes 294944 | tf_op jit(solution)/shard_map/ppermute | solution.py:618
  86.5 1.7 %collective-permute-start.8 = (bf16[384,768]{1,0:T(8,128)(2,1)S(1)}, bf16[384,768]{1,0:T(8,128)(2,1)S(1)}, u32[]{:S(2)}, u32[]{:S(2)}) collective-permute-start(bf16[384,768]{1,0:T(8,128)(2,1)S(1)} %pad_maximum_fusion.1), channel_id=1, source_target_pairs={{0,4},{1,5},{2,3},{3,2},{4,0},{5,1},{6,7},{7,6},{8,12},{9,13},{10,... | collective-permute-start | bytes 1769480 | tf_op jit(solution)/shard_map/ppermute | solution.py:618
  88.1 8.3 %collective-permute-done.8 = bf16[384,768]{1,0:T(8,128)(2,1)S(1)} collective-permute-done((bf16[384,768]{1,0:T(8,128)(2,1)S(1)}, bf16[384,768]{1,0:T(8,128)(2,1)S(1)}, u32[]{:S(2)}, u32[]{:S(2)}) %collective-permute-start.8) | collective-permute-done | bytes 589856 | tf_op jit(solution)/shard_map/ppermute | solution.py:618
  97.4 1.5 %collective-permute-start.10 = (bf16[128,128]{1,0:T(8,128)(2,1)S(1)}, bf16[128,128]{1,0:T(8,128)(2,1)S(1)}, u32[]{:S(2)}, u32[]{:S(2)}) collective-permute-start(bf16[128,128]{1,0:T(8,128)(2,1)S(1)} %copy-done.5), channel_id=1, source_target_pairs={{0,1},{1,0},{2,3},{3,2},{4,5},{5,4},{6,7},{7,6},{8,9},{9,8},{10,11... | collective-permute-start | bytes 98312 | tf_op jit(solution)/shard_map/ppermute | solution.py:618
  99.6 1.7 %collective-permute-done.10.recv_ref = bf16[128,128]{1,0:T(8,128)(2,1)S(1)} collective-permute-done((bf16[128,128]{1,0:T(8,128)(2,1)S(1)}, bf16[128,128]{1,0:T(8,128)(2,1)S(1)}, u32[]{:S(2)}, u32[]{:S(2)}) %collective-permute-start.10) | collective-permute-done | bytes 32800 | tf_op jit(solution)/shard_map/ppermute | solution.py:618
  102.3 6.6 %final.1 = (f32[64,18304]{1,0:T(8,128)}, f32[64,18304]{1,0:T(8,128)}, f32[1,64]{1,0:T(1,128)}, f32[1,64]{1,0:T(1,128)}, f32[1,64]{1,0:T(1,128)}, /*index=5*/f32[...) custom-call(s32[2]{0:T(128)} %pad_add_fusion.where_ref, f32[1,5]{1,0:T(1,128)} %amp_ref.5, bf16[768,768]{1,0:T(8,128)(2,1)} %copy-done, ...), custom_call_target="tpu_custom_call" | custom-call | tf_op jit(solution)/shard_map/final/pallas_call | solution.py:729
  (37 shorter events, 8.1 us)
Async XLA Ops:
  21.9 5.7 %collective-permute-start = (bf16[336,128]{1,0:T(8,128)(2,1)}, bf16[336,128]{1,0:T(8,128)(2,1)S(1)}, u32[]{:S(2)}, u32[]{:S(2)}) collective-permute-start(bf16[336,128]{1,0:T(8,128)(2,1)} %get-tuple-element.31), channel_id=1, source_target_pairs={{0,1},{1,0},{2,3},{3,2},{4,5},{5,4},{6,7},{7,6},{8,9},{9,8},{10,11... | collective-permute-start | bytes 258056 | tf_op jit(solution)/shard_map/ppermute | solution.py:618
  27.6 0.6 copy-start.2
  46.0 2.3 %collective-permute-start.1 = (bf16[384,768]{1,0:T(8,128)(2,1)}, bf16[384,768]{1,0:T(8,128)(2,1)S(1)}, u32[]{:S(2)}, u32[]{:S(2)}) collective-permute-start(bf16[384,768]{1,0:T(8,128)(2,1)} %get-tuple-element.41), channel_id=1, source_target_pairs={{0,2},{1,3},{2,0},{3,1},{4,6},{5,7},{6,4},{7,5},{8,10},{9,11},{10,... | collective-permute-start | bytes 1769480 | tf_op jit(solution)/shard_map/ppermute | solution.py:618
  49.5 6.8 %collective-permute-start.2 = (bf16[192,768]{1,0:T(8,128)(2,1)S(1)}, bf16[192,768]{1,0:T(8,128)(2,1)S(1)}, u32[]{:S(2)}, u32[]{:S(2)}) collective-permute-start(bf16[192,768]{1,0:T(8,128)(2,1)S(1)} %dynamic-slice_convert_fusion), channel_id=1, source_target_pairs={{0,4},{1,5},{2,10},{3,11},{4,0},{5,1},{6,14},{7,15},{8,12},{9,13},... | collective-permute-start | bytes 884744 | tf_op jit(solution)/shard_map/ppermute | solution.py:618
  56.4 5.2 %collective-permute-start.3 = (bf16[96,768]{1,0:T(8,128)(2,1)S(1)}, bf16[96,768]{1,0:T(8,128)(2,1)S(1)}, u32[]{:S(2)}, u32[]{:S(2)}) collective-permute-start(bf16[96,768]{1,0:T(8,128)(2,1)S(1)} %dynamic-slice_convert_fusion.1), channel_id=1, source_target_pairs={{0,8},{1,9},{2,6},{3,7},{4,12},{5,13},{6,2},{7,3},{8,0},{9,1},{10,... | collective-permute-start | bytes 442376 | tf_op jit(solution)/shard_map/ppermute | solution.py:618
  61.7 5.4 %collective-permute-start.4 = (bf16[48,768]{1,0:T(8,128)(2,1)S(1)}, bf16[48,768]{1,0:T(8,128)(2,1)S(1)}, u32[]{:S(2)}, u32[]{:S(2)}) collective-permute-start(bf16[48,768]{1,0:T(8,128)(2,1)S(1)} %dynamic-slice_convert_fusion.2), channel_id=1, source_target_pairs={{0,16},{1,17},{2,18},{3,19},{4,20},{5,21},{6,22},{7,23},{8,24},{9,... | collective-permute-start | bytes 221192 | tf_op jit(solution)/shard_map/ppermute | solution.py:618
  67.1 5.7 %collective-permute-start.5 = (bf16[48,768]{1,0:T(8,128)(2,1)S(1)}, bf16[48,768]{1,0:T(8,128)(2,1)S(1)}, u32[]{:S(2)}, u32[]{:S(2)}) collective-permute-start(bf16[48,768]{1,0:T(8,128)(2,1)S(1)} %add_convert_fusion), channel_id=1, source_target_pairs={{0,16},{1,17},{2,18},{3,19},{4,20},{5,21},{6,22},{7,23},{8,24},{9,... | collective-permute-start | bytes 221192 | tf_op jit(solution)/shard_map/ppermute | solution.py:618
  72.8 5.2 %collective-permute-start.6 = (bf16[96,768]{1,0:T(8,128)(2,1)S(1)}, bf16[96,768]{1,0:T(8,128)(2,1)S(1)}, u32[]{:S(2)}, u32[]{:S(2)}) collective-permute-start(bf16[96,768]{1,0:T(8,128)(2,1)S(1)} %pad_maximum_fusion.3), channel_id=1, source_target_pairs={{0,1},{1,0},{2,10},{3,11},{4,5},{5,4},{6,14},{7,15},{8,9},{9,8},{1... | collective-permute-start | bytes 442376 | tf_op jit(solution)/shard_map/ppermute | solution.py:618
  78.1 8.2 %collective-permute-start.7 = (bf16[192,768]{1,0:T(8,128)(2,1)S(1)}, bf16[192,768]{1,0:T(8,128)(2,1)S(1)}, u32[]{:S(2)}, u32[]{:S(2)}) collective-permute-start(bf16[192,768]{1,0:T(8,128)(2,1)S(1)} %pad_maximum_fusion.2), channel_id=1, source_target_pairs={{0,8},{1,9},{2,6},{3,7},{4,12},{5,13},{6,2},{7,3},{8,0},{9,1},{10,... | collective-permute-start | bytes 884744 | tf_op jit(solution)/shard_map/ppermute | solution.py:618
  86.5 9.9 %collective-permute-start.8 = (bf16[384,768]{1,0:T(8,128)(2,1)S(1)}, bf16[384,768]{1,0:T(8,128)(2,1)S(1)}, u32[]{:S(2)}, u32[]{:S(2)}) collective-permute-start(bf16[384,768]{1,0:T(8,128)(2,1)S(1)} %pad_maximum_fusion.1), channel_id=1, source_target_pairs={{0,4},{1,5},{2,3},{3,2},{4,0},{5,1},{6,7},{7,6},{8,12},{9,13},{10,... | collective-permute-start | bytes 1769480 | tf_op jit(solution)/shard_map/ppermute | solution.py:618
  96.6 0.8 copy-start.5
  96.6 2.3 %copy-start.4 = (bf16[112,128]{1,0:T(8,128)(2,1)S(1)}, bf16[112,128]{1,0:T(8,128)(2,1)}, u32[]{:S(2)}) copy-start(bf16[112,128]{1,0:T(8,128)(2,1)} %get-tuple-element.39) | copy-start | bytes 86020
  96.7 4.6 %copy-start = (bf16[768,768]{1,0:T(8,128)(2,1)}, bf16[768,768]{1,0:T(8,128)(2,1)S(1)}, u32[]{:S(2)}) copy-start(bf16[768,768]{1,0:T(8,128)(2,1)S(1)} %pad_maximum_fusion.mine_ref) | copy-start | bytes 3538948
  96.8 4.6 %collective-permute-start.9 = (bf16[768,768]{1,0:T(8,128)(2,1)S(1)}, bf16[768,768]{1,0:T(8,128)(2,1)S(1)}, u32[]{:S(2)}, u32[]{:S(2)}) collective-permute-start(bf16[768,768]{1,0:T(8,128)(2,1)S(1)} %pad_maximum_fusion.mine_ref), channel_id=1, source_target_pairs={{0,2},{1,3},{2,0},{3,1},{4,6},{5,7},{6,4},{7,5},{8,10},{9,11},{10,... | collective-permute-start | bytes 3538952 | tf_op jit(solution)/shard_map/ppermute | solution.py:618
  97.4 3.9 %collective-permute-start.10 = (bf16[128,128]{1,0:T(8,128)(2,1)S(1)}, bf16[128,128]{1,0:T(8,128)(2,1)S(1)}, u32[]{:S(2)}, u32[]{:S(2)}) collective-permute-start(bf16[128,128]{1,0:T(8,128)(2,1)S(1)} %copy-done.5), channel_id=1, source_target_pairs={{0,1},{1,0},{2,3},{3,2},{4,5},{5,4},{6,7},{7,6},{8,9},{9,8},{10,11... | collective-permute-start | bytes 98312 | tf_op jit(solution)/shard_map/ppermute | solution.py:618
  101.3 0.6 copy-start.3
  101.3 1.0 copy-start.1

commit v2 on v0

v2 whole, which is shorter than its diff:
```python
import functools
import math

import jax
import jax.numpy as jnp
from jax import lax
from jax.experimental import pallas as pl
from jax.experimental.pallas import tpu as pltpu
from jax.sharding import PartitionSpec as P

D = 64
FF = 64
K = 5
TAPS = 286
STEPS = 432
PMAX = 48
GRID = 480
HALF = STEPS // 2
LANES = 128
kernel_sizes = (1, 3, 5, 7, 9, 11)
epsilon = 1e-05
f32 = jnp.float32
bf16 = jnp.bfloat16

PAIR = 448
FOLD = PAIR // 2
QUART = GRID // 4
NEAR = 5 * PMAX
WIDE = 12 * 32
FULL = 12 * D
HALF_IN = 1024
STEP = 48


def tap_index(size, row, col):
    radius = (size - 1) // 2
    first = sum(k * k for k in kernel_sizes if k < size)
    return first + (row + radius) * size + col + radius


def tap_place(tap):
    for size in kernel_sizes:
        inside = tap - tap_index(size, -(size // 2), -(size // 2))
        if 0 <= inside < size * size:
            return inside // size - size // 2 + 5, inside % size - size // 2 + 5
    return None


def lane_of(rows):
    return lax.broadcasted_iota(jnp.int32, (rows, LANES), 1)


def row_of(rows):
    return lax.broadcasted_iota(jnp.int32, (rows, LANES), 0)


def low_half(rows):
    return lane_of(rows) < D


def span(plane):
    return slice(plane * LANES, (plane + 1) * LANES)


def four_quarters(v):
    v = v + pltpu.roll(v, 64, 1)
    return v + pltpu.roll(v, 32, 1)


def quarter_select(parts, rows):
    lane = lane_of(rows)
    upper = jnp.where(lane < 96, parts[2], parts[3])
    lower = jnp.where(lane < 32, parts[0], parts[1])
    return jnp.where(lane < 64, lower, upper)


def pack_pieces(load, store, temp):
    rows = 24
    pieces = []
    for r in range(0, 2 * QUART, rows):

        def piece(r=r):
            low = low_half(rows)
            a, b = load(r, rows), load(2 * QUART + r, rows)
            temp[r : r + rows, :] = jnp.where(low, a, b) + pltpu.roll(jnp.where(low, b, a), 64, 1)

        pieces.append(piece)
    for r in range(0, QUART, rows):

        def piece(r=r):
            even = lane_of(rows) // 32 % 2 == 0
            a, b = temp[r : r + rows, :], temp[QUART + r : QUART + r + rows, :]
            other = jnp.where(even, pltpu.roll(a, 96, 1), pltpu.roll(b, 32, 1))
            store(r, rows, jnp.where(even, a, b) + other)

        pieces.append(piece)
    return pieces


def spread_pieces(read, target, start):
    rows = 40
    pieces = []
    for r in range(0, QUART, rows):

        def piece(r=r):
            packed = read(r, rows)
            turned = [packed if s == 0 else pltpu.roll(packed, 32 * s, 1) for s in range(4)]
            for q in range(4):
                lanes = slice(32 * q, 32 * q + 32)
                for block in range(4):
                    target[pl.ds(start(q) + block * QUART + r, rows), lanes] = turned[
                        (q - block) % 4
                    ][:, lanes]

        pieces.append(piece)
    return pieces


def rounded(v):
    return v.astype(bf16).astype(f32)


def spread_pairs(pairs, ref, start):
    rows = pairs.shape[0]
    other = pltpu.roll(pairs, D, 1)
    low = low_half(rows)
    ref[pl.ds(start, rows, stride=2), :] = jnp.where(low, pairs, other)
    ref[pl.ds(start + 1, rows, stride=2), :] = jnp.where(low, other, pairs)


def flat_pairs(ref, rows):
    return ref[...].astype(f32).reshape(rows, LANES)


def gather_pairs(ref, start, rows):
    return jnp.where(
        low_half(rows),
        ref[pl.ds(start, rows, stride=2), :],
        ref[pl.ds(start + 1, rows, stride=2), :],
    )


def combine_tile(load, rows, row, plane):
    low = low_half(rows)
    col0, col1 = 2 * plane - 5, 2 * plane - 4
    even = odd = None
    for size in kernel_sizes:
        radius = (size - 1) // 2
        in0, in1 = abs(col0) <= radius, abs(col1) <= radius
        if abs(row) > radius or not (in0 or in1):
            continue
        first = tap_index(size, row, col0)
        if first % 2 == 0:
            v = load(first // 2)
            if not in0:
                v = jnp.where(low, 0.0, v)
            if not in1:
                v = jnp.where(low, v, 0.0)
            even = v if even is None else even + v
        else:
            left = load(first // 2) if in0 else 0.0
            right = load(first // 2 + 1) if in1 else 0.0
            v = jnp.where(low, right, left)
            odd = v if odd is None else odd + v
    if odd is not None:
        odd = pltpu.roll(odd, D, 1)
        even = odd if even is None else even + odd
    return even


def widths(period):
    width = jnp.full((8, LANES), period, jnp.int32).astype(f32)
    return width, 1.0 / width


def column_of(width, inverse, rows, ahead, start):
    position = (row_of(rows) + ahead + start).astype(f32)
    many = jnp.broadcast_to(width[0:1, :], (rows, LANES))
    turns = jnp.floor((position + 0.5) * jnp.broadcast_to(inverse[0:1, :], (rows, LANES)))
    return position - turns * many


def mixing_of(amp):
    shifted = jnp.exp(amp - jnp.max(amp, axis=-1, keepdims=True))
    return shifted / jnp.sum(shifted, axis=-1, keepdims=True)


def gelu_both(v):
    cdf = 0.5 * (1.0 + lax.erf(v * (1.0 / math.sqrt(2.0))))
    density = jnp.exp(-0.5 * v * v) * (1.0 / math.sqrt(2.0 * math.pi))
    return v * cdf, cdf + v * density


def contract(a, b, dim_a, dim_b):
    return lax.dot_general(
        a, b, (((dim_a,), (dim_b,)), ((), ())), preferred_element_type=f32
    )


def together(*streams):
    lists = [list(stream) for stream in streams]
    marks = []
    for number, pieces in enumerate(lists):
        for index, piece in enumerate(pieces):
            marks.append(((index + 0.5) / len(pieces), number, piece))
    for _, _, piece in sorted(marks, key=lambda mark: mark[:2]):
        piece()


def unfold_columns(period, shifted, target):
    pieces = []
    for t in range(0, GRID, STEP):

        def piece(t=t):
            width, inverse = widths(period)
            many = jnp.broadcast_to(width[0:1, :], (STEP, LANES)).astype(bf16)
            zero = jnp.zeros((STEP, LANES), bf16)
            col = column_of(width, inverse, STEP, 0, t)
            col = (col + jnp.where(low_half(STEP), 0.0, 1.0)).astype(bf16)
            for plane in range(6):
                shift = 2 * plane - 5
                inside = (col >= jnp.asarray(-shift, bf16)) & (col < many - jnp.asarray(shift, bf16))
                target[t : t + STEP, span(plane)] = jnp.where(
                    inside, shifted[plane, t : t + STEP, :], zero
                )

        pieces.append(piece)
    return pieces


def shift_columns(xs, shifted):
    for t in range(0, GRID, STEP):
        low = low_half(STEP)
        for plane in range(6):
            at = 16 + t + 2 * plane - 5
            shifted[plane, t : t + STEP, :] = jnp.where(
                low, xs[pl.ds(at, STEP), :], xs[pl.ds(at + 1, STEP), :]
            ).astype(bf16)


def product_pieces(read, read_weight, target, start, planes, dims):
    pieces = []
    for plane in range(0, planes, 2):

        def piece(plane=plane):
            count = min(2, planes - plane)
            lanes = slice(plane * LANES, (plane + count) * LANES)
            product = contract(read(), read_weight(lanes), *dims)
            for index in range(count):
                target[plane + index, start : start + GRID, :] = product[:, span(index)]

        pieces.append(piece)
    return pieces


def weight_pieces(read, read_other, total, first):
    def piece():
        value = contract(read(), read_other(), 0, 0)
        if first:
            total[...] = value
        else:
            total[...] += value

    return [piece]


def forward_kernel(
    where_ref,
    periods_hbm,
    amp_hbm,
    x_hbm,
    cot_hbm,
    conv_in_hbm,
    conv_out_hbm,
    bias_in_hbm,
    bias_out_hbm,
    send_ref,
    total,
    part_ref,
    w1_hbm,
    w2_hbm,
    xs,
    ua_ref,
    slope_ref,
    w1_wide,
    w2_wide,
    r2,
    ux_ref,
    periods_ref,
    amp_ref,
    x_ref,
    cot_ref,
    conv_in_ref,
    conv_out_ref,
    bias_in_ref,
    bias_out_ref,
    xb,
    c2,
    act0,
    act1,
    ys0,
    ys1,
    ys2,
    zs0,
    zs1,
    ss0,
    ss1,
    st0,
    st1,
    tp0,
    tp1,
    sems,
    sent,
):
    side = where_ref[0]
    half = pl.multiple_of(side * 32, 32)
    sources = [
        (x_hbm, x_ref),
        (periods_hbm, periods_ref),
        (amp_hbm, amp_ref),
        (bias_in_hbm, bias_in_ref),
        (bias_out_hbm, bias_out_ref),
        (cot_hbm, cot_ref),
    ]
    for piece in range(2):
        rows = pl.ds(pl.multiple_of(half + 16 * piece, 16), 16)
        sources.append((conv_in_hbm.at[rows, :], conv_in_ref.at[pl.ds(16 * piece, 16), :]))
    for piece in range(4):
        rows = pl.ds(16 * piece, 16)
        sources.append((conv_out_hbm.at[rows, :], conv_out_ref.at[rows, :]))
    copies = [pltpu.make_async_copy(a, b, sems.at[i]) for i, (a, b) in enumerate(sources)]
    for copy in copies:
        copy.start()
    xs[...] = jnp.zeros_like(xs)
    for ref in (act0, act1):
        ref[...] = jnp.zeros_like(ref)
    for ref in (ys0, ys1, ys2, zs0, zs1):
        ref[:, 0:NEAR, :] = jnp.zeros((ref.shape[0], NEAR, LANES), f32)
        ref[:, NEAR + GRID :, :] = jnp.zeros((ref.shape[0], ref.shape[1] - NEAR - GRID, LANES), f32)
    source = lax.broadcasted_iota(jnp.int32, (2 * LANES, LANES), 0)
    target = lax.broadcasted_iota(jnp.int32, (2 * LANES, LANES), 1)
    wanted = (target // 32) * 64 + side * 32 + target % 32
    choose = (source == wanted).astype(f32).astype(bf16)
    w1_wide[352:384, :] = jnp.zeros((32, FULL), bf16)
    c2[704:768, :] = jnp.zeros((64, FULL), bf16)
    r2[704:768, :] = jnp.zeros((64, 2 * LANES), bf16)

    copies[0].wait()
    spread_pairs(flat_pairs(x_ref, HALF), xs, 16)
    shift_columns(xs, xb)
    for copy in copies[1:6]:
        copy.wait()
    bias_in = jnp.concatenate([bias_in_ref[...], bias_in_ref[...]], axis=1)
    bias_in = jnp.where(side == 0, bias_in, pltpu.roll(bias_in, 96, 1))
    bias_in = four_quarters(jnp.where(lane_of(1) < 32, bias_in, 0.0))
    bias_out = jnp.concatenate([bias_out_ref[...], bias_out_ref[...]], axis=1)
    bias_out = jnp.where(side == 0, bias_out, 0.0)
    mixing = mixing_of(amp_ref[...])
    leaving = []

    def leave(ref, target):
        copy = pltpu.make_async_copy(ref, target, sent.at[len(leaving)])
        copy.start()
        leaving.append(copy)

    def unfold(k):
        return unfold_columns(periods_ref[0, k], xb, ux_ref.at[k])

    def first_product(k):
        target = (ys0, ys1, ys2)[k % 3]

        def piece():
            product = contract(ux_ref[k], w1_wide[...], 1, 1)
            for plane in range(3):
                value = product[:, span(plane)]
                if plane == 1:
                    value = value + product[:, span(3)]
                target[plane, NEAR : NEAR + GRID, :] = value

        return [piece]

    def second_product(k):
        target = (zs0, zs1)[k % 2]
        pieces = []
        for plane in range(0, 6, 2):

            def piece(plane=plane):
                lanes = slice(plane * LANES, (plane + 2) * LANES)
                value = ua_ref[k]
                value = jnp.concatenate([value, value[:, span(1)]], axis=1)
                product = contract(value, w2_wide[lanes, :], 1, 1)
                for index in range(2):
                    target[plane + index, NEAR : NEAR + GRID, :] = product[:, span(index)]

            pieces.append(piece)
        return pieces

    def activate(k):
        ys, ss, act, temp = (ys0, ys1, ys2)[k % 3], (ss0, ss1)[k % 2], (act0, act1)[k % 2], (tp0, tp1)[k % 2]
        period = periods_ref[0, k]
        used = lax.div(STEPS + period - 1, period) * period
        pieces = []
        for t in range(0, GRID + 3 * PMAX, STEP):

            def piece(t=t):
                value = ys[0, pl.ds(NEAR + t - 5 * period, STEP), :]
                for plane in range(1, 3):
                    value = value + ys[plane, pl.ds(NEAR + t + (4 * plane - 5) * period, STEP), :]
                ss[t : t + STEP, :] = value

            pieces.append(piece)

        def load(r, rows):
            return quarter_select([ss[pl.ds(r + q * period, rows), :] for q in range(4)], rows)

        def store(r, rows, value):
            hidden = value * (1.0 / 6.0) + bias_in
            active, slope = gelu_both(hidden)
            position = row_of(rows) + r + QUART * (lane_of(rows) // 32)
            slope_ref[k, r : r + rows, :] = jnp.where(position < used, slope, 0.0)
            temp[r : r + rows, :] = jnp.where(position < used, active, 0.0)

        pieces += pack_pieces(load, store, temp)
        pieces += spread_pieces(lambda r, rows: temp[r : r + rows, :], act, lambda q: 16 - q)
        for t in range(0, GRID, STEP):

            def piece(t=t):
                width, inverse = widths(period)
                many = jnp.broadcast_to(width[0:1, :], (STEP, LANES)).astype(bf16)
                zero = jnp.zeros((STEP, LANES), bf16)
                col = column_of(width, inverse, STEP, 0, t) + (lane_of(STEP) // 32).astype(f32)
                col = col.astype(bf16)
                for plane in range(3):
                    shift = 4 * plane - 5
                    inside = (col >= jnp.asarray(-shift, bf16)) & (
                        col < many - jnp.asarray(shift, bf16)
                    )
                    moved = act[pl.ds(16 + t + shift, STEP), :].astype(bf16)
                    ua_ref[k, t : t + STEP, span(plane)] = jnp.where(inside, moved, zero)

            pieces.append(piece)
        return pieces

    def finish(k):
        zs, ss = (zs0, zs1)[k % 2], (st0, st1)[k % 2]
        period = periods_ref[0, k]
        weight = mixing[:, k : k + 1]
        pieces = []
        for t in range(0, GRID + PMAX, STEP):

            def piece(t=t):
                value = zs[0, pl.ds(NEAR + t - 5 * period, STEP), :]
                for plane in range(1, 6):
                    value = value + zs[plane, pl.ds(NEAR + t + (2 * plane - 5) * period, STEP), :]
                ss[t : t + STEP, :] = value

            pieces.append(piece)
        rows = 32
        for r in range(0, FOLD, rows):

            def piece(r=r):
                low = low_half(rows)
                near = jnp.where(low, ss[pl.ds(r, rows), :], ss[pl.ds(FOLD + r + period, rows), :])
                far = jnp.where(low, ss[pl.ds(FOLD + r, rows), :], ss[pl.ds(r + period, rows), :])
                out = (near + pltpu.roll(far, D, 1)) * (1.0 / 6.0) + bias_out
                part_ref[k, r : r + rows, :] = out
                if k == 0:
                    total[r : r + rows, :] = weight * out
                else:
                    total[r : r + rows, :] += weight * out

            pieces.append(piece)
        return pieces

    def combine_in():
        pieces = []
        for row in range(-5, 6):

            def piece(row=row):
                at = (row + 5) * 32
                for plane in range(6):
                    v = combine_tile(lambda tile: conv_in_ref[:, span(tile)].astype(f32), 32, row, plane)
                    w1_wide[at : at + 32, span(plane)] = v.astype(bf16)
                    if -1 <= row <= 2:
                        w1_wide[WIDE + at - 128 : WIDE + at - 96, span(plane)] = (v - rounded(v)).astype(bf16)

            pieces.append(piece)
        return pieces

    def combine_out():
        pieces = []
        for row in range(-5, 6):

            def piece(row=row):
                at = (row + 5) * 64
                for plane in range(6):
                    v = combine_tile(lambda tile: conv_out_ref[:, span(tile)].astype(f32), 64, row, plane)
                    c2[at : at + 64, span(plane)] = v.astype(bf16)
                    if plane // 2 == 1:
                        r2[at : at + 64, span(plane % 2)] = (v - rounded(v)).astype(bf16)

            pieces.append(piece)
        return pieces

    def choose_half():
        pieces = []
        for plane in range(3):

            def piece(plane=plane):
                lanes = slice(2 * plane * LANES, 2 * (plane + 1) * LANES)
                w2_wide[:, span(plane)] = jnp.dot(
                    c2[:, lanes], choose, preferred_element_type=f32
                ).astype(bf16)

            pieces.append(piece)

        def piece():
            w2_wide[:, span(3)] = jnp.dot(r2[...], choose, preferred_element_type=f32).astype(bf16)

        return pieces + [piece]

    together(unfold(0))
    together(unfold(1))
    for copy in copies[6:]:
        copy.wait()
    together(combine_in())
    leave(w1_wide.at[pl.ds(0, WIDE), :], w1_hbm)
    combining = combine_out()
    together(first_product(0), combining[:6])
    together(first_product(1), combining[6:], unfold(2))
    together(choose_half(), activate(0))
    leave(w2_wide.at[:, pl.ds(0, WIDE)], w2_hbm)
    together(first_product(2), activate(1), unfold(3))
    together(second_product(0), activate(2))
    together(first_product(3), finish(0), unfold(4))
    together(second_product(1), activate(3))
    together(first_product(4), finish(1))
    together(second_product(2), activate(4))
    together(second_product(3), finish(2))
    together(second_product(4), finish(3))
    together(finish(4))

    send_ref[0:FOLD, :] = total[...].astype(bf16)
    send_ref[FOLD:, :] = jnp.concatenate(
        [flat_pairs(cot_ref, HALF // 2), jnp.zeros((4, LANES), f32)], axis=0
    ).astype(bf16)
    for copy in leaving:
        copy.wait()


def outer_kernel(
    where_ref,
    periods_ref,
    amp_ref,
    cot_ref,
    recv_ref,
    own_ref,
    xs,
    part_ref,
    w1_hbm,
    w2_hbm,
    ua_ref,
    slope_ref,
    gain_ref,
    shift_ref,
    out_hbm,
    keep_ref,
    send_ref,
    grad_ref,
    merged_ref,
    dots_ref,
    small,
    w1_ref,
    other,
    cot,
    outs,
    gm,
    gmp,
    rw0,
    rw1,
    gb0,
    gb1,
    zs0,
    zs1,
    vs0,
    vs1,
    tp0,
    tp1,
    dw,
    packed,
    w2_ref,
    out_ref,
    sems,
    out_sem,
):
    coming = [
        pltpu.make_async_copy(w2_hbm, w2_ref, sems.at[0]),
        pltpu.make_async_copy(w1_hbm, w1_ref, sems.at[1]),
    ]
    for copy in coming:
        copy.start()
    side = where_ref[0]
    core = where_ref[1]
    mixing = mixing_of(amp_ref[...])
    small[...] = jnp.zeros_like(small)
    for ref in (rw0, rw1):
        ref[0:NEAR, :] = jnp.zeros((NEAR, LANES), f32)
        ref[NEAR + GRID :, :] = jnp.zeros((NEAR, LANES), f32)
    for ref in (zs0, zs1):
        ref[:, 0:16, :] = jnp.zeros((3, 16, LANES), f32)
        ref[:, 16 + GRID :, :] = jnp.zeros((3, 16, LANES), f32)
    gm[0:PMAX, :] = jnp.zeros((PMAX, LANES), f32)
    gm[PMAX + PAIR :, :] = jnp.zeros((GRID - PAIR, LANES), f32)

    low = low_half(FOLD)
    v = own_ref[...] + recv_ref[0:FOLD, :].astype(f32)
    turned = pltpu.roll(v, D, 1)
    other[0:FOLD, :] = jnp.where(low, v, turned)
    other[FOLD:, :] = jnp.where(low, turned, v)
    mine = flat_pairs(cot_ref, HALF // 2)
    theirs = recv_ref[FOLD:, :].astype(f32)[: HALF // 2, :]
    cot[STEPS:, :] = jnp.zeros((PAIR - STEPS, LANES), f32)
    spread_pairs(jnp.where(side == 0, mine, theirs), cot, 0)
    spread_pairs(jnp.where(side == 0, theirs, mine), cot, HALF)
    gain = jnp.concatenate([gain_ref[...], gain_ref[...]], axis=1)
    shift = jnp.concatenate([shift_ref[...], shift_ref[...]], axis=1)
    grad_gain = grad_shift = grad_bias = jnp.zeros((8, LANES), f32)

    def eights(v):
        return jnp.sum(v.reshape(-1, 8, LANES), axis=0)

    for t in range(0, PAIR, 56):
        rows = slice(t, t + 56)
        total = xs[16 + t : 16 + t + 56, :] + other[rows, :]
        centred = total - jnp.mean(total, axis=-1, keepdims=True)
        variance = jnp.mean(centred * centred, axis=-1, keepdims=True)
        inverse = lax.rsqrt(variance + epsilon)
        normed = centred * inverse
        outs[rows, :] = normed * gain + shift
        c = cot[rows, :]
        grad_gain = grad_gain + eights(c * normed)
        grad_shift = grad_shift + eights(c)
        e = c * gain
        grad = inverse * (
            e
            - jnp.mean(e, axis=-1, keepdims=True)
            - normed * jnp.mean(e * normed, axis=-1, keepdims=True)
        )
        gm[PMAX + t : PMAX + t + 56, :] = grad
        merged_ref[rows, :] = grad
        grad_bias = grad_bias + eights(grad)
    grad_bias = grad_bias * jnp.sum(mixing, axis=-1, keepdims=True)
    small[1:2, :] = jnp.sum(grad_bias, axis=0, keepdims=True)
    small[2:3, :] = jnp.sum(grad_gain, axis=0, keepdims=True)
    small[3:4, :] = jnp.sum(grad_shift, axis=0, keepdims=True)
    first = pl.multiple_of(side * HALF, 8)
    out_ref[...] = gather_pairs(outs, first, HALF // 2).reshape(1, HALF * D).astype(bf16)
    leaving = pltpu.make_async_copy(out_ref, out_hbm, out_sem)
    leaving.start()
    rows = 32
    for r in range(0, FOLD, rows):
        gmp[r : r + rows, :] = jnp.where(
            low_half(rows),
            gm[PMAX + r : PMAX + r + rows, :],
            gm[PMAX + FOLD + r : PMAX + FOLD + r + rows, :],
        )

    def unfold(k):
        rowed, gab = (rw0, rw1)[k % 2], (gb0, gb1)[k % 2]
        period = periods_ref[0, k]
        weight = mixing[:, k : k + 1]
        pieces = []
        for t in range(0, GRID, STEP):

            def piece(t=t):
                here = gm[PMAX + t : PMAX + t + STEP, :]
                back = gm[pl.ds(PMAX + t - period, STEP), :]
                rowed[NEAR + t : NEAR + t + STEP, :] = weight * jnp.where(low_half(STEP), here, back)

            pieces.append(piece)
        for t in range(0, GRID, STEP):

            def piece(t=t):
                for plane in range(6):
                    gab[t : t + STEP, span(plane)] = rowed[
                        pl.ds(NEAR + t - (2 * plane - 5) * period, STEP), :
                    ].astype(bf16)

            pieces.append(piece)
        return pieces

    def back(k):
        return product_pieces(
            lambda: (gb0, gb1)[k % 2][...], lambda lanes: w2_ref[:, lanes], (zs0, zs1)[k % 2], 16, 3, (1, 0)
        )

    def weigh(k):
        return weight_pieces(lambda: ua_ref[k], lambda: (gb0, gb1)[k % 2][...], dw, k == 0)

    def fold(k):
        zs, vs, temp = (zs0, zs1)[k % 2], (vs0, vs1)[k % 2], (tp0, tp1)[k % 2]
        period = periods_ref[0, k]
        rows = 16
        pieces = []
        for t in range(0, GRID + 16, rows):

            def piece(t=t):
                width, inverse = widths(period)
                many = jnp.broadcast_to(width[0:1, :], (rows, LANES))
                quarter = lane_of(rows) // 32
                place = column_of(width, inverse, rows, quarter, t - 8) - quarter.astype(f32)
                value = None
                for plane in range(3):
                    s = 4 * plane - 5
                    v = zs[plane, pl.ds(16 - 8 + t - s, rows), :]
                    v = jnp.where((place >= s) & (place < many + s), v, 0.0)
                    value = v if value is None else value + v
                vs[t : t + rows, :] = value

            pieces.append(piece)

        def load(r, rows):
            return quarter_select([vs[pl.ds(8 + r - q, rows), :] for q in range(4)], rows)

        def store(r, rows, value):
            grad_ref[k, r : r + rows, :] = value * slope_ref[k, r : r + rows, :] * (1.0 / 6.0)

        return pieces + pack_pieces(load, store, temp)

    together(unfold(0))
    coming[0].wait()
    for k in range(K):
        streams = [back(k)]
        if k + 1 < K:
            streams.append(unfold(k + 1))
        together(*streams)
        together(weigh(k), fold(k))
    coming[1].wait()
    leaving.wait()
    bias = None
    for k in range(K):
        v = jnp.sum(grad_ref[k], axis=0, keepdims=True)
        bias = v if bias is None else bias + v
        dots_ref[k : k + 1, :] = jnp.sum(gmp[...] * part_ref[k], axis=0, keepdims=True)
    dots_ref[K:, :] = jnp.zeros((8 - K, LANES), f32)
    small[0:1, :] = four_quarters(bias)
    count = keep_ref.shape[0]
    turned = jnp.transpose((dw[...] * (1.0 / 6.0)).astype(bf16))
    for part in range(2):
        for plane in range(3):
            for row in range(11):
                target = part * count + plane * 352 + row * 32
                source = row * 64 + part * 32
                packed[target : target + 32, :] = turned[source : source + 32, span(plane)]
        packed[part * count + 1056 : (part + 1) * count, :] = jnp.zeros((count - 1056, LANES), bf16)
    keep_ref[...] = packed[pl.ds(pl.multiple_of(core * count, 16), count), :]
    send_ref[...] = packed[pl.ds(pl.multiple_of((1 - core) * count, 16), count), :]


def unfold_rows(period, read, rowed, target, clear):
    edge = 3 * PMAX
    pieces = []
    if clear:

        def piece():
            rowed[edge : 2 * edge, :] = jnp.zeros((edge, LANES), f32)
            rowed[edge + GRID : 2 * edge + GRID, :] = jnp.zeros((edge, LANES), f32)

        pieces.append(piece)
    pieces += spread_pieces(read, rowed, lambda q: edge + q * period)
    for t in range(0, GRID, STEP):

        def piece(t=t):
            for plane in range(3):
                target[t : t + STEP, span(plane)] = rowed[
                    pl.ds(edge + t - (4 * plane - 5) * period, STEP), :
                ].astype(bf16)

        pieces.append(piece)
    return pieces


def copy_scale():
    number = row_of(48) // 4 * 2 + lane_of(48) // D
    return jnp.exp(number.astype(f32) * (math.log(2.0) / 24.0))


def inner_kernel(
    where_ref,
    periods_ref,
    grad_ref,
    small_ref,
    xs,
    keep_ref,
    send_ref,
    hr0,
    hr1,
    xb,
    gh0,
    gh1,
    ux0,
    ux1,
    dw,
    packed,
):
    core = where_ref[1]
    for ref in (hr0, hr1):
        ref[...] = jnp.zeros_like(ref)
    shift_columns(xs, xb)

    def unfold(k):
        return unfold_rows(
            periods_ref[0, k],
            lambda r, rows: grad_ref[k, r : r + rows, :],
            (hr0, hr1)[k % 2],
            (gh0, gh1)[k % 2],
            k > 1,
        )

    def again(k):
        return unfold_columns(periods_ref[0, k], xb, (ux0, ux1)[k % 2])

    def weigh(k):
        return weight_pieces(lambda: (gh0, gh1)[k % 2][...], lambda: (ux0, ux1)[k % 2][...], dw, k == 0)

    together(unfold(0), again(0))
    for k in range(K):
        streams = [weigh(k)]
        if k + 1 < K:
            streams += [unfold(k + 1), again(k + 1)]
        together(*streams)

    sixth = 1.0 / 6.0
    for part in range(2):
        at = part * HALF_IN
        for row in range(11):
            source = slice(row * 32 + part * 16, row * 32 + part * 16 + 16)
            for plane in range(5):
                target = at + plane * 176 + row * 16
                packed[target : target + 16, :] = (dw[source, span(plane)] * sixth).astype(bf16)
        for row in range(6):
            source = slice(row * 32 + part * 16, row * 32 + part * 16 + 16)
            other = slice((row + 6) * 32 + part * 16, (row + 6) * 32 + part * 16 + 16)
            v = jnp.where(low_half(16), dw[source, span(5)], pltpu.roll(dw[other, span(5)], D, 1))
            packed[at + 880 + row * 16 : at + 896 + row * 16, :] = (v * sixth).astype(bf16)
        packed[at + 976 : at + 1024, :] = (
            jnp.concatenate([small_ref[0:4, :]] * 12, axis=0) * copy_scale()
        ).astype(bf16)
    count = HALF_IN
    keep_ref[...] = packed[pl.ds(pl.multiple_of(core * count, count), count), :]
    send_ref[...] = packed[pl.ds(pl.multiple_of((1 - core) * count, count), count), :]


def series_pieces(branches, periods_ref, grad_ref, w1_ref, vs, begun, rowed, hidden, planes):
    for ref in rowed:
        ref[...] = jnp.zeros_like(ref)
    for ref in planes:
        ref[:, 0:16, :] = jnp.zeros((6, 16, LANES), f32)
        ref[:, 16 + GRID :, :] = jnp.zeros((6, 16, LANES), f32)

    def unfold(index):
        k = branches[index]
        return unfold_rows(
            periods_ref[0, k],
            lambda r, rows: grad_ref[k, r : r + rows, :],
            rowed[index % 2],
            hidden[index % 2],
            index > 1,
        )

    def back(index):
        return product_pieces(
            lambda: hidden[index % 2][...],
            lambda lanes: w1_ref[:, lanes],
            planes[index % 2],
            16,
            6,
            (1, 0),
        )

    def fold(index):
        zs = planes[index % 2]
        period = periods_ref[0, branches[index]]
        rows = 16
        pieces = []
        for t in range(0, PAIR + 16, rows):

            def piece(t=t):
                width, inverse = widths(period)
                many = jnp.broadcast_to(width[0:1, :], (rows, LANES))
                half = lane_of(rows) // D
                place = column_of(width, inverse, rows, half, t - 8) - half.astype(f32)
                value = None if begun is None or index else begun[t : t + rows, :]
                for plane in range(6):
                    s = 2 * plane - 5
                    v = zs[plane, pl.ds(16 - 8 + t - s, rows), :]
                    v = jnp.where((place >= s) & (place < many + s), v, 0.0)
                    value = v if value is None else value + v
                if index == 0:
                    vs[t : t + rows, :] = value
                else:
                    vs[t : t + rows, :] += value

            pieces.append(piece)
        return pieces

    count = len(branches)
    together(unfold(0))
    together(back(0), *([unfold(1)] if count > 1 else []))
    for index in range(count):
        streams = [fold(index)]
        if index + 1 < count:
            streams.append(back(index + 1))
        if index + 2 < count:
            streams.append(unfold(index + 2))
        together(*streams)


def series_kernel(periods_ref, grad_ref, w1_ref, vs, hr0, hr1, gh0, gh1, zs0, zs1):
    series_pieces(
        range(0, 3), periods_ref, grad_ref, w1_ref, vs, None, (hr0, hr1), (gh0, gh1), (zs0, zs1)
    )


def series_rest_kernel(
    where_ref,
    periods_ref,
    grad_ref,
    merged_ref,
    dots_ref,
    w1_ref,
    begun_ref,
    own_ref,
    other_ref,
    table_ref,
    hr0,
    hr1,
    gh0,
    gh1,
    zs0,
    zs1,
    vs,
    dx,
    outs,
):
    side = where_ref[0]
    series_pieces(
        range(3, K), periods_ref, grad_ref, w1_ref, vs, begun_ref, (hr0, hr1), (gh0, gh1), (zs0, zs1)
    )
    rows = 56
    for t in range(0, PAIR, rows):
        v = jnp.where(low_half(rows), vs[pl.ds(8 + t, rows), :], vs[pl.ds(8 + t - 1, rows), :])
        v = (v + pltpu.roll(v, D, 1)) * (1.0 / 6.0)
        dx[t : t + rows, :] = v
        outs[t : t + rows, :] = v + merged_ref[t : t + rows, :]
    own_ref[...] = gather_pairs(outs, pl.multiple_of(side * HALF, 8), HALF // 2)
    other_ref[0:112, :] = gather_pairs(dx, pl.multiple_of((1 - side) * HALF, 8), 112).astype(bf16)
    table = jnp.broadcast_to(jnp.sum(dots_ref[...], axis=1, keepdims=True), (8, LANES))
    table_ref[...] = table
    upper = table.astype(bf16).astype(f32)
    other_ref[112:128, :] = jnp.concatenate([upper, table - upper], axis=0).astype(bf16)


def rows_of(places, block, read, part, side, start, count):
    pieces = []
    while count:
        index, inside = divmod(start, block)
        take = min(count, block - inside)
        at = places[part][side][index] * block + inside
        pieces.append(read(at, take))
        start, count = start + take, count - take
    return pieces[0] if len(pieces) == 1 else jnp.concatenate(pieces, axis=0)


def half_turns():
    source = lax.broadcasted_iota(jnp.int32, (2 * LANES, 2 * LANES), 0)
    target = lax.broadcasted_iota(jnp.int32, (2 * LANES, 2 * LANES), 1)
    return (source == target // LANES * LANES + (target + D) % LANES).astype(f32).astype(bf16)


def expand(straight, turned, rows, grads, send):
    low = low_half(rows)
    copies = []
    for tile in range(TAPS // 2):
        (a0, b0), (a1, b1) = tap_place(2 * tile), tap_place(2 * tile + 1)
        left = (straight if b0 % 2 == 0 else turned)[b0 // 2, a0 * rows : (a0 + 1) * rows, :]
        right = (straight if b1 % 2 == 1 else turned)[b1 // 2, a1 * rows : (a1 + 1) * rows, :]
        grads[:, span(tile)] = jnp.where(low, left, right)
        if tile % 13 == 12:
            copies += send(tile // 13, pl.ds((tile - 12) * LANES, 13 * LANES))
    return copies


def read_half(places, block, core, part_is_mine, half_ref):
    part = core if part_is_mine else 1 - core

    def rows(side, start, count):
        def value(which):
            return rows_of(
                places, block, lambda at, take: half_ref[at : at + take, :], which, side, start, count
            )

        return jnp.where(part == 0, value(0), value(1))

    return part, rows


def expand_inner(part, rows, grad_hbm, both, straight, turned, grads, sems):
    for side in range(2):
        for row in range(11):
            at = row * 32 + side * 16
            for plane in range(5):
                both[at : at + 16, span(plane)] = rows(side, plane * 176 + row * 16, 16)
            v = rows(side, 880 + row % 6 * 16, 16)
            if row >= 6:
                v = pltpu.roll(v.astype(f32), D, 1).astype(bf16)
            both[at : at + 16, span(5)] = v
    turn = half_turns()
    for pair in range(3):
        lanes = slice(2 * pair * LANES, 2 * (pair + 1) * LANES)
        v = both[:, lanes]
        swapped = jnp.dot(v, turn, preferred_element_type=f32)
        for plane in range(2):
            straight[2 * pair + plane] = v[:, span(plane)].astype(f32)
            turned[2 * pair + plane] = swapped[:, span(plane)]

    def send(index, lanes):
        copies = []
        for side in range(2):
            target = pl.ds(pl.multiple_of(side * 32 + part * 16, 16), 16)
            copy = pltpu.make_async_copy(
                grads.at[pl.ds(side * 16, 16), lanes], grad_hbm.at[target, lanes], sems.at[2 * index + side]
            )
            copy.start()
            copies.append(copy)
        return copies

    return expand(straight, turned, 32, grads, send)


def expand_outer(part, rows, grad_hbm, both, straight, turned, grads, sems):
    for side in range(2):
        for plane in range(3):
            both[:, span(2 * plane + side)] = rows(side, plane * 352, 352)
    source = lax.broadcasted_iota(jnp.int32, (2 * LANES, 2 * LANES), 0)
    target = lax.broadcasted_iota(jnp.int32, (2 * LANES, 2 * LANES), 1)
    wanted = (target // 64) * 32 + target % 32 + LANES * (target // 32 % 2)
    place = (source == wanted).astype(f32).astype(bf16)
    other = target // LANES * LANES + (target + D) % LANES
    wanted = (other // 64) * 32 + other % 32 + LANES * (other // 32 % 2)
    place_turned = (source == wanted).astype(f32).astype(bf16)
    for pair in range(3):
        v = both[:, 2 * pair * LANES : 2 * (pair + 1) * LANES]
        for target_ref, matrix in ((straight, place), (turned, place_turned)):
            moved = jnp.dot(v, matrix, preferred_element_type=f32)
            for plane in range(2):
                target_ref[2 * pair + plane] = moved[:, span(plane)]

    def send(index, lanes):
        target = pl.ds(pl.multiple_of(part * 32, 32), 32)
        copy = pltpu.make_async_copy(grads.at[:, lanes], grad_hbm.at[target, lanes], sems.at[index])
        copy.start()
        return [copy]

    return expand(straight, turned, 32, grads, send)


def first_last_kernel(plan_out, where_ref, mine_ref, grad_hbm, *scratch):
    part, rows = read_half(*plan_out, where_ref[1], True, mine_ref)
    for copy in expand_outer(part, rows, grad_hbm, *scratch):
        copy.wait()


def second_last_kernel(
    plan_out,
    plan_in,
    where_ref,
    amp_ref,
    theirs_ref,
    mine_ref,
    own_ref,
    recv_ref,
    table_ref,
    begun_hbm,
    grad_out_hbm,
    grad_in_hbm,
    series_hbm,
    amps_hbm,
    series_ref,
    amps_ref,
    small_sems,
    *scratch,
):
    core = where_ref[1]
    gained = own_ref[...] + recv_ref[0:112, :].astype(f32)[: HALF // 2, :]
    series_ref[...] = gained.reshape(1, HALF * D)
    tail = recv_ref[112:128, :].astype(f32)
    dots = table_ref[...] + tail[0:8, :] + tail[8:16, :]
    mixing = mixing_of(amp_ref[...])
    pick = (
        lax.broadcasted_iota(jnp.int32, (8, K), 0) == lax.broadcasted_iota(jnp.int32, (8, K), 1)
    )
    table = jnp.sum(jnp.where(pick, dots[:, 0:K], 0.0), axis=0, keepdims=True)
    amps_ref[...] = mixing * (table - jnp.sum(mixing * table, axis=-1, keepdims=True))
    copies = [
        pltpu.make_async_copy(series_ref, series_hbm, small_sems.at[0]),
        pltpu.make_async_copy(amps_ref, amps_hbm, small_sems.at[1]),
    ]
    for copy in copies:
        copy.start()
    part, rows = read_half(*plan_out, core, False, theirs_ref)
    copies += expand_outer(part, rows, grad_out_hbm, *scratch[:5])
    part, rows = read_half(*plan_in, core, True, mine_ref)
    copies += expand_inner(part, rows, grad_in_hbm, *scratch[5:])
    for copy in copies:
        copy.wait()


def third_last_kernel(
    plan_in,
    where_ref,
    mine_ref,
    theirs_ref,
    begun_hbm,
    grad_hbm,
    bias_in_hbm,
    bias_out_hbm,
    gain_hbm,
    shift_hbm,
    bias_in_ref,
    bias_out_ref,
    gain_ref,
    shift_ref,
    small_sems,
    *scratch,
):
    core = where_ref[1]
    part, rows = read_half(*plan_in, core, False, theirs_ref)
    _, mine = read_half(*plan_in, core, True, mine_ref)

    def mean(side):
        both = rows(side, 976, 48).astype(f32) + mine(side, 976, 48).astype(f32)
        v = jnp.sum((both / copy_scale()).reshape(12, 4, LANES), axis=0) * (1.0 / 24.0)
        return (v + pltpu.roll(v, D, 1)) * 0.5

    spare, other = mean(0), mean(1)
    bias_in_ref[...] = jnp.concatenate([spare[0:1, 0:32], other[0:1, 0:32]], axis=1)
    bias_out_ref[...] = spare[1:2, 0:64]
    gain_ref[...] = spare[2:3, 0:64]
    shift_ref[...] = spare[3:4, 0:64]
    small = []
    for index, (source, target) in enumerate(
        (
            (bias_in_ref, bias_in_hbm),
            (bias_out_ref, bias_out_hbm),
            (gain_ref, gain_hbm),
            (shift_ref, shift_hbm),
        )
    ):
        copy = pltpu.make_async_copy(source, target, small_sems.at[index])
        copy.start()
        small.append(copy)
    copies = expand_inner(part, rows, grad_hbm, *scratch) + small
    for copy in copies:
        copy.wait()


def on_device(
    series,
    amplitudes,
    periods,
    conv_in,
    bias_in,
    conv_out,
    bias_out,
    norm_gain,
    norm_bias,
    cotangent,
):
    items = lax.axis_size("items")
    bits = items.bit_length() - 1
    me = lax.axis_index("items")
    side = lax.axis_index("narrow")
    core = me % 2
    where = jnp.stack([side, core]).astype(jnp.int32)
    vmem = pl.BlockSpec(memory_space=pltpu.VMEM)
    smem = pl.BlockSpec(memory_space=pltpu.SMEM)
    hbm = pl.BlockSpec(memory_space=pltpu.HBM)
    shape = jax.ShapeDtypeStruct

    def limit(mib):
        return pltpu.CompilerParams(vmem_limit_bytes=mib * 1024 * 1024)

    def cost(flops):
        return pl.CostEstimate(flops=flops, bytes_accessed=4 << 20, transcendentals=0)

    def stay(arrays):
        return [pltpu.with_memory_space_constraint(a, pltpu.VMEM) for a in arrays]

    def far(arrays):
        return [pltpu.with_memory_space_constraint(a, pltpu.HBM) for a in arrays]

    def two(rows, lanes, kind=f32, lead=None):
        dims = (rows, lanes) if lead is None else (lead, rows, lanes)
        return [pltpu.VMEM(dims, kind)] * 2

    margin = NEAR + GRID + 336
    halved = list(range(1, bits - 1))
    blocks = 2 ** len(halved)
    half_out = -(-1056 // (16 * blocks)) * 16 * blocks
    send, total, part, w1, w2, xs, ua, slope = pl.pallas_call(
        forward_kernel,
        out_shape=(
            pltpu.VMEM((FOLD + 112, LANES), bf16),
            pltpu.VMEM((FOLD, LANES), f32),
            pltpu.VMEM((K, FOLD, LANES), f32),
            pltpu.HBM((WIDE, FULL), bf16),
            pltpu.HBM((FULL, WIDE), bf16),
            pltpu.VMEM((512, LANES), f32),
            pltpu.VMEM((K, GRID, WIDE), bf16),
            pltpu.VMEM((K, QUART, LANES), f32),
        ),
        in_specs=[smem] + [hbm] * 8,
        out_specs=[vmem, vmem, vmem, hbm, hbm, vmem, vmem, vmem],
        scratch_shapes=[
            pltpu.VMEM((WIDE + LANES, FULL), bf16),
            pltpu.VMEM((FULL, WIDE + LANES), bf16),
            pltpu.VMEM((FULL, 2 * LANES), bf16),
            pltpu.VMEM((K, GRID, FULL), bf16),
            pltpu.SMEM((1, K), jnp.int32),
            pltpu.VMEM((1, K), f32),
            pltpu.VMEM((1, STEPS * D), bf16),
            pltpu.VMEM((1, HALF * D), bf16),
            pltpu.VMEM((32, TAPS * D), bf16),
            pltpu.VMEM((64, TAPS * D), bf16),
            pltpu.VMEM((1, FF), f32),
            pltpu.VMEM((1, D), f32),
            pltpu.VMEM((6, GRID, LANES), bf16),
            pltpu.VMEM((FULL, FULL), bf16),
            *two(512, LANES),
            *two(margin, LANES, f32, 3),
            pltpu.VMEM((3, margin, LANES), f32),
            *two(margin, LANES, f32, 6),
            *two(GRID + 3 * PMAX, LANES),
            *two(GRID + PMAX, LANES),
            *two(2 * QUART, LANES),
            pltpu.SemaphoreType.DMA((12,)),
            pltpu.SemaphoreType.DMA((2,)),
        ],
        compiler_params=limit(28),
        cost_estimate=cost(1 << 33),
        name="forward",
    )(
        where,
        *far(
            [
                periods,
                amplitudes,
                series,
                cotangent,
                conv_in.T,
                conv_out.T,
                bias_in[None, :],
                bias_out[None, :],
            ]
        ),
    )

    def exchange(value, partner):
        pairs = []
        for item in range(items):
            for col in range(2):
                to_item, to_col = partner(item, col)
                pairs.append((item * 2 + col, to_item * 2 + to_col))
        return lax.ppermute(value, ("items", "narrow"), pairs)

    across = lambda item, col: (item, 1 - col)
    chip = lambda item, col: (item ^ 1, col)
    recv = exchange(send, across)

    out, keep_out, give_out, grad, merged, dots, small, w1 = pl.pallas_call(
        outer_kernel,
        out_shape=(
            shape((1, HALF * D), bf16),
            pltpu.VMEM((half_out, LANES), bf16),
            pltpu.VMEM((half_out, LANES), bf16),
            pltpu.VMEM((K, QUART, LANES), f32),
            pltpu.VMEM((PAIR, LANES), f32),
            pltpu.VMEM((8, LANES), f32),
            pltpu.VMEM((8, LANES), f32),
            pltpu.VMEM((WIDE, FULL), bf16),
        ),
        in_specs=[smem, smem] + [vmem] * 6 + [hbm] * 2 + [vmem] * 4,
        out_specs=[hbm] + [vmem] * 7,
        scratch_shapes=[
            pltpu.VMEM((PAIR, LANES), f32),
            pltpu.VMEM((PAIR, LANES), f32),
            pltpu.VMEM((PAIR, LANES), f32),
            pltpu.VMEM((PMAX + GRID, LANES), f32),
            pltpu.VMEM((FOLD, LANES), f32),
            *two(NEAR + GRID + NEAR, LANES),
            *two(GRID, FULL, bf16),
            *two(GRID + 32, LANES, f32, 3),
            *two(GRID + 16, LANES),
            *two(2 * QUART, LANES),
            pltpu.VMEM((WIDE, FULL), f32),
            pltpu.VMEM((2 * half_out, LANES), bf16),
            pltpu.VMEM((FULL, WIDE), bf16),
            pltpu.VMEM((1, HALF * D), bf16),
            pltpu.SemaphoreType.DMA((2,)),
            pltpu.SemaphoreType.DMA,
        ],
        compiler_params=limit(16),
        cost_estimate=cost(1 << 33),
        name="outer",
    )(
        where,
        periods,
        amplitudes,
        cotangent,
        *stay([recv, total, xs, part]),
        *far([w1, w2]),
        *stay([ua, slope]),
        norm_gain[None, :],
        norm_bias[None, :],
    )

    keep_in, give_in = pl.pallas_call(
        inner_kernel,
        out_shape=(
            pltpu.VMEM((HALF_IN, LANES), bf16),
            pltpu.VMEM((HALF_IN, LANES), bf16),
        ),
        in_specs=[smem, smem] + [vmem] * 3,
        out_specs=[vmem] * 2,
        scratch_shapes=[
            *two(3 * PMAX + GRID + NEAR, LANES),
            pltpu.VMEM((6, GRID, LANES), bf16),
            *two(GRID, WIDE, bf16),
            *two(GRID, FULL, bf16),
            pltpu.VMEM((WIDE, FULL), f32),
            pltpu.VMEM((2 * HALF_IN, LANES), bf16),
        ],
        compiler_params=limit(16),
        cost_estimate=cost(1 << 33),
        name="inner",
    )(where, periods, *stay([grad, small, xs]))

    by_rows = [
        *two(3 * PMAX + GRID + NEAR, LANES),
        *two(GRID, WIDE, bf16),
        *two(GRID + 32, LANES, f32, 6),
    ]

    def series_begin(grad, w1):
        return pl.pallas_call(
            series_kernel,
            out_shape=pltpu.VMEM((GRID, LANES), f32),
            in_specs=[smem] + [vmem] * 2,
            out_specs=vmem,
            scratch_shapes=by_rows,
            compiler_params=limit(16),
            cost_estimate=cost(1 << 31),
            name="series",
        )(periods, *stay([grad, w1]))

    def series_rest(grad, w1, begun):
        return pl.pallas_call(
            series_rest_kernel,
            out_shape=(
                pltpu.VMEM((HALF // 2, LANES), f32),
                pltpu.VMEM((128, LANES), bf16),
                pltpu.VMEM((8, LANES), f32),
            ),
            in_specs=[smem, smem] + [vmem] * 5,
            out_specs=[vmem] * 3,
            scratch_shapes=[
                *by_rows,
                pltpu.VMEM((GRID, LANES), f32),
                pltpu.VMEM((PAIR, LANES), f32),
                pltpu.VMEM((PAIR, LANES), f32),
            ],
            compiler_params=limit(16),
            cost_estimate=cost(1 << 31),
            name="series_rest",
        )(where, periods, *stay([grad, merged, dots, w1, begun]))

    def partner_of(stage):
        def partner(item, col):
            axis = stage[item % 2]
            if axis is None:
                return (item, 1 - col)
            return (item ^ (1 << axis), col)

        return partner

    def bit_of(stage):
        values = [side if axis is None else (me >> axis) & 1 for axis in stage]
        return jnp.where(core == 0, values[0], values[1])

    def merge(bit, a, b):
        return jnp.concatenate([jnp.where(bit == 0, a, b), jnp.where(bit == 0, b, a)], axis=0)

    orders = (halved, halved[1::-1] + halved[2:])
    sequences = ([None] + halved[::-1], halved[::-1] + [None])

    def start_chain(keep, give):
        return keep.astype(f32) + exchange(give, chip).astype(f32)

    def halve(acc, position):
        stage = (orders[0][position], orders[1][position])
        bit = bit_of(stage)
        size = acc.shape[0] // 2
        gone = lax.dynamic_slice_in_dim(acc, (1 - bit) * size, size, 0).astype(bf16)
        kept = lax.dynamic_slice_in_dim(acc, bit * size, size, 0)
        return kept, gone, stage

    def sum_last(acc):
        mine = acc.astype(bf16)
        if bits > 1:
            theirs = exchange(mine, partner_of((bits - 1, bits - 1)))
            mine = (mine.astype(f32) + theirs.astype(f32)).astype(bf16)
        return mine

    def gather(mine, extra=None):
        came = []
        for position in range(len(sequences[0])):
            stage = (sequences[0][position], sequences[1][position])
            if extra is not None and None in stage:
                both = exchange(jnp.concatenate([mine, extra], axis=0), partner_of(stage))
                theirs = both[: mine.shape[0]]
                came.append(both[mine.shape[0] :])
            else:
                theirs = exchange(mine, partner_of(stage))
            mine = merge(bit_of(stage), mine, theirs)
        received = None if extra is None else jnp.where(core == 0, came[0], came[-1])
        return mine, exchange(mine, chip), received

    acc_out = start_chain(keep_out, give_out)
    acc_in = start_chain(keep_in, give_in)
    begun = None
    for position in range(len(halved)):
        kept_out, gone_out, stage = halve(acc_out, position)
        acc_out = kept_out + exchange(gone_out, partner_of(stage)).astype(f32)
        kept_in, gone_in, stage = halve(acc_in, position)
        if position < 2:
            gone_in, grad = lax.optimization_barrier((gone_in, grad))
        came_in = exchange(gone_in, partner_of(stage))
        if position == 0:
            begun = series_begin(grad, w1)
        if position == 1:
            own, other, table = series_rest(grad, w1, begun)
        acc_in = kept_in + came_in.astype(f32)
    if len(halved) < 1:
        begun = series_begin(grad, w1)
    if len(halved) < 2:
        own, other, table = series_rest(grad, w1, begun)
    mine_out, theirs_out, _ = gather(sum_last(acc_out))
    mine_in, theirs_in, received = gather(sum_last(acc_in), other)

    places = []
    for half in range(2):
        by_side = []
        for narrow in range(2):
            listed = []
            for index in range(blocks):
                value = {None: narrow}
                for position, axis in enumerate(orders[half]):
                    value[axis] = (index >> (len(halved) - 1 - position)) & 1
                place = 0
                for position, axis in enumerate(sequences[half]):
                    place += value[axis] << position
                listed.append(place)
            by_side.append(tuple(listed))
        places.append(tuple(by_side))
    places = tuple(places)

    plan_out = (places, half_out // blocks)
    plan_in = (places, HALF_IN // blocks)
    expanding = [
        pltpu.VMEM((352, FULL), bf16),
        pltpu.VMEM((6, 352, LANES), f32),
        pltpu.VMEM((6, 352, LANES), f32),
        pltpu.VMEM((32, TAPS * D), f32),
        pltpu.SemaphoreType.DMA((22,)),
    ]
    grad_out = pl.pallas_call(
        functools.partial(first_last_kernel, plan_out),
        out_shape=shape((D, TAPS * FF), f32),
        in_specs=[smem, vmem],
        out_specs=hbm,
        scratch_shapes=expanding,
        compiler_params=limit(16),
        cost_estimate=cost(1 << 31),
        name="first_last",
    )(where, mine_out)
    grad_out, grad_in, g_series, g_amps = pl.pallas_call(
        functools.partial(second_last_kernel, plan_out, plan_in),
        out_shape=(
            shape((D, TAPS * FF), f32),
            shape((FF, TAPS * D), f32),
            shape((1, HALF * D), f32),
            shape((1, K), f32),
        ),
        in_specs=[smem] + [vmem] * 6 + [hbm],
        out_specs=[hbm] * 4,
        input_output_aliases={7: 0},
        scratch_shapes=[
            pltpu.VMEM((1, HALF * D), f32),
            pltpu.VMEM((1, K), f32),
            pltpu.SemaphoreType.DMA((2,)),
            *expanding,
            *expanding,
        ],
        compiler_params=limit(24),
        cost_estimate=cost(1 << 32),
        name="second_last",
    )(where, amplitudes, theirs_out, mine_in, own, received, table, grad_out)
    grad_in, g_bias_in, g_bias_out, g_gain, g_shift = pl.pallas_call(
        functools.partial(third_last_kernel, plan_in),
        out_shape=(
            shape((FF, TAPS * D), f32),
            shape((1, FF), f32),
            shape((1, D), f32),
            shape((1, D), f32),
            shape((1, D), f32),
        ),
        in_specs=[smem, vmem, vmem, hbm],
        out_specs=[hbm] * 5,
        input_output_aliases={3: 0},
        scratch_shapes=[pltpu.VMEM((1, D), f32)] * 4 + [pltpu.SemaphoreType.DMA((4,))] + expanding,
        compiler_params=limit(16),
        cost_estimate=cost(1 << 31),
        name="third_last",
    )(where, mine_in, theirs_in, grad_in)
    return (
        out,
        g_series,
        g_amps,
        grad_in.T,
        g_bias_in[0],
        grad_out.T,
        g_bias_out[0],
        g_gain[0],
        g_shift[0],
    )


def solution(mesh):
    in_specs = (
        P("items", None),
        P("items", None),
        P("items", None),
        P(),
        P(),
        P(),
        P(),
        P(),
        P(),
        P("items", "narrow"),
    )
    out_specs = (
        P("items", "narrow"),
        P("items", "narrow"),
        P("items", None),
        P(),
        P(),
        P(),
        P(),
        P(),
        P(),
    )
    return jax.shard_map(
        on_device, mesh=mesh, in_specs=in_specs, out_specs=out_specs, check_vma=False
    )
```

time: 2640 us -> 75.1 us (0.03); the launches traced: 2600 us -> 74.9 us
  other arithmetic: 1260 us -> 0.86 us
  local copies, waits for them, and re-layouts: 729 us -> 0.1 us
  matrix products: 203 us -> 0 us
  waiting for transfers between devices: 207 us -> 14.6 us
  loops' own time: 126 us -> 0 us
  blocking collectives: 52 us -> 0 us
  Pallas kernels: 0 us -> 34.2 us
    while x1650 -> x0, other arithmetic: 692 us -> none
    while x248 -> x0, local copies, waits for them, and re-layouts: 649 us -> none
    select_n x175 -> x7, other arithmetic: 512 us -> 0.39 us  [the longest x6 0.38 us: merge(): jnp.where(bit == 0, a, b)]
    dot_general x21 -> x0, matrix products: 203 us -> none  [the longest x12 126 us: apply_weight(): product = jnp.dot(unfolded, prepared, preferred_element_type=jnp.float32)]
    psum x1 -> x0, waiting for transfers between devices: 163 us -> none  [on_device(): lax.psum((grad_conv_in, grad_bias_in, grad_conv_out, grad_bias_out, grad_...]
    another operation x3 -> x0, loops' own time: 126 us -> none  [the longest x1 46.8 us: on_device(): lax.map(forward_slot, (item_index, slot_period))]
    psum x2 -> x0, blocking collectives: 47 us -> none  [the longest x1 42 us: on_device(): lax.psum((grad_conv_in, grad_bias_in, grad_conv_out, grad_bias_out, grad_...]
    unnamed x3 -> x0, waiting for transfers between devices: 44.2 us -> none
  transfers between devices with their start and end apart: 3 -> 17, of which waited for: 2 -> 11; matrix products, arithmetic and copies ran while one was open for 2% -> 1% of each run, Pallas kernels for 0% -> 14%
where the time goes in v2:
time: 75.1 us; the launch traced here: 74.9 us
  Pallas kernels  34.2 us (46%)
  starting transfers between devices  24 us (32%)
  waiting for transfers between devices  14.6 us (19%)
  between operations  1.13 us (2%)
  other arithmetic  0.86 us (1%)
    ppermute x17, starting transfers between devices, exchange(): return lax.ppermute(value, ('items', 'narrow'), pairs)  24 us
    ppermute x17, waiting for transfers between devices, exchange(): return lax.ppermute(value, ('items', 'narrow'), pairs)  14.6 us
    pallas_call x1, Pallas kernels, on_device(): pl.pallas_call(forward_kernel, out_shape=(pltpu.VMEM((FOLD + 112, LANES),...  10 us
    pallas_call x1, Pallas kernels, on_device(): pl.pallas_call(outer_kernel, out_shape=(shape((1, HALF * D), bf16), pltpu...  6.97 us
    pallas_call x1, Pallas kernels, on_device(): pl.pallas_call(inner_kernel, out_shape=(pltpu.VMEM((HALF_IN, LANES), bf16...  4.13 us
    pallas_call x1, Pallas kernels, on_device(): pl.pallas_call(functools.partial(second_last_kernel, plan_out, plan_in),...  3.59 us
    pallas_call x1, Pallas kernels, on_device(): pl.pallas_call(functools.partial(first_last_kernel, plan_out), out_shape=...  2.48 us
    pallas_call x1, Pallas kernels, on_device(): pl.pallas_call(functools.partial(third_last_kernel, plan_in), out_shape=(...  2.48 us
  transfers between devices with their start and end apart: 17, of which 11 were waited for; matrix products, arithmetic and copies ran while one was open for 1% of the time, Pallas kernels for 14%

profile of v2, /device:TPU:0, one launch (start us, length us, event | category | flops | bytes accessed | tf_op | source)
XLA Modules:
  0.0 74.9 jit_solution(900365206916631617)
XLA Ops:
  0.8 10.0 %forward.1 = (bf16[336,128]{1,0:T(8,128)(2,1)S(1)}, f32[224,128]{1,0:T(8,128)S(1)}, f32[5,224,128]{2,1,0:T(8,128)S(1)}, bf16[384,768]{1,0:T(8,128)(2,1)}, bf16[7...) custom-call(s32[2]{0:T(128)S(1)} %pad_add_fusion.where_ref, ...), custom_call_target="tpu_custom_call" | custom-call | flops 8589934592 | bytes 4194304 | tf_op jit(solution)/shard_map/forward/pallas_call | solution.py:1211
  10.8 3.0 %collective-permute-start = (bf16[336,128]{1,0:T(8,128)(2,1)S(1)}, bf16[336,128]{1,0:T(8,128)(2,1)S(1)}, u32[]{:S(2)}, u32[]{:S(2)}) collective-permute-start(bf16[336,128]{1,0:T(8,128)(2,1)S(1)} %get-tuple-element.43), channel_id=1, source_target_pairs={{0,1},{1,0},{2,3},{3,2},{4,5},{5,4},{6,7},{7,6},{8,9},{9,8},{10,11... | collective-permute-start | bytes 258056 | tf_op jit(solution)/shard_map/ppermute | solution.py:1275
  13.8 2.6 %collective-permute-done.recv_ref = bf16[336,128]{1,0:T(8,128)(2,1)S(1)} collective-permute-done((bf16[336,128]{1,0:T(8,128)(2,1)S(1)}, bf16[336,128]{1,0:T(8,128)(2,1)S(1)}, u32[]{:S(2)}, u32[]{:S(2)}) %collective-permute-start) | collective-permute-done | bytes 86048 | tf_op jit(solution)/shard_map/ppermute | solution.py:1275
  16.4 7.0 %outer.1 = (bf16[1,13824]{1,0:T(2,128)(2,1)}, bf16[1088,128]{1,0:T(8,128)(2,1)S(1)}, bf16[1088,128]{1,0:T(8,128)(2,1)S(1)}, f32[5,120,128]{2,1,0:T(8,128)S(1)}, ...) custom-call(s32[2]{0:T(128)S(1)} %pad_add_fusion.where_ref, ...), custom_call_target="tpu_custom_call" | custom-call | flops 8589934592 | bytes 4194304 | tf_op jit(solution)/shard_map/outer/pallas_call | solution.py:1281
  23.4 4.1 %inner.1 = (bf16[1024,128]{1,0:T(8,128)(2,1)S(1)}, bf16[1024,128]{1,0:T(8,128)(2,1)S(1)}) custom-call(s32[2]{0:T(128)S(1)} %pad_add_fusion.where_ref, s32[1,5]{1,0:T(1,128)S(1)} %copy-done.3, f32[5,120,128]{2,1,0:T(8,128)S(1)} %get-tuple-element.61.grad_ref, f32[8,128]{1,0:T(8,128)S(1)} %get-tuple-element.55.small_ref, f32[512,128]{1,0:T(8,128)S(1)} %get-tuple-element.45.xs), custom_call_target="tpu_custom_call" | custom-call | flops 8589934592 | bytes 4194304 | tf_op jit(solution)/shard_map/inner/pallas_call | solution.py:1328
  29.2 2.1 %collective-permute-start.10 = (bf16[512,128]{1,0:T(8,128)(2,1)S(1)}, bf16[512,128]{1,0:T(8,128)(2,1)S(1)}, u32[]{:S(2)}, u32[]{:S(2)}) collective-permute-start(bf16[512,128]{1,0:T(8,128)(2,1)S(1)} %dynamic-slice_convert_fusion.1), channel_id=1, source_target_pairs={{0,4},{1,5},{2,10},{3,11},{4,0},{5,1},{6,14},{7,15},{8,12},{9,13},... | collective-permute-start | bytes 393224 | tf_op jit(solution)/shard_map/ppermute | solution.py:1275
  31.3 2.5 %series.1.begun_ref = f32[480,128]{1,0:T(8,128)S(1)} custom-call(s32[1,5]{1,0:T(1,128)S(1)} %copy-done.3, f32[5,120,128]{2,1,0:T(8,128)S(1)} %get-tuple-element.61.grad_ref, bf16[384,768]{1,0:T(8,128)(2,1)S(1)} %get-tuple-element.64.w1_ref), custom_call_target="tpu_custom_call" | custom-call | flops 2147483648 | bytes 4194304 | tf_op jit(solution)/shard_map/series/pallas_call | solution.py:1356
  34.3 2.2 %collective-permute-start.11 = (bf16[256,128]{1,0:T(8,128)(2,1)S(1)}, bf16[256,128]{1,0:T(8,128)(2,1)S(1)}, u32[]{:S(2)}, u32[]{:S(2)}) collective-permute-start(bf16[256,128]{1,0:T(8,128)(2,1)S(1)} %dynamic-slice_convert_fusion.3), channel_id=1, source_target_pairs={{0,8},{1,9},{2,6},{3,7},{4,12},{5,13},{6,2},{7,3},{8,0},{9,1},{10,... | collective-permute-start | bytes 196616 | tf_op jit(solution)/shard_map/ppermute | solution.py:1275
  36.5 2.1 %series_rest.1 = (f32[108,128]{1,0:T(8,128)S(1)}, bf16[128,128]{1,0:T(8,128)(2,1)S(1)}, f32[8,128]{1,0:T(8,128)S(1)}) custom-call(s32[2]{0:T(128)S(1)} %pad_add_fusion.where_ref, s32[1,5]{1,0:T(1,128)S(1)} %copy-done.3, f32[5,120,128]{2,1,0:T(8,128)S(1)} %get-tuple-element.61.grad_ref, f32[448,128]{1,0:T(8,128)S(1)} %get-tuple-element.62.merged_ref, ...), custom_call_target="tpu_custom_call" | custom-call | flops 2147483648 | bytes 4194304 | tf_op jit(solution)/shard_map/series_rest/pallas_call | solution.py:1368
  39.1 1.7 %collective-permute-start.3 = (bf16[272,128]{1,0:T(8,128)(2,1)S(1)}, bf16[272,128]{1,0:T(8,128)(2,1)S(1)}, u32[]{:S(2)}, u32[]{:S(2)}) collective-permute-start(bf16[272,128]{1,0:T(8,128)(2,1)S(1)} %dynamic-slice_convert_fusion.2), channel_id=1, source_target_pairs={{0,8},{1,9},{2,6},{3,7},{4,12},{5,13},{6,2},{7,3},{8,0},{9,1},{10,... | collective-permute-start | bytes 208904 | tf_op jit(solution)/shard_map/ppermute | solution.py:1275
  40.8 2.7 %collective-permute-start.12 = (bf16[256,128]{1,0:T(8,128)(2,1)S(1)}, bf16[256,128]{1,0:T(8,128)(2,1)S(1)}, u32[]{:S(2)}, u32[]{:S(2)}) collective-permute-start(bf16[256,128]{1,0:T(8,128)(2,1)S(1)} %add_convert_fusion.3), channel_id=1, source_target_pairs={{0,16},{1,17},{2,18},{3,19},{4,20},{5,21},{6,22},{7,23},{8,24},{9,... | collective-permute-start | bytes 196616 | tf_op jit(solution)/shard_map/ppermute | solution.py:1275
  43.5 2.8 %collective-permute-start.4 = (bf16[272,128]{1,0:T(8,128)(2,1)S(1)}, bf16[272,128]{1,0:T(8,128)(2,1)S(1)}, u32[]{:S(2)}, u32[]{:S(2)}) collective-permute-start(bf16[272,128]{1,0:T(8,128)(2,1)S(1)} %add_convert_fusion.1), channel_id=1, source_target_pairs={{0,16},{1,17},{2,18},{3,19},{4,20},{5,21},{6,22},{7,23},{8,24},{9,... | collective-permute-start | bytes 208904 | tf_op jit(solution)/shard_map/ppermute | solution.py:1275
  46.3 1.7 %collective-permute-done.12 = bf16[256,128]{1,0:T(8,128)(2,1)S(1)} collective-permute-done((bf16[256,128]{1,0:T(8,128)(2,1)S(1)}, bf16[256,128]{1,0:T(8,128)(2,1)S(1)}, u32[]{:S(2)}, u32[]{:S(2)}) %collective-permute-start.12) | collective-permute-done | bytes 65568 | tf_op jit(solution)/shard_map/ppermute | solution.py:1275
  49.0 1.6 %collective-permute-start.5 = (bf16[272,128]{1,0:T(8,128)(2,1)S(1)}, bf16[272,128]{1,0:T(8,128)(2,1)S(1)}, u32[]{:S(2)}, u32[]{:S(2)}) collective-permute-start(bf16[272,128]{1,0:T(8,128)(2,1)S(1)} %add_convert_fusion), channel_id=1, source_target_pairs={{0,1},{1,0},{2,10},{3,11},{4,5},{5,4},{6,14},{7,15},{8,9},{9,8},{1... | collective-permute-start | bytes 208904 | tf_op jit(solution)/shard_map/ppermute | solution.py:1275
  51.1 2.2 %collective-permute-done.5 = bf16[272,128]{1,0:T(8,128)(2,1)S(1)} collective-permute-done((bf16[272,128]{1,0:T(8,128)(2,1)S(1)}, bf16[272,128]{1,0:T(8,128)(2,1)S(1)}, u32[]{:S(2)}, u32[]{:S(2)}) %collective-permute-start.5) | collective-permute-done | bytes 69664 | tf_op jit(solution)/shard_map/ppermute | solution.py:1275
  53.4 1.9 %collective-permute-start.6 = (bf16[544,128]{1,0:T(8,128)(2,1)S(1)}, bf16[544,128]{1,0:T(8,128)(2,1)S(1)}, u32[]{:S(2)}, u32[]{:S(2)}) collective-permute-start(bf16[544,128]{1,0:T(8,128)(2,1)S(1)} %pad_maximum_fusion.5), channel_id=1, source_target_pairs={{0,8},{1,9},{2,6},{3,7},{4,12},{5,13},{6,2},{7,3},{8,0},{9,1},{10,... | collective-permute-start | bytes 417800 | tf_op jit(solution)/shard_map/ppermute | solution.py:1275
  55.3 1.9 %collective-permute-start.14 = (bf16[512,128]{1,0:T(8,128)(2,1)S(1)}, bf16[512,128]{1,0:T(8,128)(2,1)S(1)}, u32[]{:S(2)}, u32[]{:S(2)}) collective-permute-start(bf16[512,128]{1,0:T(8,128)(2,1)S(1)} %pad_maximum_fusion.6), channel_id=1, source_target_pairs={{0,8},{1,9},{2,6},{3,7},{4,12},{5,13},{6,2},{7,3},{8,0},{9,1},{10,... | collective-permute-start | bytes 393224 | tf_op jit(solution)/shard_map/ppermute | solution.py:1275
  57.1 1.3 %collective-permute-done.6 = bf16[544,128]{1,0:T(8,128)(2,1)S(1)} collective-permute-done((bf16[544,128]{1,0:T(8,128)(2,1)S(1)}, bf16[544,128]{1,0:T(8,128)(2,1)S(1)}, u32[]{:S(2)}, u32[]{:S(2)}) %collective-permute-start.6) | collective-permute-done | bytes 139296 | tf_op jit(solution)/shard_map/ppermute | solution.py:1275
  58.6 1.4 %collective-permute-start.7 = (bf16[1088,128]{1,0:T(8,128)(2,1)S(1)}, bf16[1088,128]{1,0:T(8,128)(2,1)S(1)}, u32[]{:S(2)}, u32[]{:S(2)}) collective-permute-start(bf16[1088,128]{1,0:T(8,128)(2,1)S(1)} %pad_maximum_fusion.3), channel_id=1, source_target_pairs={{0,4},{1,5},{2,3},{3,2},{4,0},{5,1},{6,7},{7,6},{8,12},{9,13},{10,... | collective-permute-start | bytes 835592 | tf_op jit(solution)/shard_map/ppermute | solution.py:1275
  60.4 1.4 %collective-permute-start.15 = (bf16[1152,128]{1,0:T(8,128)(2,1)S(1)}, bf16[1152,128]{1,0:T(8,128)(2,1)S(1)}, u32[]{:S(2)}, u32[]{:S(2)}) collective-permute-start(bf16[1152,128]{1,0:T(8,128)(2,1)S(1)} %pad_maximum_fusion.2), channel_id=1, source_target_pairs={{0,4},{1,5},{2,3},{3,2},{4,0},{5,1},{6,7},{7,6},{8,12},{9,13},{10,... | collective-permute-start | bytes 884744 | tf_op jit(solution)/shard_map/ppermute | solution.py:1275
  61.8 3.4 %collective-permute-done.7 = bf16[1088,128]{1,0:T(8,128)(2,1)S(1)} collective-permute-done((bf16[1088,128]{1,0:T(8,128)(2,1)S(1)}, bf16[1088,128]{1,0:T(8,128)(2,1)S(1)}, u32[]{:S(2)}, u32[]{:S(2)}) %collective-permute-start.7) | collective-permute-done | bytes 278560 | tf_op jit(solution)/shard_map/ppermute | solution.py:1275
  65.5 2.5 %first_last.1.begun_hbm = f32[64,18304]{1,0:T(8,128)} custom-call(s32[2]{0:T(128)S(1)} %pad_add_fusion.where_ref, bf16[2176,128]{1,0:T(8,128)(2,1)S(1)} %pad_maximum_fusion.mine_ref), custom_call_target="tpu_custom_call" | custom-call | flops 2147483648 | bytes 4194304 | tf_op jit(solution)/shard_map/first_last/pallas_call | solution.py:1487
  68.7 3.6 %second_last.1 = (f32[64,18304]{1,0:T(8,128)}, f32[64,18304]{1,0:T(8,128)}, f32[1,13824]{1,0:T(1,128)}, f32[1,5]{1,0:T(1,128)}) custom-call(s32[2]{0:T(128)S(1)} %pad_add_fusion.where_ref, f32[1,5]{1,0:T(1,128)S(1)} %copy-done.4, bf16[2176,128]{1,0:T(8,128)(2,1)S(1)} %collective-permute-done.8.theirs_ref, ...), custom_call_target="tpu_custom_call", output_to_operand_aliasing={{0}: (7, {})} | custom-call | flops 4294967296 | bytes 4194304 | tf_op jit(solution)/shard_map/second_last/pallas_call | solution.py:1497
  72.3 2.5 %third_last.1 = (f32[64,18304]{1,0:T(8,128)}, f32[1,64]{1,0:T(1,128)}, f32[1,64]{1,0:T(1,128)}, f32[1,64]{1,0:T(1,128)}, f32[1,64]{1,0:T(1,128)}) custom-call(s32[2]{0:T(128)S(1)} %pad_add_fusion.where_ref, bf16[2048,128]{1,0:T(8,128)(2,1)S(1)} %pad_maximum_fusion.1.mine_ref, ...), custom_call_target="tpu_custom_call", output_to_operand_aliasing={{0}: (3, {})} | custom-call | flops 2147483648 | bytes 4194304 | tf_op jit(solution)/shard_map/third_last/pallas_call | solution.py:1519
  (55 shorter events, 5.8 us)
Async XLA Ops:
  0.7 15.7 %copy-start = (bf16[1,13824]{1,0:T(2,128)(2,1)S(1)}, bf16[1,13824]{1,0:T(2,128)(2,1)}, u32[]{:S(2)}) copy-start(bf16[1,13824]{1,0:T(2,128)(2,1)} %cot_ref.1) | copy-start | bytes 82948
  0.7 15.7 %copy-start.1 = (f32[64]{0:T(128)S(1)}, f32[64]{0:T(128)}, u32[]{:S(2)}) copy-start(f32[64]{0:T(128)} %param.17) | copy-start | bytes 772
  0.7 15.7 %copy-start.2 = (f32[64]{0:T(128)S(1)}, f32[64]{0:T(128)}, u32[]{:S(2)}) copy-start(f32[64]{0:T(128)} %param.18) | copy-start | bytes 772
  0.7 15.7 %copy-start.3 = (s32[1,5]{1,0:T(1,128)S(1)}, s32[1,5]{1,0:T(1,128)}, u32[]{:S(2)}) copy-start(s32[1,5]{1,0:T(1,128)} %periods_ref.7) | copy-start | bytes 64
  0.7 15.7 %copy-start.4 = (f32[1,5]{1,0:T(1,128)S(1)}, f32[1,5]{1,0:T(1,128)}, u32[]{:S(2)}) copy-start(f32[1,5]{1,0:T(1,128)} %amp_ref.3) | copy-start | bytes 64
  10.8 5.6 %collective-permute-start = (bf16[336,128]{1,0:T(8,128)(2,1)S(1)}, bf16[336,128]{1,0:T(8,128)(2,1)S(1)}, u32[]{:S(2)}, u32[]{:S(2)}) collective-permute-start(bf16[336,128]{1,0:T(8,128)(2,1)S(1)} %get-tuple-element.43), channel_id=1, source_target_pairs={{0,1},{1,0},{2,3},{3,2},{4,5},{5,4},{6,7},{7,6},{8,9},{9,8},{10,11... | collective-permute-start | bytes 258056 | tf_op jit(solution)/shard_map/ppermute | solution.py:1275
  27.5 1.6 %collective-permute-start.9 = (bf16[1024,128]{1,0:T(8,128)(2,1)S(1)}, bf16[1024,128]{1,0:T(8,128)(2,1)S(1)}, u32[]{:S(2)}, u32[]{:S(2)}) collective-permute-start(bf16[1024,128]{1,0:T(8,128)(2,1)S(1)} %get-tuple-element.57), channel_id=1, source_target_pairs={{0,2},{1,3},{2,0},{3,1},{4,6},{5,7},{6,4},{7,5},{8,10},{9,11},{10,... | collective-permute-start | bytes 786440 | tf_op jit(solution)/shard_map/ppermute | solution.py:1275
  27.7 6.1 %collective-permute-start.1 = (bf16[1088,128]{1,0:T(8,128)(2,1)S(1)}, bf16[1088,128]{1,0:T(8,128)(2,1)S(1)}, u32[]{:S(2)}, u32[]{:S(2)}) collective-permute-start(bf16[1088,128]{1,0:T(8,128)(2,1)S(1)} %get-tuple-element.53), channel_id=1, source_target_pairs={{0,2},{1,3},{2,0},{3,1},{4,6},{5,7},{6,4},{7,5},{8,10},{9,11},{10,... | collective-permute-start | bytes 835592 | tf_op jit(solution)/shard_map/ppermute | solution.py:1275
  29.2 5.0 %collective-permute-start.10 = (bf16[512,128]{1,0:T(8,128)(2,1)S(1)}, bf16[512,128]{1,0:T(8,128)(2,1)S(1)}, u32[]{:S(2)}, u32[]{:S(2)}) collective-permute-start(bf16[512,128]{1,0:T(8,128)(2,1)S(1)} %dynamic-slice_convert_fusion.1), channel_id=1, source_target_pairs={{0,4},{1,5},{2,10},{3,11},{4,0},{5,1},{6,14},{7,15},{8,12},{9,13},... | collective-permute-start | bytes 393224 | tf_op jit(solution)/shard_map/ppermute | solution.py:1275
  33.9 5.1 %collective-permute-start.2 = (bf16[544,128]{1,0:T(8,128)(2,1)S(1)}, bf16[544,128]{1,0:T(8,128)(2,1)S(1)}, u32[]{:S(2)}, u32[]{:S(2)}) collective-permute-start(bf16[544,128]{1,0:T(8,128)(2,1)S(1)} %dynamic-slice_convert_fusion), channel_id=1, source_target_pairs={{0,4},{1,5},{2,10},{3,11},{4,0},{5,1},{6,14},{7,15},{8,12},{9,13},... | collective-permute-start | bytes 417800 | tf_op jit(solution)/shard_map/ppermute | solution.py:1275
  34.3 6.4 %collective-permute-start.11 = (bf16[256,128]{1,0:T(8,128)(2,1)S(1)}, bf16[256,128]{1,0:T(8,128)(2,1)S(1)}, u32[]{:S(2)}, u32[]{:S(2)}) collective-permute-start(bf16[256,128]{1,0:T(8,128)(2,1)S(1)} %dynamic-slice_convert_fusion.3), channel_id=1, source_target_pairs={{0,8},{1,9},{2,6},{3,7},{4,12},{5,13},{6,2},{7,3},{8,0},{9,1},{10,... | collective-permute-start | bytes 196616 | tf_op jit(solution)/shard_map/ppermute | solution.py:1275
  39.1 4.4 %collective-permute-start.3 = (bf16[272,128]{1,0:T(8,128)(2,1)S(1)}, bf16[272,128]{1,0:T(8,128)(2,1)S(1)}, u32[]{:S(2)}, u32[]{:S(2)}) collective-permute-start(bf16[272,128]{1,0:T(8,128)(2,1)S(1)} %dynamic-slice_convert_fusion.2), channel_id=1, source_target_pairs={{0,8},{1,9},{2,6},{3,7},{4,12},{5,13},{6,2},{7,3},{8,0},{9,1},{10,... | collective-permute-start | bytes 208904 | tf_op jit(solution)/shard_map/ppermute | solution.py:1275
  40.8 7.2 %collective-permute-start.12 = (bf16[256,128]{1,0:T(8,128)(2,1)S(1)}, bf16[256,128]{1,0:T(8,128)(2,1)S(1)}, u32[]{:S(2)}, u32[]{:S(2)}) collective-permute-start(bf16[256,128]{1,0:T(8,128)(2,1)S(1)} %add_convert_fusion.3), channel_id=1, source_target_pairs={{0,16},{1,17},{2,18},{3,19},{4,20},{5,21},{6,22},{7,23},{8,24},{9,... | collective-permute-start | bytes 196616 | tf_op jit(solution)/shard_map/ppermute | solution.py:1275
  43.5 5.4 %collective-permute-start.4 = (bf16[272,128]{1,0:T(8,128)(2,1)S(1)}, bf16[272,128]{1,0:T(8,128)(2,1)S(1)}, u32[]{:S(2)}, u32[]{:S(2)}) collective-permute-start(bf16[272,128]{1,0:T(8,128)(2,1)S(1)} %add_convert_fusion.1), channel_id=1, source_target_pairs={{0,16},{1,17},{2,18},{3,19},{4,20},{5,21},{6,22},{7,23},{8,24},{9,... | collective-permute-start | bytes 208904 | tf_op jit(solution)/shard_map/ppermute | solution.py:1275
  49.0 4.4 %collective-permute-start.5 = (bf16[272,128]{1,0:T(8,128)(2,1)S(1)}, bf16[272,128]{1,0:T(8,128)(2,1)S(1)}, u32[]{:S(2)}, u32[]{:S(2)}) collective-permute-start(bf16[272,128]{1,0:T(8,128)(2,1)S(1)} %add_convert_fusion), channel_id=1, source_target_pairs={{0,1},{1,0},{2,10},{3,11},{4,5},{5,4},{6,14},{7,15},{8,9},{9,8},{1... | collective-permute-start | bytes 208904 | tf_op jit(solution)/shard_map/ppermute | solution.py:1275
  50.6 4.7 %collective-permute-start.13 = (bf16[384,128]{1,0:T(8,128)(2,1)S(1)}, bf16[384,128]{1,0:T(8,128)(2,1)S(1)}, u32[]{:S(2)}, u32[]{:S(2)}) collective-permute-start(bf16[384,128]{1,0:T(8,128)(2,1)S(1)} %pad_maximum_fusion.7), channel_id=1, source_target_pairs={{0,1},{1,0},{2,10},{3,11},{4,5},{5,4},{6,14},{7,15},{8,9},{9,8},{1... | collective-permute-start | bytes 294920 | tf_op jit(solution)/shard_map/ppermute | solution.py:1275
  53.4 5.1 %collective-permute-start.6 = (bf16[544,128]{1,0:T(8,128)(2,1)S(1)}, bf16[544,128]{1,0:T(8,128)(2,1)S(1)}, u32[]{:S(2)}, u32[]{:S(2)}) collective-permute-start(bf16[544,128]{1,0:T(8,128)(2,1)S(1)} %pad_maximum_fusion.5), channel_id=1, source_target_pairs={{0,8},{1,9},{2,6},{3,7},{4,12},{5,13},{6,2},{7,3},{8,0},{9,1},{10,... | collective-permute-start | bytes 417800 | tf_op jit(solution)/shard_map/ppermute | solution.py:1275
  55.3 5.0 %collective-permute-start.14 = (bf16[512,128]{1,0:T(8,128)(2,1)S(1)}, bf16[512,128]{1,0:T(8,128)(2,1)S(1)}, u32[]{:S(2)}, u32[]{:S(2)}) collective-permute-start(bf16[512,128]{1,0:T(8,128)(2,1)S(1)} %pad_maximum_fusion.6), channel_id=1, source_target_pairs={{0,8},{1,9},{2,6},{3,7},{4,12},{5,13},{6,2},{7,3},{8,0},{9,1},{10,... | collective-permute-start | bytes 393224 | tf_op jit(solution)/shard_map/ppermute | solution.py:1275
  58.6 6.6 %collective-permute-start.7 = (bf16[1088,128]{1,0:T(8,128)(2,1)S(1)}, bf16[1088,128]{1,0:T(8,128)(2,1)S(1)}, u32[]{:S(2)}, u32[]{:S(2)}) collective-permute-start(bf16[1088,128]{1,0:T(8,128)(2,1)S(1)} %pad_maximum_fusion.3), channel_id=1, source_target_pairs={{0,4},{1,5},{2,3},{3,2},{4,0},{5,1},{6,7},{7,6},{8,12},{9,13},{10,... | collective-permute-start | bytes 835592 | tf_op jit(solution)/shard_map/ppermute | solution.py:1275
  60.4 8.0 %collective-permute-start.15 = (bf16[1152,128]{1,0:T(8,128)(2,1)S(1)}, bf16[1152,128]{1,0:T(8,128)(2,1)S(1)}, u32[]{:S(2)}, u32[]{:S(2)}) collective-permute-start(bf16[1152,128]{1,0:T(8,128)(2,1)S(1)} %pad_maximum_fusion.2), channel_id=1, source_target_pairs={{0,4},{1,5},{2,3},{3,2},{4,0},{5,1},{6,7},{7,6},{8,12},{9,13},{10,... | collective-permute-start | bytes 884744 | tf_op jit(solution)/shard_map/ppermute | solution.py:1275
  65.4 3.3 %collective-permute-start.8 = (bf16[2176,128]{1,0:T(8,128)(2,1)S(1)}, bf16[2176,128]{1,0:T(8,128)(2,1)S(1)}, u32[]{:S(2)}, u32[]{:S(2)}) collective-permute-start(bf16[2176,128]{1,0:T(8,128)(2,1)S(1)} %pad_maximum_fusion.mine_ref), channel_id=1, source_target_pairs={{0,2},{1,3},{2,0},{3,1},{4,6},{5,7},{6,4},{7,5},{8,10},{9,11},{10,... | collective-permute-start | bytes 1671176 | tf_op jit(solution)/shard_map/ppermute | solution.py:1275
  68.5 3.8 %collective-permute-start.16 = (bf16[2048,128]{1,0:T(8,128)(2,1)S(1)}, bf16[2048,128]{1,0:T(8,128)(2,1)S(1)}, u32[]{:S(2)}, u32[]{:S(2)}) collective-permute-start(bf16[2048,128]{1,0:T(8,128)(2,1)S(1)} %pad_maximum_fusion.1.mine_ref), channel_id=1, source_target_pairs={{0,2},{1,3},{2,0},{3,1},{4,6},{5,7},{6,4},{7,5},{8,10},{9,11},{10,... | collective-permute-start | bytes 1572872 | tf_op jit(solution)/shard_map/ppermute | solution.py:1275

commit v3 on v2

--- a/solution.py
+++ b/solution.py
@@ -278,8 +278,8 @@
     total,
     part_ref,
     w1_hbm,
-    w2_hbm,
-    xs,
+    w2_ref,
+    item_ref,
     ua_ref,
     slope_ref,
     w1_wide,
@@ -294,6 +294,7 @@
     conv_out_ref,
     bias_in_ref,
     bias_out_ref,
+    xs,
     xb,
     c2,
     act0,
@@ -309,6 +310,7 @@
     st1,
     tp0,
     tp1,
+    slopes,
     sems,
     sent,
 ):
@@ -332,11 +334,18 @@
     for copy in copies:
         copy.start()
     xs[...] = jnp.zeros_like(xs)
+    slopes[QUART:, :] = jnp.zeros((128 - QUART, LANES), f32)
     for ref in (act0, act1):
         ref[...] = jnp.zeros_like(ref)
-    for ref in (ys0, ys1, ys2, zs0, zs1):
-        ref[:, 0:NEAR, :] = jnp.zeros((ref.shape[0], NEAR, LANES), f32)
-        ref[:, NEAR + GRID :, :] = jnp.zeros((ref.shape[0], ref.shape[1] - NEAR - GRID, LANES), f32)
+    for refs, per_plane, ahead in (((ys0, ys1, ys2), 4, 3 * PMAX), ((zs0, zs1), 2, PMAX)):
+        for plane in range(12 // per_plane):
+            moved = per_plane * plane - 5
+            top = -moved * PMAX if moved < 0 else 0
+            bottom = ahead + (2 * moved if moved < 0 else moved * PMAX)
+            for ref in refs:
+                if top:
+                    ref[plane, NEAR - top : NEAR, :] = jnp.zeros((top, LANES), f32)
+                ref[plane, NEAR + GRID : NEAR + GRID + bottom, :] = jnp.zeros((bottom, LANES), f32)
     source = lax.broadcasted_iota(jnp.int32, (2 * LANES, LANES), 0)
     target = lax.broadcasted_iota(jnp.int32, (2 * LANES, LANES), 1)
     wanted = (target // 32) * 64 + side * 32 + target % 32
@@ -417,10 +426,14 @@
             hidden = value * (1.0 / 6.0) + bias_in
             active, slope = gelu_both(hidden)
             position = row_of(rows) + r + QUART * (lane_of(rows) // 32)
-            slope_ref[k, r : r + rows, :] = jnp.where(position < used, slope, 0.0)
+            slopes[r : r + rows, :] = jnp.where(position < used, slope, 0.0)
             temp[r : r + rows, :] = jnp.where(position < used, active, 0.0)
 
+        def keep_slope():
+            slope_ref[k] = slopes[...].astype(bf16)
+
         pieces += pack_pieces(load, store, temp)
+        pieces.append(keep_slope)
         pieces += spread_pieces(lambda r, rows: temp[r : r + rows, :], act, lambda q: 16 - q)
         for t in range(0, GRID, STEP):
 
@@ -529,7 +542,7 @@
     together(first_product(0), combining[:6])
     together(first_product(1), combining[6:], unfold(2))
     together(choose_half(), activate(0))
-    leave(w2_wide.at[:, pl.ds(0, WIDE)], w2_hbm)
+    w2_ref[...] = w2_wide[:, 0:WIDE]
     together(first_product(2), activate(1), unfold(3))
     together(second_product(0), activate(2))
     together(first_product(3), finish(0), unfold(4))
@@ -541,6 +554,7 @@
     together(finish(4))
 
     send_ref[0:FOLD, :] = total[...].astype(bf16)
+    item_ref[...] = xs[16 : 16 + PAIR, :].astype(bf16)
     send_ref[FOLD:, :] = jnp.concatenate(
         [flat_pairs(cot_ref, HALF // 2), jnp.zeros((4, LANES), f32)], axis=0
     ).astype(bf16)
@@ -555,10 +569,10 @@
     cot_ref,
     recv_ref,
     own_ref,
-    xs,
+    item_ref,
     part_ref,
     w1_hbm,
-    w2_hbm,
+    w2_ref,
     ua_ref,
     slope_ref,
     gain_ref,
@@ -588,17 +602,16 @@
     tp1,
     dw,
     packed,
-    w2_ref,
+    slopes,
+    item,
     out_ref,
-    sems,
+    sem,
     out_sem,
 ):
-    coming = [
-        pltpu.make_async_copy(w2_hbm, w2_ref, sems.at[0]),
-        pltpu.make_async_copy(w1_hbm, w1_ref, sems.at[1]),
-    ]
-    for copy in coming:
-        copy.start()
+    coming = pltpu.make_async_copy(w1_hbm, w1_ref, sem)
+    coming.start()
+    slopes[...] = slope_ref[...].astype(f32)
+    item[...] = item_ref[...].astype(f32)
     side = where_ref[0]
     core = where_ref[1]
     mixing = mixing_of(amp_ref[...])
@@ -631,7 +644,7 @@
 
     for t in range(0, PAIR, 56):
         rows = slice(t, t + 56)
-        total = xs[16 + t : 16 + t + 56, :] + other[rows, :]
+        total = item[rows, :] + other[rows, :]
         centred = total - jnp.mean(total, axis=-1, keepdims=True)
         variance = jnp.mean(centred * centred, axis=-1, keepdims=True)
         inverse = lax.rsqrt(variance + epsilon)
@@ -723,19 +736,18 @@
             return quarter_select([vs[pl.ds(8 + r - q, rows), :] for q in range(4)], rows)
 
         def store(r, rows, value):
-            grad_ref[k, r : r + rows, :] = value * slope_ref[k, r : r + rows, :] * (1.0 / 6.0)
+            grad_ref[k, r : r + rows, :] = value * slopes[k, r : r + rows, :] * (1.0 / 6.0)
 
         return pieces + pack_pieces(load, store, temp)
 
     together(unfold(0))
-    coming[0].wait()
     for k in range(K):
         streams = [back(k)]
         if k + 1 < K:
             streams.append(unfold(k + 1))
         together(*streams)
         together(weigh(k), fold(k))
-    coming[1].wait()
+    coming.wait()
     leaving.wait()
     bias = None
     for k in range(K):
@@ -790,11 +802,12 @@
     periods_ref,
     grad_ref,
     small_ref,
-    xs,
+    item_ref,
     keep_ref,
     send_ref,
     hr0,
     hr1,
+    xs,
     xb,
     gh0,
     gh1,
@@ -806,6 +819,9 @@
     core = where_ref[1]
     for ref in (hr0, hr1):
         ref[...] = jnp.zeros_like(ref)
+    xs[0:16, :] = jnp.zeros((16, LANES), f32)
+    xs[16 : 16 + PAIR, :] = item_ref[...].astype(f32)
+    xs[16 + PAIR :, :] = jnp.zeros((512 - 16 - PAIR, LANES), f32)
     shift_columns(xs, xb)
 
     def unfold(k):
@@ -1215,13 +1231,13 @@
             pltpu.VMEM((FOLD, LANES), f32),
             pltpu.VMEM((K, FOLD, LANES), f32),
             pltpu.HBM((WIDE, FULL), bf16),
-            pltpu.HBM((FULL, WIDE), bf16),
-            pltpu.VMEM((512, LANES), f32),
+            pltpu.VMEM((FULL, WIDE), bf16),
+            pltpu.VMEM((PAIR, LANES), bf16),
             pltpu.VMEM((K, GRID, WIDE), bf16),
-            pltpu.VMEM((K, QUART, LANES), f32),
+            pltpu.VMEM((K, 128, LANES), bf16),
         ),
         in_specs=[smem] + [hbm] * 8,
-        out_specs=[vmem, vmem, vmem, hbm, hbm, vmem, vmem, vmem],
+        out_specs=[vmem, vmem, vmem, hbm, vmem, vmem, vmem, vmem],
         scratch_shapes=[
             pltpu.VMEM((WIDE + LANES, FULL), bf16),
             pltpu.VMEM((FULL, WIDE + LANES), bf16),
@@ -1235,6 +1251,7 @@
             pltpu.VMEM((64, TAPS * D), bf16),
             pltpu.VMEM((1, FF), f32),
             pltpu.VMEM((1, D), f32),
+            pltpu.VMEM((512, LANES), f32),
             pltpu.VMEM((6, GRID, LANES), bf16),
             pltpu.VMEM((FULL, FULL), bf16),
             *two(512, LANES),
@@ -1244,8 +1261,9 @@
             *two(GRID + 3 * PMAX, LANES),
             *two(GRID + PMAX, LANES),
             *two(2 * QUART, LANES),
+            pltpu.VMEM((128, LANES), f32),
             pltpu.SemaphoreType.DMA((12,)),
-            pltpu.SemaphoreType.DMA((2,)),
+            pltpu.SemaphoreType.DMA((1,)),
         ],
         compiler_params=limit(28),
         cost_estimate=cost(1 << 33),
@@ -1290,7 +1308,7 @@
             pltpu.VMEM((8, LANES), f32),
             pltpu.VMEM((WIDE, FULL), bf16),
         ),
-        in_specs=[smem, smem] + [vmem] * 6 + [hbm] * 2 + [vmem] * 4,
+        in_specs=[smem, smem] + [vmem] * 6 + [hbm] + [vmem] * 5,
         out_specs=[hbm] + [vmem] * 7,
         scratch_shapes=[
             pltpu.VMEM((PAIR, LANES), f32),
@@ -1305,9 +1323,10 @@
             *two(2 * QUART, LANES),
             pltpu.VMEM((WIDE, FULL), f32),
             pltpu.VMEM((2 * half_out, LANES), bf16),
-            pltpu.VMEM((FULL, WIDE), bf16),
+            pltpu.VMEM((K, 128, LANES), f32),
+            pltpu.VMEM((PAIR, LANES), f32),
             pltpu.VMEM((1, HALF * D), bf16),
-            pltpu.SemaphoreType.DMA((2,)),
+            pltpu.SemaphoreType.DMA,
             pltpu.SemaphoreType.DMA,
         ],
         compiler_params=limit(16),
@@ -1319,8 +1338,8 @@
         amplitudes,
         cotangent,
         *stay([recv, total, xs, part]),
-        *far([w1, w2]),
-        *stay([ua, slope]),
+        *far([w1]),
+        *stay([w2, ua, slope]),
         norm_gain[None, :],
         norm_bias[None, :],
     )
@@ -1335,6 +1354,7 @@
         out_specs=[vmem] * 2,
         scratch_shapes=[
             *two(3 * PMAX + GRID + NEAR, LANES),
+            pltpu.VMEM((512, LANES), f32),
             pltpu.VMEM((6, GRID, LANES), bf16),
             *two(GRID, WIDE, bf16),
             *two(GRID, FULL, bf16),

time: 75.1 us -> 74.9 us (level)
  transfers between devices with their start and end apart: 17 -> 17, of which waited for: 11 -> 12; matrix products, arithmetic and copies ran while one was open for 1% -> 1% of each run, Pallas kernels for 14% -> 14%
where the time goes in v3:
time: 74.9 us; the launch traced here: 74.8 us
  Pallas kernels  34.2 us (46%)
  starting transfers between devices  23.7 us (32%)
  waiting for transfers between devices  14.8 us (20%)
  between operations  1.13 us (2%)
  other arithmetic  0.86 us (1%)
    ppermute x17, starting transfers between devices, exchange(): return lax.ppermute(value, ('items', 'narrow'), pairs)  23.7 us
    ppermute x17, waiting for transfers between devices, exchange(): return lax.ppermute(value, ('items', 'narrow'), pairs)  14.8 us
    pallas_call x1, Pallas kernels, on_device(): pl.pallas_call(forward_kernel, out_shape=(pltpu.VMEM((FOLD + 112, LANES),...  10.3 us
    pallas_call x1, Pallas kernels, on_device(): pl.pallas_call(outer_kernel, out_shape=(shape((1, HALF * D), bf16), pltpu...  6.85 us
    pallas_call x1, Pallas kernels, on_device(): pl.pallas_call(inner_kernel, out_shape=(pltpu.VMEM((HALF_IN, LANES), bf16...  3.92 us
    pallas_call x1, Pallas kernels, on_device(): pl.pallas_call(functools.partial(second_last_kernel, plan_out, plan_in),...  3.59 us
    pallas_call x1, Pallas kernels, series_begin(): pl.pallas_call(series_kernel, out_shape=pltpu.VMEM((GRID, LANES), f32), i...  2.52 us
    pallas_call x1, Pallas kernels, on_device(): pl.pallas_call(functools.partial(first_last_kernel, plan_out), out_shape=...  2.48 us
  transfers between devices with their start and end apart: 17, of which 12 were waited for; matrix products, arithmetic and copies ran while one was open for 1% of the time, Pallas kernels for 14%

profile of v3, /device:TPU:0, one launch (start us, length us, event | category | flops | bytes accessed | tf_op | source)
XLA Modules:
  0.0 74.8 jit_solution(15922121850897256917)
XLA Ops:
  0.8 10.3 %forward.1 = (bf16[336,128]{1,0:T(8,128)(2,1)S(1)}, f32[224,128]{1,0:T(8,128)S(1)}, f32[5,224,128]{2,1,0:T(8,128)S(1)}, bf16[384,768]{1,0:T(8,128)(2,1)}, bf16[7...) custom-call(s32[2]{0:T(128)S(1)} %pad_add_fusion.where_ref, ...), custom_call_target="tpu_custom_call" | custom-call | flops 8589934592 | bytes 4194304 | tf_op jit(solution)/shard_map/forward/pallas_call | solution.py:1227
  11.1 3.0 %collective-permute-start = (bf16[336,128]{1,0:T(8,128)(2,1)S(1)}, bf16[336,128]{1,0:T(8,128)(2,1)S(1)}, u32[]{:S(2)}, u32[]{:S(2)}) collective-permute-start(bf16[336,128]{1,0:T(8,128)(2,1)S(1)} %get-tuple-element.43), channel_id=1, source_target_pairs={{0,1},{1,0},{2,3},{3,2},{4,5},{5,4},{6,7},{7,6},{8,9},{9,8},{10,11... | collective-permute-start | bytes 258056 | tf_op jit(solution)/shard_map/ppermute | solution.py:1293
  14.1 2.5 %collective-permute-done.recv_ref = bf16[336,128]{1,0:T(8,128)(2,1)S(1)} collective-permute-done((bf16[336,128]{1,0:T(8,128)(2,1)S(1)}, bf16[336,128]{1,0:T(8,128)(2,1)S(1)}, u32[]{:S(2)}, u32[]{:S(2)}) %collective-permute-start) | collective-permute-done | bytes 86048 | tf_op jit(solution)/shard_map/ppermute | solution.py:1293
  16.6 6.9 %outer.1 = (bf16[1,13824]{1,0:T(2,128)(2,1)}, bf16[1088,128]{1,0:T(8,128)(2,1)S(1)}, bf16[1088,128]{1,0:T(8,128)(2,1)S(1)}, f32[5,120,128]{2,1,0:T(8,128)S(1)}, ...) custom-call(s32[2]{0:T(128)S(1)} %pad_add_fusion.where_ref, ...), custom_call_target="tpu_custom_call" | custom-call | flops 8589934592 | bytes 4194304 | tf_op jit(solution)/shard_map/outer/pallas_call | solution.py:1299
  23.5 3.9 %inner.1 = (bf16[1024,128]{1,0:T(8,128)(2,1)S(1)}, bf16[1024,128]{1,0:T(8,128)(2,1)S(1)}) custom-call(s32[2]{0:T(128)S(1)} %pad_add_fusion.where_ref, s32[1,5]{1,0:T(1,128)S(1)} %copy-done.3, f32[5,120,128]{2,1,0:T(8,128)S(1)} %get-tuple-element.61.grad_ref, f32[8,128]{1,0:T(8,128)S(1)} %get-tuple-element.55.small_ref, ...), custom_call_target="tpu_custom_call" | custom-call | flops 8589934592 | bytes 4194304 | tf_op jit(solution)/shard_map/inner/pallas_call | solution.py:1347
  29.1 1.9 %collective-permute-start.10 = (bf16[512,128]{1,0:T(8,128)(2,1)S(1)}, bf16[512,128]{1,0:T(8,128)(2,1)S(1)}, u32[]{:S(2)}, u32[]{:S(2)}) collective-permute-start(bf16[512,128]{1,0:T(8,128)(2,1)S(1)} %dynamic-slice_convert_fusion.1), channel_id=1, source_target_pairs={{0,4},{1,5},{2,10},{3,11},{4,0},{5,1},{6,14},{7,15},{8,12},{9,13},... | collective-permute-start | bytes 393224 | tf_op jit(solution)/shard_map/ppermute | solution.py:1293
  31.1 2.5 %series.1.begun_ref = f32[480,128]{1,0:T(8,128)S(1)} custom-call(s32[1,5]{1,0:T(1,128)S(1)} %copy-done.3, f32[5,120,128]{2,1,0:T(8,128)S(1)} %get-tuple-element.61.grad_ref, bf16[384,768]{1,0:T(8,128)(2,1)S(1)} %get-tuple-element.64.w1_ref), custom_call_target="tpu_custom_call" | custom-call | flops 2147483648 | bytes 4194304 | tf_op jit(solution)/shard_map/series/pallas_call | solution.py:1376
  34.2 2.1 %collective-permute-start.11 = (bf16[256,128]{1,0:T(8,128)(2,1)S(1)}, bf16[256,128]{1,0:T(8,128)(2,1)S(1)}, u32[]{:S(2)}, u32[]{:S(2)}) collective-permute-start(bf16[256,128]{1,0:T(8,128)(2,1)S(1)} %dynamic-slice_convert_fusion.3), channel_id=1, source_target_pairs={{0,8},{1,9},{2,6},{3,7},{4,12},{5,13},{6,2},{7,3},{8,0},{9,1},{10,... | collective-permute-start | bytes 196616 | tf_op jit(solution)/shard_map/ppermute | solution.py:1293
  36.3 2.1 %series_rest.1 = (f32[108,128]{1,0:T(8,128)S(1)}, bf16[128,128]{1,0:T(8,128)(2,1)S(1)}, f32[8,128]{1,0:T(8,128)S(1)}) custom-call(s32[2]{0:T(128)S(1)} %pad_add_fusion.where_ref, s32[1,5]{1,0:T(1,128)S(1)} %copy-done.3, f32[5,120,128]{2,1,0:T(8,128)S(1)} %get-tuple-element.61.grad_ref, f32[448,128]{1,0:T(8,128)S(1)} %get-tuple-element.62.merged_ref, ...), custom_call_target="tpu_custom_call" | custom-call | flops 2147483648 | bytes 4194304 | tf_op jit(solution)/shard_map/series_rest/pallas_call | solution.py:1388
  38.9 1.7 %collective-permute-start.3 = (bf16[272,128]{1,0:T(8,128)(2,1)S(1)}, bf16[272,128]{1,0:T(8,128)(2,1)S(1)}, u32[]{:S(2)}, u32[]{:S(2)}) collective-permute-start(bf16[272,128]{1,0:T(8,128)(2,1)S(1)} %dynamic-slice_convert_fusion.2), channel_id=1, source_target_pairs={{0,8},{1,9},{2,6},{3,7},{4,12},{5,13},{6,2},{7,3},{8,0},{9,1},{10,... | collective-permute-start | bytes 208904 | tf_op jit(solution)/shard_map/ppermute | solution.py:1293
  40.6 2.6 %collective-permute-start.12 = (bf16[256,128]{1,0:T(8,128)(2,1)S(1)}, bf16[256,128]{1,0:T(8,128)(2,1)S(1)}, u32[]{:S(2)}, u32[]{:S(2)}) collective-permute-start(bf16[256,128]{1,0:T(8,128)(2,1)S(1)} %add_convert_fusion.3), channel_id=1, source_target_pairs={{0,16},{1,17},{2,18},{3,19},{4,20},{5,21},{6,22},{7,23},{8,24},{9,... | collective-permute-start | bytes 196616 | tf_op jit(solution)/shard_map/ppermute | solution.py:1293
  43.3 2.6 %collective-permute-start.4 = (bf16[272,128]{1,0:T(8,128)(2,1)S(1)}, bf16[272,128]{1,0:T(8,128)(2,1)S(1)}, u32[]{:S(2)}, u32[]{:S(2)}) collective-permute-start(bf16[272,128]{1,0:T(8,128)(2,1)S(1)} %add_convert_fusion.1), channel_id=1, source_target_pairs={{0,16},{1,17},{2,18},{3,19},{4,20},{5,21},{6,22},{7,23},{8,24},{9,... | collective-permute-start | bytes 208904 | tf_op jit(solution)/shard_map/ppermute | solution.py:1293
  45.9 2.0 %collective-permute-done.12 = bf16[256,128]{1,0:T(8,128)(2,1)S(1)} collective-permute-done((bf16[256,128]{1,0:T(8,128)(2,1)S(1)}, bf16[256,128]{1,0:T(8,128)(2,1)S(1)}, u32[]{:S(2)}, u32[]{:S(2)}) %collective-permute-start.12) | collective-permute-done | bytes 65568 | tf_op jit(solution)/shard_map/ppermute | solution.py:1293
  48.8 1.6 %collective-permute-start.5 = (bf16[272,128]{1,0:T(8,128)(2,1)S(1)}, bf16[272,128]{1,0:T(8,128)(2,1)S(1)}, u32[]{:S(2)}, u32[]{:S(2)}) collective-permute-start(bf16[272,128]{1,0:T(8,128)(2,1)S(1)} %add_convert_fusion), channel_id=1, source_target_pairs={{0,1},{1,0},{2,10},{3,11},{4,5},{5,4},{6,14},{7,15},{8,9},{9,8},{1... | collective-permute-start | bytes 208904 | tf_op jit(solution)/shard_map/ppermute | solution.py:1293
  51.0 2.2 %collective-permute-done.5 = bf16[272,128]{1,0:T(8,128)(2,1)S(1)} collective-permute-done((bf16[272,128]{1,0:T(8,128)(2,1)S(1)}, bf16[272,128]{1,0:T(8,128)(2,1)S(1)}, u32[]{:S(2)}, u32[]{:S(2)}) %collective-permute-start.5) | collective-permute-done | bytes 69664 | tf_op jit(solution)/shard_map/ppermute | solution.py:1293
  53.2 1.9 %collective-permute-start.6 = (bf16[544,128]{1,0:T(8,128)(2,1)S(1)}, bf16[544,128]{1,0:T(8,128)(2,1)S(1)}, u32[]{:S(2)}, u32[]{:S(2)}) collective-permute-start(bf16[544,128]{1,0:T(8,128)(2,1)S(1)} %pad_maximum_fusion.5), channel_id=1, source_target_pairs={{0,8},{1,9},{2,6},{3,7},{4,12},{5,13},{6,2},{7,3},{8,0},{9,1},{10,... | collective-permute-start | bytes 417800 | tf_op jit(solution)/shard_map/ppermute | solution.py:1293
  55.2 1.9 %collective-permute-start.14 = (bf16[512,128]{1,0:T(8,128)(2,1)S(1)}, bf16[512,128]{1,0:T(8,128)(2,1)S(1)}, u32[]{:S(2)}, u32[]{:S(2)}) collective-permute-start(bf16[512,128]{1,0:T(8,128)(2,1)S(1)} %pad_maximum_fusion.6), channel_id=1, source_target_pairs={{0,8},{1,9},{2,6},{3,7},{4,12},{5,13},{6,2},{7,3},{8,0},{9,1},{10,... | collective-permute-start | bytes 393224 | tf_op jit(solution)/shard_map/ppermute | solution.py:1293
  57.0 1.3 %collective-permute-done.6 = bf16[544,128]{1,0:T(8,128)(2,1)S(1)} collective-permute-done((bf16[544,128]{1,0:T(8,128)(2,1)S(1)}, bf16[544,128]{1,0:T(8,128)(2,1)S(1)}, u32[]{:S(2)}, u32[]{:S(2)}) %collective-permute-start.6) | collective-permute-done | bytes 139296 | tf_op jit(solution)/shard_map/ppermute | solution.py:1293
  58.4 1.4 %collective-permute-start.7 = (bf16[1088,128]{1,0:T(8,128)(2,1)S(1)}, bf16[1088,128]{1,0:T(8,128)(2,1)S(1)}, u32[]{:S(2)}, u32[]{:S(2)}) collective-permute-start(bf16[1088,128]{1,0:T(8,128)(2,1)S(1)} %pad_maximum_fusion.3), channel_id=1, source_target_pairs={{0,4},{1,5},{2,3},{3,2},{4,0},{5,1},{6,7},{7,6},{8,12},{9,13},{10,... | collective-permute-start | bytes 835592 | tf_op jit(solution)/shard_map/ppermute | solution.py:1293
  60.3 1.4 %collective-permute-start.15 = (bf16[1152,128]{1,0:T(8,128)(2,1)S(1)}, bf16[1152,128]{1,0:T(8,128)(2,1)S(1)}, u32[]{:S(2)}, u32[]{:S(2)}) collective-permute-start(bf16[1152,128]{1,0:T(8,128)(2,1)S(1)} %pad_maximum_fusion.2), channel_id=1, source_target_pairs={{0,4},{1,5},{2,3},{3,2},{4,0},{5,1},{6,7},{7,6},{8,12},{9,13},{10,... | collective-permute-start | bytes 884744 | tf_op jit(solution)/shard_map/ppermute | solution.py:1293
  61.6 3.4 %collective-permute-done.7 = bf16[1088,128]{1,0:T(8,128)(2,1)S(1)} collective-permute-done((bf16[1088,128]{1,0:T(8,128)(2,1)S(1)}, bf16[1088,128]{1,0:T(8,128)(2,1)S(1)}, u32[]{:S(2)}, u32[]{:S(2)}) %collective-permute-start.7) | collective-permute-done | bytes 278560 | tf_op jit(solution)/shard_map/ppermute | solution.py:1293
  65.3 2.5 %first_last.1.begun_hbm = f32[64,18304]{1,0:T(8,128)} custom-call(s32[2]{0:T(128)S(1)} %pad_add_fusion.where_ref, bf16[2176,128]{1,0:T(8,128)(2,1)S(1)} %pad_maximum_fusion.mine_ref), custom_call_target="tpu_custom_call" | custom-call | flops 2147483648 | bytes 4194304 | tf_op jit(solution)/shard_map/first_last/pallas_call | solution.py:1507
  68.5 3.6 %second_last.1 = (f32[64,18304]{1,0:T(8,128)}, f32[64,18304]{1,0:T(8,128)}, f32[1,13824]{1,0:T(1,128)}, f32[1,5]{1,0:T(1,128)}) custom-call(s32[2]{0:T(128)S(1)} %pad_add_fusion.where_ref, f32[1,5]{1,0:T(1,128)S(1)} %copy-done.4, bf16[2176,128]{1,0:T(8,128)(2,1)S(1)} %collective-permute-done.8.theirs_ref, ...), custom_call_target="tpu_custom_call", output_to_operand_aliasing={{0}: (7, {})} | custom-call | flops 4294967296 | bytes 4194304 | tf_op jit(solution)/shard_map/second_last/pallas_call | solution.py:1517
  72.1 2.5 %third_last.1 = (f32[64,18304]{1,0:T(8,128)}, f32[1,64]{1,0:T(1,128)}, f32[1,64]{1,0:T(1,128)}, f32[1,64]{1,0:T(1,128)}, f32[1,64]{1,0:T(1,128)}) custom-call(s32[2]{0:T(128)S(1)} %pad_add_fusion.where_ref, bf16[2048,128]{1,0:T(8,128)(2,1)S(1)} %pad_maximum_fusion.1.mine_ref, ...), custom_call_target="tpu_custom_call", output_to_operand_aliasing={{0}: (3, {})} | custom-call | flops 2147483648 | bytes 4194304 | tf_op jit(solution)/shard_map/third_last/pallas_call | solution.py:1539
  (55 shorter events, 5.9 us)
Async XLA Ops:
  0.7 15.9 %copy-start = (bf16[1,13824]{1,0:T(2,128)(2,1)S(1)}, bf16[1,13824]{1,0:T(2,128)(2,1)}, u32[]{:S(2)}) copy-start(bf16[1,13824]{1,0:T(2,128)(2,1)} %cot_ref.1) | copy-start | bytes 82948
  0.7 15.9 %copy-start.1 = (f32[64]{0:T(128)S(1)}, f32[64]{0:T(128)}, u32[]{:S(2)}) copy-start(f32[64]{0:T(128)} %param.17) | copy-start | bytes 772
  0.7 15.9 %copy-start.2 = (f32[64]{0:T(128)S(1)}, f32[64]{0:T(128)}, u32[]{:S(2)}) copy-start(f32[64]{0:T(128)} %param.18) | copy-start | bytes 772
  0.7 15.9 %copy-start.3 = (s32[1,5]{1,0:T(1,128)S(1)}, s32[1,5]{1,0:T(1,128)}, u32[]{:S(2)}) copy-start(s32[1,5]{1,0:T(1,128)} %periods_ref.7) | copy-start | bytes 64
  0.7 15.9 %copy-start.4 = (f32[1,5]{1,0:T(1,128)S(1)}, f32[1,5]{1,0:T(1,128)}, u32[]{:S(2)}) copy-start(f32[1,5]{1,0:T(1,128)} %amp_ref.3) | copy-start | bytes 64
  11.1 5.5 %collective-permute-start = (bf16[336,128]{1,0:T(8,128)(2,1)S(1)}, bf16[336,128]{1,0:T(8,128)(2,1)S(1)}, u32[]{:S(2)}, u32[]{:S(2)}) collective-permute-start(bf16[336,128]{1,0:T(8,128)(2,1)S(1)} %get-tuple-element.43), channel_id=1, source_target_pairs={{0,1},{1,0},{2,3},{3,2},{4,5},{5,4},{6,7},{7,6},{8,9},{9,8},{10,11... | collective-permute-start | bytes 258056 | tf_op jit(solution)/shard_map/ppermute | solution.py:1293
  27.4 1.6 %collective-permute-start.9 = (bf16[1024,128]{1,0:T(8,128)(2,1)S(1)}, bf16[1024,128]{1,0:T(8,128)(2,1)S(1)}, u32[]{:S(2)}, u32[]{:S(2)}) collective-permute-start(bf16[1024,128]{1,0:T(8,128)(2,1)S(1)} %get-tuple-element.57), channel_id=1, source_target_pairs={{0,2},{1,3},{2,0},{3,1},{4,6},{5,7},{6,4},{7,5},{8,10},{9,11},{10,... | collective-permute-start | bytes 786440 | tf_op jit(solution)/shard_map/ppermute | solution.py:1293
  27.6 6.0 %collective-permute-start.1 = (bf16[1088,128]{1,0:T(8,128)(2,1)S(1)}, bf16[1088,128]{1,0:T(8,128)(2,1)S(1)}, u32[]{:S(2)}, u32[]{:S(2)}) collective-permute-start(bf16[1088,128]{1,0:T(8,128)(2,1)S(1)} %get-tuple-element.53), channel_id=1, source_target_pairs={{0,2},{1,3},{2,0},{3,1},{4,6},{5,7},{6,4},{7,5},{8,10},{9,11},{10,... | collective-permute-start | bytes 835592 | tf_op jit(solution)/shard_map/ppermute | solution.py:1293
  29.1 5.0 %collective-permute-start.10 = (bf16[512,128]{1,0:T(8,128)(2,1)S(1)}, bf16[512,128]{1,0:T(8,128)(2,1)S(1)}, u32[]{:S(2)}, u32[]{:S(2)}) collective-permute-start(bf16[512,128]{1,0:T(8,128)(2,1)S(1)} %dynamic-slice_convert_fusion.1), channel_id=1, source_target_pairs={{0,4},{1,5},{2,10},{3,11},{4,0},{5,1},{6,14},{7,15},{8,12},{9,13},... | collective-permute-start | bytes 393224 | tf_op jit(solution)/shard_map/ppermute | solution.py:1293
  33.7 5.1 %collective-permute-start.2 = (bf16[544,128]{1,0:T(8,128)(2,1)S(1)}, bf16[544,128]{1,0:T(8,128)(2,1)S(1)}, u32[]{:S(2)}, u32[]{:S(2)}) collective-permute-start(bf16[544,128]{1,0:T(8,128)(2,1)S(1)} %dynamic-slice_convert_fusion), channel_id=1, source_target_pairs={{0,4},{1,5},{2,10},{3,11},{4,0},{5,1},{6,14},{7,15},{8,12},{9,13},... | collective-permute-start | bytes 417800 | tf_op jit(solution)/shard_map/ppermute | solution.py:1293
  34.2 6.4 %collective-permute-start.11 = (bf16[256,128]{1,0:T(8,128)(2,1)S(1)}, bf16[256,128]{1,0:T(8,128)(2,1)S(1)}, u32[]{:S(2)}, u32[]{:S(2)}) collective-permute-start(bf16[256,128]{1,0:T(8,128)(2,1)S(1)} %dynamic-slice_convert_fusion.3), channel_id=1, source_target_pairs={{0,8},{1,9},{2,6},{3,7},{4,12},{5,13},{6,2},{7,3},{8,0},{9,1},{10,... | collective-permute-start | bytes 196616 | tf_op jit(solution)/shard_map/ppermute | solution.py:1293
  38.9 4.4 %collective-permute-start.3 = (bf16[272,128]{1,0:T(8,128)(2,1)S(1)}, bf16[272,128]{1,0:T(8,128)(2,1)S(1)}, u32[]{:S(2)}, u32[]{:S(2)}) collective-permute-start(bf16[272,128]{1,0:T(8,128)(2,1)S(1)} %dynamic-slice_convert_fusion.2), channel_id=1, source_target_pairs={{0,8},{1,9},{2,6},{3,7},{4,12},{5,13},{6,2},{7,3},{8,0},{9,1},{10,... | collective-permute-start | bytes 208904 | tf_op jit(solution)/shard_map/ppermute | solution.py:1293
  40.6 7.3 %collective-permute-start.12 = (bf16[256,128]{1,0:T(8,128)(2,1)S(1)}, bf16[256,128]{1,0:T(8,128)(2,1)S(1)}, u32[]{:S(2)}, u32[]{:S(2)}) collective-permute-start(bf16[256,128]{1,0:T(8,128)(2,1)S(1)} %add_convert_fusion.3), channel_id=1, source_target_pairs={{0,16},{1,17},{2,18},{3,19},{4,20},{5,21},{6,22},{7,23},{8,24},{9,... | collective-permute-start | bytes 196616 | tf_op jit(solution)/shard_map/ppermute | solution.py:1293
  43.3 5.4 %collective-permute-start.4 = (bf16[272,128]{1,0:T(8,128)(2,1)S(1)}, bf16[272,128]{1,0:T(8,128)(2,1)S(1)}, u32[]{:S(2)}, u32[]{:S(2)}) collective-permute-start(bf16[272,128]{1,0:T(8,128)(2,1)S(1)} %add_convert_fusion.1), channel_id=1, source_target_pairs={{0,16},{1,17},{2,18},{3,19},{4,20},{5,21},{6,22},{7,23},{8,24},{9,... | collective-permute-start | bytes 208904 | tf_op jit(solution)/shard_map/ppermute | solution.py:1293
  48.8 4.4 %collective-permute-start.5 = (bf16[272,128]{1,0:T(8,128)(2,1)S(1)}, bf16[272,128]{1,0:T(8,128)(2,1)S(1)}, u32[]{:S(2)}, u32[]{:S(2)}) collective-permute-start(bf16[272,128]{1,0:T(8,128)(2,1)S(1)} %add_convert_fusion), channel_id=1, source_target_pairs={{0,1},{1,0},{2,10},{3,11},{4,5},{5,4},{6,14},{7,15},{8,9},{9,8},{1... | collective-permute-start | bytes 208904 | tf_op jit(solution)/shard_map/ppermute | solution.py:1293
  50.4 4.7 %collective-permute-start.13 = (bf16[384,128]{1,0:T(8,128)(2,1)S(1)}, bf16[384,128]{1,0:T(8,128)(2,1)S(1)}, u32[]{:S(2)}, u32[]{:S(2)}) collective-permute-start(bf16[384,128]{1,0:T(8,128)(2,1)S(1)} %pad_maximum_fusion.7), channel_id=1, source_target_pairs={{0,1},{1,0},{2,10},{3,11},{4,5},{5,4},{6,14},{7,15},{8,9},{9,8},{1... | collective-permute-start | bytes 294920 | tf_op jit(solution)/shard_map/ppermute | solution.py:1293
  53.2 5.1 %collective-permute-start.6 = (bf16[544,128]{1,0:T(8,128)(2,1)S(1)}, bf16[544,128]{1,0:T(8,128)(2,1)S(1)}, u32[]{:S(2)}, u32[]{:S(2)}) collective-permute-start(bf16[544,128]{1,0:T(8,128)(2,1)S(1)} %pad_maximum_fusion.5), channel_id=1, source_target_pairs={{0,8},{1,9},{2,6},{3,7},{4,12},{5,13},{6,2},{7,3},{8,0},{9,1},{10,... | collective-permute-start | bytes 417800 | tf_op jit(solution)/shard_map/ppermute | solution.py:1293
  55.2 5.0 %collective-permute-start.14 = (bf16[512,128]{1,0:T(8,128)(2,1)S(1)}, bf16[512,128]{1,0:T(8,128)(2,1)S(1)}, u32[]{:S(2)}, u32[]{:S(2)}) collective-permute-start(bf16[512,128]{1,0:T(8,128)(2,1)S(1)} %pad_maximum_fusion.6), channel_id=1, source_target_pairs={{0,8},{1,9},{2,6},{3,7},{4,12},{5,13},{6,2},{7,3},{8,0},{9,1},{10,... | collective-permute-start | bytes 393224 | tf_op jit(solution)/shard_map/ppermute | solution.py:1293
  58.4 6.6 %collective-permute-start.7 = (bf16[1088,128]{1,0:T(8,128)(2,1)S(1)}, bf16[1088,128]{1,0:T(8,128)(2,1)S(1)}, u32[]{:S(2)}, u32[]{:S(2)}) collective-permute-start(bf16[1088,128]{1,0:T(8,128)(2,1)S(1)} %pad_maximum_fusion.3), channel_id=1, source_target_pairs={{0,4},{1,5},{2,3},{3,2},{4,0},{5,1},{6,7},{7,6},{8,12},{9,13},{10,... | collective-permute-start | bytes 835592 | tf_op jit(solution)/shard_map/ppermute | solution.py:1293
  60.3 7.9 %collective-permute-start.15 = (bf16[1152,128]{1,0:T(8,128)(2,1)S(1)}, bf16[1152,128]{1,0:T(8,128)(2,1)S(1)}, u32[]{:S(2)}, u32[]{:S(2)}) collective-permute-start(bf16[1152,128]{1,0:T(8,128)(2,1)S(1)} %pad_maximum_fusion.2), channel_id=1, source_target_pairs={{0,4},{1,5},{2,3},{3,2},{4,0},{5,1},{6,7},{7,6},{8,12},{9,13},{10,... | collective-permute-start | bytes 884744 | tf_op jit(solution)/shard_map/ppermute | solution.py:1293
  65.2 3.3 %collective-permute-start.8 = (bf16[2176,128]{1,0:T(8,128)(2,1)S(1)}, bf16[2176,128]{1,0:T(8,128)(2,1)S(1)}, u32[]{:S(2)}, u32[]{:S(2)}) collective-permute-start(bf16[2176,128]{1,0:T(8,128)(2,1)S(1)} %pad_maximum_fusion.mine_ref), channel_id=1, source_target_pairs={{0,2},{1,3},{2,0},{3,1},{4,6},{5,7},{6,4},{7,5},{8,10},{9,11},{10,... | collective-permute-start | bytes 1671176 | tf_op jit(solution)/shard_map/ppermute | solution.py:1293
  68.4 3.8 %collective-permute-start.16 = (bf16[2048,128]{1,0:T(8,128)(2,1)S(1)}, bf16[2048,128]{1,0:T(8,128)(2,1)S(1)}, u32[]{:S(2)}, u32[]{:S(2)}) collective-permute-start(bf16[2048,128]{1,0:T(8,128)(2,1)S(1)} %pad_maximum_fusion.1.mine_ref), channel_id=1, source_target_pairs={{0,2},{1,3},{2,0},{3,1},{4,6},{5,7},{6,4},{7,5},{8,10},{9,11},{10,... | collective-permute-start | bytes 1572872 | tf_op jit(solution)/shard_map/ppermute | solution.py:1293

commit v4 on v3

--- a/solution.py
+++ b/solution.py
@@ -1108,6 +1108,8 @@
     *scratch,
 ):
     core = where_ref[1]
+    part, rows = read_half(*plan_out, core, False, theirs_ref)
+    copies = expand_outer(part, rows, grad_out_hbm, *scratch[:5])
     gained = own_ref[...] + recv_ref[0:112, :].astype(f32)[: HALF // 2, :]
     series_ref[...] = gained.reshape(1, HALF * D)
     tail = recv_ref[112:128, :].astype(f32)
@@ -1118,14 +1120,13 @@
     )
     table = jnp.sum(jnp.where(pick, dots[:, 0:K], 0.0), axis=0, keepdims=True)
     amps_ref[...] = mixing * (table - jnp.sum(mixing * table, axis=-1, keepdims=True))
-    copies = [
+    small = [
         pltpu.make_async_copy(series_ref, series_hbm, small_sems.at[0]),
         pltpu.make_async_copy(amps_ref, amps_hbm, small_sems.at[1]),
     ]
-    for copy in copies:
+    for copy in small:
         copy.start()
-    part, rows = read_half(*plan_out, core, False, theirs_ref)
-    copies += expand_outer(part, rows, grad_out_hbm, *scratch[:5])
+    copies += small
     part, rows = read_half(*plan_in, core, True, mine_ref)
     copies += expand_inner(part, rows, grad_in_hbm, *scratch[5:])
     for copy in copies:
@@ -1152,6 +1153,7 @@
 ):
     core = where_ref[1]
     part, rows = read_half(*plan_in, core, False, theirs_ref)
+    copies = expand_inner(part, rows, grad_hbm, *scratch)
     _, mine = read_half(*plan_in, core, True, mine_ref)
 
     def mean(side):
@@ -1164,7 +1166,6 @@
     bias_out_ref[...] = spare[1:2, 0:64]
     gain_ref[...] = spare[2:3, 0:64]
     shift_ref[...] = spare[3:4, 0:64]
-    small = []
     for index, (source, target) in enumerate(
         (
             (bias_in_ref, bias_in_hbm),
@@ -1175,8 +1176,7 @@
     ):
         copy = pltpu.make_async_copy(source, target, small_sems.at[index])
         copy.start()
-        small.append(copy)
-    copies = expand_inner(part, rows, grad_hbm, *scratch) + small
+        copies.append(copy)
     for copy in copies:
         copy.wait()
 
@@ -1419,7 +1419,7 @@
         return jnp.where(core == 0, values[0], values[1])
 
     def merge(bit, a, b):
-        return jnp.concatenate([jnp.where(bit == 0, a, b), jnp.where(bit == 0, b, a)], axis=0)
+        return jnp.where(bit == 0, jnp.concatenate([a, b], axis=0), jnp.concatenate([b, a], axis=0))
 
     orders = (halved, halved[1::-1] + halved[2:])
     sequences = ([None] + halved[::-1], halved[::-1] + [None])

time: 74.9 us -> 74.9 us (level)
  no operation moved by 1% of the time
where the time goes in v4:
time: 74.9 us; the launch traced here: 74.8 us
  Pallas kernels  34.1 us (46%)
  starting transfers between devices  23.9 us (32%)
  waiting for transfers between devices  14.6 us (19%)
  between operations  1.09 us (1%)
  other arithmetic  0.9 us (1%)
    ppermute x17, starting transfers between devices, exchange(): return lax.ppermute(value, ('items', 'narrow'), pairs)  23.9 us
    ppermute x17, waiting for transfers between devices, exchange(): return lax.ppermute(value, ('items', 'narrow'), pairs)  14.6 us
    pallas_call x1, Pallas kernels, on_device(): pl.pallas_call(forward_kernel, out_shape=(pltpu.VMEM((FOLD + 112, LANES),...  10.3 us
    pallas_call x1, Pallas kernels, on_device(): pl.pallas_call(outer_kernel, out_shape=(shape((1, HALF * D), bf16), pltpu...  6.79 us
    pallas_call x1, Pallas kernels, on_device(): pl.pallas_call(inner_kernel, out_shape=(pltpu.VMEM((HALF_IN, LANES), bf16...  3.91 us
    pallas_call x1, Pallas kernels, on_device(): pl.pallas_call(functools.partial(second_last_kernel, plan_out, plan_in),...  3.6 us
    pallas_call x1, Pallas kernels, on_device(): pl.pallas_call(functools.partial(third_last_kernel, plan_in), out_shape=(...  2.48 us
    pallas_call x1, Pallas kernels, on_device(): pl.pallas_call(functools.partial(first_last_kernel, plan_out), out_shape=...  2.48 us
  transfers between devices with their start and end apart: 17, of which 12 were waited for; matrix products, arithmetic and copies ran while one was open for 1% of the time, Pallas kernels for 14%

profile of v4, /device:TPU:0, one launch (start us, length us, event | category | flops | bytes accessed | tf_op | source)
XLA Modules:
  0.0 74.8 jit_solution(1111786622100364)
XLA Ops:
  0.8 10.3 %forward.1 = (bf16[336,128]{1,0:T(8,128)(2,1)S(1)}, f32[224,128]{1,0:T(8,128)S(1)}, f32[5,224,128]{2,1,0:T(8,128)S(1)}, bf16[384,768]{1,0:T(8,128)(2,1)}, bf16[7...) custom-call(s32[2]{0:T(128)S(1)} %pad_add_fusion.where_ref, ...), custom_call_target="tpu_custom_call" | custom-call | flops 8589934592 | bytes 4194304 | tf_op jit(solution)/shard_map/forward/pallas_call | solution.py:1227
  11.1 3.0 %collective-permute-start = (bf16[336,128]{1,0:T(8,128)(2,1)S(1)}, bf16[336,128]{1,0:T(8,128)(2,1)S(1)}, u32[]{:S(2)}, u32[]{:S(2)}) collective-permute-start(bf16[336,128]{1,0:T(8,128)(2,1)S(1)} %get-tuple-element.43), channel_id=1, source_target_pairs={{0,1},{1,0},{2,3},{3,2},{4,5},{5,4},{6,7},{7,6},{8,9},{9,8},{10,11... | collective-permute-start | bytes 258056 | tf_op jit(solution)/shard_map/ppermute | solution.py:1293
  14.1 2.5 %collective-permute-done.recv_ref = bf16[336,128]{1,0:T(8,128)(2,1)S(1)} collective-permute-done((bf16[336,128]{1,0:T(8,128)(2,1)S(1)}, bf16[336,128]{1,0:T(8,128)(2,1)S(1)}, u32[]{:S(2)}, u32[]{:S(2)}) %collective-permute-start) | collective-permute-done | bytes 86048 | tf_op jit(solution)/shard_map/ppermute | solution.py:1293
  16.6 6.8 %outer.1 = (bf16[1,13824]{1,0:T(2,128)(2,1)}, bf16[1088,128]{1,0:T(8,128)(2,1)S(1)}, bf16[1088,128]{1,0:T(8,128)(2,1)S(1)}, f32[5,120,128]{2,1,0:T(8,128)S(1)}, ...) custom-call(s32[2]{0:T(128)S(1)} %pad_add_fusion.where_ref, ...), custom_call_target="tpu_custom_call" | custom-call | flops 8589934592 | bytes 4194304 | tf_op jit(solution)/shard_map/outer/pallas_call | solution.py:1299
  23.4 3.9 %inner.1 = (bf16[1024,128]{1,0:T(8,128)(2,1)S(1)}, bf16[1024,128]{1,0:T(8,128)(2,1)S(1)}) custom-call(s32[2]{0:T(128)S(1)} %pad_add_fusion.where_ref, s32[1,5]{1,0:T(1,128)S(1)} %copy-done.3, f32[5,120,128]{2,1,0:T(8,128)S(1)} %get-tuple-element.61.grad_ref, f32[8,128]{1,0:T(8,128)S(1)} %get-tuple-element.55.small_ref, ...), custom_call_target="tpu_custom_call" | custom-call | flops 8589934592 | bytes 4194304 | tf_op jit(solution)/shard_map/inner/pallas_call | solution.py:1347
  29.0 2.1 %collective-permute-start.10 = (bf16[512,128]{1,0:T(8,128)(2,1)S(1)}, bf16[512,128]{1,0:T(8,128)(2,1)S(1)}, u32[]{:S(2)}, u32[]{:S(2)}) collective-permute-start(bf16[512,128]{1,0:T(8,128)(2,1)S(1)} %dynamic-slice_convert_fusion.1), channel_id=1, source_target_pairs={{0,4},{1,5},{2,10},{3,11},{4,0},{5,1},{6,14},{7,15},{8,12},{9,13},... | collective-permute-start | bytes 393224 | tf_op jit(solution)/shard_map/ppermute | solution.py:1293
  31.1 2.5 %series.1.begun_ref = f32[480,128]{1,0:T(8,128)S(1)} custom-call(s32[1,5]{1,0:T(1,128)S(1)} %copy-done.3, f32[5,120,128]{2,1,0:T(8,128)S(1)} %get-tuple-element.61.grad_ref, bf16[384,768]{1,0:T(8,128)(2,1)S(1)} %get-tuple-element.64.w1_ref), custom_call_target="tpu_custom_call" | custom-call | flops 2147483648 | bytes 4194304 | tf_op jit(solution)/shard_map/series/pallas_call | solution.py:1376
  34.1 2.1 %collective-permute-start.11 = (bf16[256,128]{1,0:T(8,128)(2,1)S(1)}, bf16[256,128]{1,0:T(8,128)(2,1)S(1)}, u32[]{:S(2)}, u32[]{:S(2)}) collective-permute-start(bf16[256,128]{1,0:T(8,128)(2,1)S(1)} %dynamic-slice_convert_fusion.3), channel_id=1, source_target_pairs={{0,8},{1,9},{2,6},{3,7},{4,12},{5,13},{6,2},{7,3},{8,0},{9,1},{10,... | collective-permute-start | bytes 196616 | tf_op jit(solution)/shard_map/ppermute | solution.py:1293
  36.3 2.1 %series_rest.1 = (f32[108,128]{1,0:T(8,128)S(1)}, bf16[128,128]{1,0:T(8,128)(2,1)S(1)}, f32[8,128]{1,0:T(8,128)S(1)}) custom-call(s32[2]{0:T(128)S(1)} %pad_add_fusion.where_ref, s32[1,5]{1,0:T(1,128)S(1)} %copy-done.3, f32[5,120,128]{2,1,0:T(8,128)S(1)} %get-tuple-element.61.grad_ref, f32[448,128]{1,0:T(8,128)S(1)} %get-tuple-element.62.merged_ref, ...), custom_call_target="tpu_custom_call" | custom-call | flops 2147483648 | bytes 4194304 | tf_op jit(solution)/shard_map/series_rest/pallas_call | solution.py:1388
  38.9 1.6 %collective-permute-start.3 = (bf16[272,128]{1,0:T(8,128)(2,1)S(1)}, bf16[272,128]{1,0:T(8,128)(2,1)S(1)}, u32[]{:S(2)}, u32[]{:S(2)}) collective-permute-start(bf16[272,128]{1,0:T(8,128)(2,1)S(1)} %dynamic-slice_convert_fusion.2), channel_id=1, source_target_pairs={{0,8},{1,9},{2,6},{3,7},{4,12},{5,13},{6,2},{7,3},{8,0},{9,1},{10,... | collective-permute-start | bytes 208904 | tf_op jit(solution)/shard_map/ppermute | solution.py:1293
  40.6 2.7 %collective-permute-start.12 = (bf16[256,128]{1,0:T(8,128)(2,1)S(1)}, bf16[256,128]{1,0:T(8,128)(2,1)S(1)}, u32[]{:S(2)}, u32[]{:S(2)}) collective-permute-start(bf16[256,128]{1,0:T(8,128)(2,1)S(1)} %add_convert_fusion.3), channel_id=1, source_target_pairs={{0,16},{1,17},{2,18},{3,19},{4,20},{5,21},{6,22},{7,23},{8,24},{9,... | collective-permute-start | bytes 196616 | tf_op jit(solution)/shard_map/ppermute | solution.py:1293
  43.3 2.8 %collective-permute-start.4 = (bf16[272,128]{1,0:T(8,128)(2,1)S(1)}, bf16[272,128]{1,0:T(8,128)(2,1)S(1)}, u32[]{:S(2)}, u32[]{:S(2)}) collective-permute-start(bf16[272,128]{1,0:T(8,128)(2,1)S(1)} %add_convert_fusion.1), channel_id=1, source_target_pairs={{0,16},{1,17},{2,18},{3,19},{4,20},{5,21},{6,22},{7,23},{8,24},{9,... | collective-permute-start | bytes 208904 | tf_op jit(solution)/shard_map/ppermute | solution.py:1293
  46.1 1.7 %collective-permute-done.12 = bf16[256,128]{1,0:T(8,128)(2,1)S(1)} collective-permute-done((bf16[256,128]{1,0:T(8,128)(2,1)S(1)}, bf16[256,128]{1,0:T(8,128)(2,1)S(1)}, u32[]{:S(2)}, u32[]{:S(2)}) %collective-permute-start.12) | collective-permute-done | bytes 65568 | tf_op jit(solution)/shard_map/ppermute | solution.py:1293
  48.8 1.6 %collective-permute-start.5 = (bf16[272,128]{1,0:T(8,128)(2,1)S(1)}, bf16[272,128]{1,0:T(8,128)(2,1)S(1)}, u32[]{:S(2)}, u32[]{:S(2)}) collective-permute-start(bf16[272,128]{1,0:T(8,128)(2,1)S(1)} %add_convert_fusion), channel_id=1, source_target_pairs={{0,1},{1,0},{2,10},{3,11},{4,5},{5,4},{6,14},{7,15},{8,9},{9,8},{1... | collective-permute-start | bytes 208904 | tf_op jit(solution)/shard_map/ppermute | solution.py:1293
  50.9 2.2 %collective-permute-done.5 = bf16[272,128]{1,0:T(8,128)(2,1)S(1)} collective-permute-done((bf16[272,128]{1,0:T(8,128)(2,1)S(1)}, bf16[272,128]{1,0:T(8,128)(2,1)S(1)}, u32[]{:S(2)}, u32[]{:S(2)}) %collective-permute-start.5) | collective-permute-done | bytes 69664 | tf_op jit(solution)/shard_map/ppermute | solution.py:1293
  53.2 1.8 %collective-permute-start.6 = (bf16[544,128]{1,0:T(8,128)(2,1)S(1)}, bf16[544,128]{1,0:T(8,128)(2,1)S(1)}, u32[]{:S(2)}, u32[]{:S(2)}) collective-permute-start(bf16[544,128]{1,0:T(8,128)(2,1)S(1)} %maximum_select_fusion.4), channel_id=1, source_target_pairs={{0,8},{1,9},{2,6},{3,7},{4,12},{5,13},{6,2},{7,3},{8,0},{9,1},{10,... | collective-permute-start | bytes 417800 | tf_op jit(solution)/shard_map/ppermute | solution.py:1293
  55.1 1.8 %collective-permute-start.14 = (bf16[512,128]{1,0:T(8,128)(2,1)S(1)}, bf16[512,128]{1,0:T(8,128)(2,1)S(1)}, u32[]{:S(2)}, u32[]{:S(2)}) collective-permute-start(bf16[512,128]{1,0:T(8,128)(2,1)S(1)} %maximum_select_fusion.5), channel_id=1, source_target_pairs={{0,8},{1,9},{2,6},{3,7},{4,12},{5,13},{6,2},{7,3},{8,0},{9,1},{10,... | collective-permute-start | bytes 393224 | tf_op jit(solution)/shard_map/ppermute | solution.py:1293
  56.9 1.4 %collective-permute-done.6 = bf16[544,128]{1,0:T(8,128)(2,1)S(1)} collective-permute-done((bf16[544,128]{1,0:T(8,128)(2,1)S(1)}, bf16[544,128]{1,0:T(8,128)(2,1)S(1)}, u32[]{:S(2)}, u32[]{:S(2)}) %collective-permute-start.6) | collective-permute-done | bytes 139296 | tf_op jit(solution)/shard_map/ppermute | solution.py:1293
  58.4 1.5 %collective-permute-start.7 = (bf16[1088,128]{1,0:T(8,128)(2,1)S(1)}, bf16[1088,128]{1,0:T(8,128)(2,1)S(1)}, u32[]{:S(2)}, u32[]{:S(2)}) collective-permute-start(bf16[1088,128]{1,0:T(8,128)(2,1)S(1)} %maximum_select_fusion.2), channel_id=1, source_target_pairs={{0,4},{1,5},{2,3},{3,2},{4,0},{5,1},{6,7},{7,6},{8,12},{9,13},{10,... | collective-permute-start | bytes 835592 | tf_op jit(solution)/shard_map/ppermute | solution.py:1293
  60.2 1.4 %collective-permute-start.15 = (bf16[1152,128]{1,0:T(8,128)(2,1)S(1)}, bf16[1152,128]{1,0:T(8,128)(2,1)S(1)}, u32[]{:S(2)}, u32[]{:S(2)}) collective-permute-start(bf16[1152,128]{1,0:T(8,128)(2,1)S(1)} %pad_maximum_fusion), channel_id=1, source_target_pairs={{0,4},{1,5},{2,3},{3,2},{4,0},{5,1},{6,7},{7,6},{8,12},{9,13},{10,... | collective-permute-start | bytes 884744 | tf_op jit(solution)/shard_map/ppermute | solution.py:1293
  61.7 3.3 %collective-permute-done.7 = bf16[1088,128]{1,0:T(8,128)(2,1)S(1)} collective-permute-done((bf16[1088,128]{1,0:T(8,128)(2,1)S(1)}, bf16[1088,128]{1,0:T(8,128)(2,1)S(1)}, u32[]{:S(2)}, u32[]{:S(2)}) %collective-permute-start.7) | collective-permute-done | bytes 278560 | tf_op jit(solution)/shard_map/ppermute | solution.py:1293
  65.2 2.5 %first_last.1.begun_hbm = f32[64,18304]{1,0:T(8,128)} custom-call(s32[2]{0:T(128)S(1)} %pad_add_fusion.where_ref, bf16[2176,128]{1,0:T(8,128)(2,1)S(1)} %maximum_select_fusion.mine_ref), custom_call_target="tpu_custom_call" | custom-call | flops 2147483648 | bytes 4194304 | tf_op jit(solution)/shard_map/first_last/pallas_call | solution.py:1507
  68.5 3.6 %second_last.1 = (f32[64,18304]{1,0:T(8,128)}, f32[64,18304]{1,0:T(8,128)}, f32[1,13824]{1,0:T(1,128)}, f32[1,5]{1,0:T(1,128)}) custom-call(s32[2]{0:T(128)S(1)} %pad_add_fusion.where_ref, f32[1,5]{1,0:T(1,128)S(1)} %copy-done.4, bf16[2176,128]{1,0:T(8,128)(2,1)S(1)} %collective-permute-done.8.theirs_ref, ...), custom_call_target="tpu_custom_call", output_to_operand_aliasing={{0}: (7, {})} | custom-call | flops 4294967296 | bytes 4194304 | tf_op jit(solution)/shard_map/second_last/pallas_call | solution.py:1517
  72.1 2.5 %third_last.1 = (f32[64,18304]{1,0:T(8,128)}, f32[1,64]{1,0:T(1,128)}, f32[1,64]{1,0:T(1,128)}, f32[1,64]{1,0:T(1,128)}, f32[1,64]{1,0:T(1,128)}) custom-call(s32[2]{0:T(128)S(1)} %pad_add_fusion.where_ref, bf16[2048,128]{1,0:T(8,128)(2,1)S(1)} %maximum_select_fusion.1.mine_ref, ...), custom_call_target="tpu_custom_call", output_to_operand_aliasing={{0}: (3, {})} | custom-call | flops 2147483648 | bytes 4194304 | tf_op jit(solution)/shard_map/third_last/pallas_call | solution.py:1539
  (52 shorter events, 5.9 us)
Async XLA Ops:
  0.7 15.9 %copy-start = (bf16[1,13824]{1,0:T(2,128)(2,1)S(1)}, bf16[1,13824]{1,0:T(2,128)(2,1)}, u32[]{:S(2)}) copy-start(bf16[1,13824]{1,0:T(2,128)(2,1)} %cot_ref.1) | copy-start | bytes 82948
  0.7 15.9 %copy-start.1 = (f32[64]{0:T(128)S(1)}, f32[64]{0:T(128)}, u32[]{:S(2)}) copy-start(f32[64]{0:T(128)} %param.17) | copy-start | bytes 772
  0.7 15.9 %copy-start.2 = (f32[64]{0:T(128)S(1)}, f32[64]{0:T(128)}, u32[]{:S(2)}) copy-start(f32[64]{0:T(128)} %param.18) | copy-start | bytes 772
  0.7 15.9 %copy-start.3 = (s32[1,5]{1,0:T(1,128)S(1)}, s32[1,5]{1,0:T(1,128)}, u32[]{:S(2)}) copy-start(s32[1,5]{1,0:T(1,128)} %periods_ref.7) | copy-start | bytes 64
  0.7 15.9 %copy-start.4 = (f32[1,5]{1,0:T(1,128)S(1)}, f32[1,5]{1,0:T(1,128)}, u32[]{:S(2)}) copy-start(f32[1,5]{1,0:T(1,128)} %amp_ref.3) | copy-start | bytes 64
  11.1 5.5 %collective-permute-start = (bf16[336,128]{1,0:T(8,128)(2,1)S(1)}, bf16[336,128]{1,0:T(8,128)(2,1)S(1)}, u32[]{:S(2)}, u32[]{:S(2)}) collective-permute-start(bf16[336,128]{1,0:T(8,128)(2,1)S(1)} %get-tuple-element.43), channel_id=1, source_target_pairs={{0,1},{1,0},{2,3},{3,2},{4,5},{5,4},{6,7},{7,6},{8,9},{9,8},{10,11... | collective-permute-start | bytes 258056 | tf_op jit(solution)/shard_map/ppermute | solution.py:1293
  27.3 1.6 %collective-permute-start.9 = (bf16[1024,128]{1,0:T(8,128)(2,1)S(1)}, bf16[1024,128]{1,0:T(8,128)(2,1)S(1)}, u32[]{:S(2)}, u32[]{:S(2)}) collective-permute-start(bf16[1024,128]{1,0:T(8,128)(2,1)S(1)} %get-tuple-element.57), channel_id=1, source_target_pairs={{0,2},{1,3},{2,0},{3,1},{4,6},{5,7},{6,4},{7,5},{8,10},{9,11},{10,... | collective-permute-start | bytes 786440 | tf_op jit(solution)/shard_map/ppermute | solution.py:1293
  27.4 6.2 %collective-permute-start.1 = (bf16[1088,128]{1,0:T(8,128)(2,1)S(1)}, bf16[1088,128]{1,0:T(8,128)(2,1)S(1)}, u32[]{:S(2)}, u32[]{:S(2)}) collective-permute-start(bf16[1088,128]{1,0:T(8,128)(2,1)S(1)} %get-tuple-element.53), channel_id=1, source_target_pairs={{0,2},{1,3},{2,0},{3,1},{4,6},{5,7},{6,4},{7,5},{8,10},{9,11},{10,... | collective-permute-start | bytes 835592 | tf_op jit(solution)/shard_map/ppermute | solution.py:1293
  29.0 5.1 %collective-permute-start.10 = (bf16[512,128]{1,0:T(8,128)(2,1)S(1)}, bf16[512,128]{1,0:T(8,128)(2,1)S(1)}, u32[]{:S(2)}, u32[]{:S(2)}) collective-permute-start(bf16[512,128]{1,0:T(8,128)(2,1)S(1)} %dynamic-slice_convert_fusion.1), channel_id=1, source_target_pairs={{0,4},{1,5},{2,10},{3,11},{4,0},{5,1},{6,14},{7,15},{8,12},{9,13},... | collective-permute-start | bytes 393224 | tf_op jit(solution)/shard_map/ppermute | solution.py:1293
  33.7 5.1 %collective-permute-start.2 = (bf16[544,128]{1,0:T(8,128)(2,1)S(1)}, bf16[544,128]{1,0:T(8,128)(2,1)S(1)}, u32[]{:S(2)}, u32[]{:S(2)}) collective-permute-start(bf16[544,128]{1,0:T(8,128)(2,1)S(1)} %dynamic-slice_convert_fusion), channel_id=1, source_target_pairs={{0,4},{1,5},{2,10},{3,11},{4,0},{5,1},{6,14},{7,15},{8,12},{9,13},... | collective-permute-start | bytes 417800 | tf_op jit(solution)/shard_map/ppermute | solution.py:1293
  34.1 6.4 %collective-permute-start.11 = (bf16[256,128]{1,0:T(8,128)(2,1)S(1)}, bf16[256,128]{1,0:T(8,128)(2,1)S(1)}, u32[]{:S(2)}, u32[]{:S(2)}) collective-permute-start(bf16[256,128]{1,0:T(8,128)(2,1)S(1)} %dynamic-slice_convert_fusion.3), channel_id=1, source_target_pairs={{0,8},{1,9},{2,6},{3,7},{4,12},{5,13},{6,2},{7,3},{8,0},{9,1},{10,... | collective-permute-start | bytes 196616 | tf_op jit(solution)/shard_map/ppermute | solution.py:1293
  38.9 4.4 %collective-permute-start.3 = (bf16[272,128]{1,0:T(8,128)(2,1)S(1)}, bf16[272,128]{1,0:T(8,128)(2,1)S(1)}, u32[]{:S(2)}, u32[]{:S(2)}) collective-permute-start(bf16[272,128]{1,0:T(8,128)(2,1)S(1)} %dynamic-slice_convert_fusion.2), channel_id=1, source_target_pairs={{0,8},{1,9},{2,6},{3,7},{4,12},{5,13},{6,2},{7,3},{8,0},{9,1},{10,... | collective-permute-start | bytes 208904 | tf_op jit(solution)/shard_map/ppermute | solution.py:1293
  40.6 7.2 %collective-permute-start.12 = (bf16[256,128]{1,0:T(8,128)(2,1)S(1)}, bf16[256,128]{1,0:T(8,128)(2,1)S(1)}, u32[]{:S(2)}, u32[]{:S(2)}) collective-permute-start(bf16[256,128]{1,0:T(8,128)(2,1)S(1)} %add_convert_fusion.3), channel_id=1, source_target_pairs={{0,16},{1,17},{2,18},{3,19},{4,20},{5,21},{6,22},{7,23},{8,24},{9,... | collective-permute-start | bytes 196616 | tf_op jit(solution)/shard_map/ppermute | solution.py:1293
  43.3 5.4 %collective-permute-start.4 = (bf16[272,128]{1,0:T(8,128)(2,1)S(1)}, bf16[272,128]{1,0:T(8,128)(2,1)S(1)}, u32[]{:S(2)}, u32[]{:S(2)}) collective-permute-start(bf16[272,128]{1,0:T(8,128)(2,1)S(1)} %add_convert_fusion.1), channel_id=1, source_target_pairs={{0,16},{1,17},{2,18},{3,19},{4,20},{5,21},{6,22},{7,23},{8,24},{9,... | collective-permute-start | bytes 208904 | tf_op jit(solution)/shard_map/ppermute | solution.py:1293
  48.8 4.4 %collective-permute-start.5 = (bf16[272,128]{1,0:T(8,128)(2,1)S(1)}, bf16[272,128]{1,0:T(8,128)(2,1)S(1)}, u32[]{:S(2)}, u32[]{:S(2)}) collective-permute-start(bf16[272,128]{1,0:T(8,128)(2,1)S(1)} %add_convert_fusion), channel_id=1, source_target_pairs={{0,1},{1,0},{2,10},{3,11},{4,5},{5,4},{6,14},{7,15},{8,9},{9,8},{1... | collective-permute-start | bytes 208904 | tf_op jit(solution)/shard_map/ppermute | solution.py:1293
  50.3 4.7 %collective-permute-start.13 = (bf16[384,128]{1,0:T(8,128)(2,1)S(1)}, bf16[384,128]{1,0:T(8,128)(2,1)S(1)}, u32[]{:S(2)}, u32[]{:S(2)}) collective-permute-start(bf16[384,128]{1,0:T(8,128)(2,1)S(1)} %pad_maximum_fusion.1), channel_id=1, source_target_pairs={{0,1},{1,0},{2,10},{3,11},{4,5},{5,4},{6,14},{7,15},{8,9},{9,8},{1... | collective-permute-start | bytes 294920 | tf_op jit(solution)/shard_map/ppermute | solution.py:1293
  53.2 5.1 %collective-permute-start.6 = (bf16[544,128]{1,0:T(8,128)(2,1)S(1)}, bf16[544,128]{1,0:T(8,128)(2,1)S(1)}, u32[]{:S(2)}, u32[]{:S(2)}) collective-permute-start(bf16[544,128]{1,0:T(8,128)(2,1)S(1)} %maximum_select_fusion.4), channel_id=1, source_target_pairs={{0,8},{1,9},{2,6},{3,7},{4,12},{5,13},{6,2},{7,3},{8,0},{9,1},{10,... | collective-permute-start | bytes 417800 | tf_op jit(solution)/shard_map/ppermute | solution.py:1293
  55.1 5.0 %collective-permute-start.14 = (bf16[512,128]{1,0:T(8,128)(2,1)S(1)}, bf16[512,128]{1,0:T(8,128)(2,1)S(1)}, u32[]{:S(2)}, u32[]{:S(2)}) collective-permute-start(bf16[512,128]{1,0:T(8,128)(2,1)S(1)} %maximum_select_fusion.5), channel_id=1, source_target_pairs={{0,8},{1,9},{2,6},{3,7},{4,12},{5,13},{6,2},{7,3},{8,0},{9,1},{10,... | collective-permute-start | bytes 393224 | tf_op jit(solution)/shard_map/ppermute | solution.py:1293
  58.4 6.6 %collective-permute-start.7 = (bf16[1088,128]{1,0:T(8,128)(2,1)S(1)}, bf16[1088,128]{1,0:T(8,128)(2,1)S(1)}, u32[]{:S(2)}, u32[]{:S(2)}) collective-permute-start(bf16[1088,128]{1,0:T(8,128)(2,1)S(1)} %maximum_select_fusion.2), channel_id=1, source_target_pairs={{0,4},{1,5},{2,3},{3,2},{4,0},{5,1},{6,7},{7,6},{8,12},{9,13},{10,... | collective-permute-start | bytes 835592 | tf_op jit(solution)/shard_map/ppermute | solution.py:1293
  60.2 7.9 %collective-permute-start.15 = (bf16[1152,128]{1,0:T(8,128)(2,1)S(1)}, bf16[1152,128]{1,0:T(8,128)(2,1)S(1)}, u32[]{:S(2)}, u32[]{:S(2)}) collective-permute-start(bf16[1152,128]{1,0:T(8,128)(2,1)S(1)} %pad_maximum_fusion), channel_id=1, source_target_pairs={{0,4},{1,5},{2,3},{3,2},{4,0},{5,1},{6,7},{7,6},{8,12},{9,13},{10,... | collective-permute-start | bytes 884744 | tf_op jit(solution)/shard_map/ppermute | solution.py:1293
  65.2 3.3 %collective-permute-start.8 = (bf16[2176,128]{1,0:T(8,128)(2,1)S(1)}, bf16[2176,128]{1,0:T(8,128)(2,1)S(1)}, u32[]{:S(2)}, u32[]{:S(2)}) collective-permute-start(bf16[2176,128]{1,0:T(8,128)(2,1)S(1)} %maximum_select_fusion.mine_ref), channel_id=1, source_target_pairs={{0,2},{1,3},{2,0},{3,1},{4,6},{5,7},{6,4},{7,5},{8,10},{9,11},{10,... | collective-permute-start | bytes 1671176 | tf_op jit(solution)/shard_map/ppermute | solution.py:1293
  68.3 3.8 %collective-permute-start.16 = (bf16[2048,128]{1,0:T(8,128)(2,1)S(1)}, bf16[2048,128]{1,0:T(8,128)(2,1)S(1)}, u32[]{:S(2)}, u32[]{:S(2)}) collective-permute-start(bf16[2048,128]{1,0:T(8,128)(2,1)S(1)} %maximum_select_fusion.1.mine_ref), channel_id=1, source_target_pairs={{0,2},{1,3},{2,0},{3,1},{4,6},{5,7},{6,4},{7,5},{8,10},{9,11},{10,... | collective-permute-start | bytes 1572872 | tf_op jit(solution)/shard_map/ppermute | solution.py:1293
